TPU v7x, 32 devices: a whole 2x2x4 slice. The times are simulated.
32 devices in a mesh: fsdp: 2 (over core), context: 8 (over z, y), tensor: 2 (over x).
Axes of the slice: x: 2, y: 2, z: 4, core: 2. Of those that a mesh axis runs over, the one named last changes fastest.
Arguments:
- latents: bfloat16 [8, 2048, 1152], P('fsdp', ('context', 'tensor')), may hold values from -6 to 6
- text: bfloat16 [8, 120, 1152], P('fsdp'), may hold values from -6 to 6
- time_vector: bfloat16 [8, 6912], P('fsdp'), may hold values from -1.796875 to 1.796875
- table: bfloat16 [6, 1152], P(None, ('fsdp', 'context')), may hold values from -1.796875 to 1.796875
- w_qkv: bfloat16 [1152, 3, 1152], P(('fsdp', 'context'), None, 'tensor'), may hold values from -0.1875 to 0.1875
- w_out: bfloat16 [1152, 1152], P('tensor', ('fsdp', 'context')), may hold values from -0.5 to 0.5
- w_cq: bfloat16 [1152, 1152], P(('fsdp', 'context'), 'tensor'), may hold values from -0.1875 to 0.1875
- w_ckv: bfloat16 [1152, 2, 1152], P(('fsdp', 'context'), None, 'tensor'), may hold values from -0.1875 to 0.1875
- w_co: bfloat16 [1152, 1152], P('tensor', ('fsdp', 'context')), may hold values from -0.1875 to 0.1875
- w_up: bfloat16 [1152, 4608], P(('fsdp', 'context'), 'tensor'), may hold values from -0.1875 to 0.1875
- w_down: bfloat16 [4608, 1152], P('tensor', ('fsdp', 'context')), may hold values from -0.09375 to 0.09375
- cotangent: bfloat16 [8, 2048, 1152], P('fsdp', ('context', 'tensor')), may hold values from -6 to 6
Outputs:
- output: bfloat16 [8, 2048, 1152], P('fsdp', ('context', 'tensor'))
- grad_latents: float32 [8, 2048, 1152], P('fsdp', ('context', 'tensor'))
- grad_text: float32 [8, 120, 1152], P('fsdp')
- grad_time: float32 [8, 6912], P('fsdp')
- grad_table: float32 [6, 1152], P(None, ('fsdp', 'context'))
- grad_qkv: float32 [1152, 3, 1152], P(('fsdp', 'context'), None, 'tensor')
- grad_out: float32 [1152, 1152], P('tensor', ('fsdp', 'context'))
- grad_cq: float32 [1152, 1152], P(('fsdp', 'context'), 'tensor')
- grad_ckv: float32 [1152, 2, 1152], P(('fsdp', 'context'), None, 'tensor')
- grad_co: float32 [1152, 1152], P('tensor', ('fsdp', 'context'))
- grad_up: float32 [1152, 4608], P(('fsdp', 'context'), 'tensor')
- grad_down: float32 [4608, 1152], P('tensor', ('fsdp', 'context'))
All inputs are finite; a program needn't handle non-finite values.
Results may differ from a plain program's by a relative error of at most 0.033.
Values may be sent and summed in bfloat16 or wider, within the bound.
No kernel may reach another device: no remote copies, remote signals or barrier semaphores. Data moves between devices by JAX's collectives and lax.ppermute only.
A program may use at most 256 MiB of HBM per device.

v0:
```python
import math
from functools import partial

import jax
import jax.numpy as jnp
from jax import lax
from jax.experimental import pallas as pl
from jax.experimental.pallas import tpu as pltpu
from jax.sharding import Mesh
from jax.sharding import PartitionSpec as P

HEAD_DIM = 72
EPSILON = 1e-06
LANES = 128
FACTOR = HEAD_DIM ** (-0.5)
FACTOR2 = FACTOR * math.log2(math.e)
VMEM_LIMIT = 56 * 1024 * 1024

f32 = jnp.float32
bf16 = jnp.bfloat16

NT = (((1,), (1,)), ((), ()))
NN = (((1,), (0,)), ((), ()))
TN = (((0,), (0,)), ((), ()))

ROW = ("sr", "hr")
PLANE = ("sr", "hr", "tensor")
HEAD_GROUP = ("hr", "tensor")


def dot(left, right, dims=NN):
    return lax.dot_general(left, right, dims, preferred_element_type=f32)


def norm_parts(values):
    center = values - jnp.mean(values, axis=-1, keepdims=True)
    inverse = lax.rsqrt(jnp.mean(center * center, axis=-1, keepdims=True) + EPSILON)
    return (center * inverse, inverse)


def norm_back(grad_hat, normed, inverse):
    first = jnp.mean(grad_hat, axis=-1, keepdims=True)
    second = jnp.mean(grad_hat * normed, axis=-1, keepdims=True)
    return inverse * (grad_hat - first - normed * second)


def send_xor(piece, axes, step):
    size = lax.axis_size(axes)
    return lax.ppermute(piece, axes, [(rank, rank ^ step) for rank in range(size)])


def pick(stack, index):
    return lax.dynamic_index_in_dim(stack, index, 0, keepdims=False)


def exchange(piece_for, axes):
    me = lax.axis_index(axes)
    got = [piece_for(me)]
    for step in range(1, lax.axis_size(axes)):
        got.append(send_xor(piece_for(jnp.bitwise_xor(me, step)), axes, step))
    return got


def give_back(pieces, axes):
    return [send_xor(piece, axes, step) if step else piece for step, piece in enumerate(pieces)]


def in_order(pieces, axes):
    me = lax.axis_index(axes)
    places = range(len(pieces))
    return jnp.stack([choose(pieces, jnp.bitwise_xor(me, place)) for place in places])


def choose(pieces, index):
    out = pieces[0]
    for place in range(1, len(pieces)):
        out = jnp.where(index == place, pieces[place], out)
    return out


def plane_sum(values, dtype):
    sent = values.astype(dtype)
    total = sent.astype(f32)
    for step in range(1, lax.axis_size(PLANE)):
        total += send_xor(sent, PLANE, step).astype(f32)
    return total


def over_latents(values):
    return in_order(give_back([values] * lax.axis_size("lat"), "lat"), "lat")


def tie(first, second):
    return lax.optimization_barrier((first, second))


def attend_kernel(heads, chunks, own, *refs):
    pieces = refs[:chunks]
    low_refs = refs[chunks : chunks + own]
    att_ref, lse_ref, queries, keys, vals, lows, column = refs[chunks + own :]
    edge = heads * HEAD_DIM
    index = pl.program_id(0)
    block = att_ref.shape[1]

    @pl.when(index == 0)
    def _():
        lane = lax.broadcasted_iota(jnp.int32, vals.shape[1:], 1)
        column[...] = jnp.zeros_like(column)
        for head in range(heads):
            vals[head] = jnp.where(lane == HEAD_DIM, 1.0, 0.0).astype(bf16)
            low = head * HEAD_DIM
            for number, piece in enumerate(pieces):
                count = piece.shape[0]
                rows = slice(number * count, (number + 1) * count)
                if number < own:
                    queries[head, rows] = piece[:, low : low + HEAD_DIM]
                keys[head, rows] = piece[:, edge + low : edge + low + HEAD_DIM]
                vals[head, rows, :HEAD_DIM] = piece[:, 2 * edge + low : 2 * edge + low + HEAD_DIM]

    mine = pl.ds(pl.multiple_of(index * block, block), block)

    def score(head):
        return dot(queries[head, mine, :], keys[head], NT)

    ahead = score(0)
    for head in range(heads):
        scores = ahead
        if head + 1 < heads:
            ahead = score(head + 1)
        top = jnp.max(scores, axis=1, keepdims=True) * FACTOR2
        weights = jnp.exp2(scores * FACTOR2 - top).astype(bf16)
        out = dot(weights, vals[head])
        total = out[:, HEAD_DIM : HEAD_DIM + 1]
        out = out[:, :HEAD_DIM] / total
        att_ref[head] = out
        lows[head, mine, :] = out.astype(bf16)
        column[:, head : head + 1] = top + jnp.log2(total)
    lse_ref[...] = column[...].T[: lse_ref.shape[0]]

    @pl.when(index == pl.num_programs(0) - 1)
    def _():
        for head in range(heads):
            low = head * HEAD_DIM
            for number, ref in enumerate(low_refs):
                count = ref.shape[0]
                ref[:, low : low + HEAD_DIM] = lows[head, number * count : (number + 1) * count, :]


def whole_block(shape):
    return pl.BlockSpec(shape, lambda i: (0,) * len(shape))


def attend(pieces, own, heads):
    count, width = pieces[0].shape
    rows, total = own * count, len(pieces) * count
    block = min(256, rows)
    edge = heads * HEAD_DIM
    slots = -(-heads // 8) * 8
    out = pl.pallas_call(
        partial(attend_kernel, heads, len(pieces), own),
        grid=(rows // block,),
        in_specs=[whole_block((count, width))] * len(pieces),
        out_specs=[whole_block((count, edge))] * own
        + [
            pl.BlockSpec((heads, block, HEAD_DIM), lambda i: (0, i, 0)),
            pl.BlockSpec((slots, block), lambda i: (0, i)),
        ],
        out_shape=[jax.ShapeDtypeStruct((count, edge), bf16)] * own
        + [
            jax.ShapeDtypeStruct((heads, rows, HEAD_DIM), f32),
            jax.ShapeDtypeStruct((slots, rows), f32),
        ],
        scratch_shapes=[
            pltpu.VMEM((heads, rows, HEAD_DIM), bf16),
            pltpu.VMEM((heads, total, HEAD_DIM), bf16),
            pltpu.VMEM((heads, total, LANES), bf16),
            pltpu.VMEM((heads, rows, HEAD_DIM), bf16),
            pltpu.VMEM((block, LANES), f32),
        ],
        cost_estimate=pl.CostEstimate(
            flops=8 * heads * rows * total * LANES,
            transcendentals=heads * rows * total,
            bytes_accessed=4 * total * width,
        ),
        compiler_params=pltpu.CompilerParams(vmem_limit_bytes=VMEM_LIMIT),
    )(*pieces)
    return (out[:own], out[own], out[own + 1])


def attend_back_kernel(heads, chunk, chunks, own, *refs):
    pieces = refs[:chunks]
    grad_refs = refs[chunks : chunks + own]
    att_ref, lse_ref = refs[chunks + own : chunks + own + 2]
    outs = refs[chunks + own + 2 : 2 * chunks + own + 2]
    queries, keys, vals, grads, turned, dq, dk, dv, column = refs[2 * chunks + own + 2 :]
    edge = heads * HEAD_DIM
    index = pl.program_id(0)
    block = att_ref.shape[1]
    total = keys.shape[1]

    @pl.when(index == 0)
    def _():
        turned[...] = jnp.zeros_like(turned)
        column[...] = jnp.zeros_like(column)
        dk[...] = jnp.zeros_like(dk)
        dv[...] = jnp.zeros_like(dv)
        for head in range(heads):
            low = head * HEAD_DIM
            for number, piece in enumerate(pieces):
                count = piece.shape[0]
                rows = slice(number * count, (number + 1) * count)
                if number < own:
                    queries[head, rows] = piece[:, low : low + HEAD_DIM]
                    grads[head, rows] = grad_refs[number][:, low : low + HEAD_DIM]
                key = piece[:, edge + low : edge + low + HEAD_DIM]
                keys[head, rows] = key
                turned[head, :HEAD_DIM, rows] = key.astype(f32).T.astype(bf16)
                vals[head, rows] = piece[:, 2 * edge + low : 2 * edge + low + HEAD_DIM]

    mine = pl.ds(pl.multiple_of(index * block, block), block)
    for head in range(heads):
        column[:, head : head + 1] = jnp.sum(
            att_ref[head] * grads[head, mine, :].astype(f32), axis=1, keepdims=True
        )
    deltas = column[...].T
    for head in range(heads):
        query = queries[head, mine, :]
        grad = grads[head, mine, :]
        lse = lse_ref[head : head + 1, :]
        delta = deltas[head : head + 1, :]
        turned_grad = jnp.zeros((turned.shape[1], block), f32)
        for start in range(0, total, chunk):
            part = slice(start, start + chunk)
            scores = dot(keys[head, part, :], query, NT)
            grad_probs = dot(vals[head, part, :], grad, NT)
            probs = jnp.exp2(scores * FACTOR2 - lse)
            grad_scores = (probs * (grad_probs - delta)).astype(bf16)
            dv[head, part, :] += dot(probs.astype(bf16), grad)
            dk[head, part, :] += dot(grad_scores, query)
            turned_grad += dot(turned[head, :, part], grad_scores)
        dq[head, mine, :] = (turned_grad.T[:, :HEAD_DIM] * FACTOR).astype(bf16)

    @pl.when(index == pl.num_programs(0) - 1)
    def _():
        for number, ref in enumerate(outs):
            count = ref.shape[0]
            rows = slice(number * count, (number + 1) * count)
            ref[...] = jnp.zeros_like(ref)
            for head in range(heads):
                low = head * HEAD_DIM
                if number < own:
                    ref[:, low : low + HEAD_DIM] = dq[head, rows]
                ref[:, edge + low : edge + low + HEAD_DIM] = (dk[head, rows] * FACTOR).astype(bf16)
                ref[:, 2 * edge + low : 2 * edge + low + HEAD_DIM] = dv[head, rows].astype(bf16)


def attend_back(pieces, own, grads, att, lse, heads):
    count, width = pieces[0].shape
    rows, total = own * count, len(pieces) * count
    block = min(256, rows)
    edge = heads * HEAD_DIM
    slots = lse.shape[0]
    return pl.pallas_call(
        partial(attend_back_kernel, heads, min(512, total), len(pieces), own),
        grid=(rows // block,),
        in_specs=[whole_block((count, width))] * len(pieces)
        + [whole_block((count, edge))] * own
        + [
            pl.BlockSpec((heads, block, HEAD_DIM), lambda i: (0, i, 0)),
            pl.BlockSpec((slots, block), lambda i: (0, i)),
        ],
        out_specs=[whole_block((count, width))] * len(pieces),
        out_shape=[jax.ShapeDtypeStruct((count, width), bf16)] * len(pieces),
        scratch_shapes=[
            pltpu.VMEM((heads, rows, HEAD_DIM), bf16),
            pltpu.VMEM((heads, total, HEAD_DIM), bf16),
            pltpu.VMEM((heads, total, HEAD_DIM), bf16),
            pltpu.VMEM((heads, rows, HEAD_DIM), bf16),
            pltpu.VMEM((heads, LANES, total), bf16),
            pltpu.VMEM((heads, rows, HEAD_DIM), bf16),
            pltpu.VMEM((heads, total, HEAD_DIM), f32),
            pltpu.VMEM((heads, total, HEAD_DIM), f32),
            pltpu.VMEM((block, LANES), f32),
        ],
        cost_estimate=pl.CostEstimate(
            flops=20 * heads * rows * total * LANES,
            transcendentals=heads * rows * total,
            bytes_accessed=8 * total * width,
        ),
        compiler_params=pltpu.CompilerParams(vmem_limit_bytes=VMEM_LIMIT),
    )(*pieces, *grads, att, lse)


def head_lanes(part):
    return [slice(low, low + HEAD_DIM) for low in range(0, part, HEAD_DIM)]


def cross_kernel(part, splits, *refs):
    q_refs, k_refs, v_refs, out_refs = (refs[splits * i : splits * (i + 1)] for i in range(4))
    for q_ref, k_ref, v_ref, out_ref in zip(q_refs, k_refs, v_refs, out_refs):
        fill = out_ref.shape[1] - part
        if fill:
            out_ref[:, part:] = jnp.zeros((out_ref.shape[0], fill), bf16)
        for lanes in head_lanes(part):
            scores = dot(q_ref[:, lanes], k_ref[:, lanes], NT) * FACTOR
            weights = jnp.exp(scores - jnp.max(scores, axis=1, keepdims=True))
            probs = weights / jnp.sum(weights, axis=1, keepdims=True)
            out_ref[:, lanes] = dot(probs.astype(bf16), v_ref[:, lanes]).astype(bf16)


def cross(queries, keys, values, part):
    splits = len(queries)
    rows, width = queries[0].shape
    texts = keys[0].shape[0]
    block = min(512, rows)
    split = pl.BlockSpec((block, width), lambda i: (i, 0))
    return pl.pallas_call(
        partial(cross_kernel, part, splits),
        grid=(rows // block,),
        in_specs=[split] * splits + [whole_block((texts, width))] * (2 * splits),
        out_specs=[split] * splits,
        out_shape=[jax.ShapeDtypeStruct((rows, width), bf16)] * splits,
        compiler_params=pltpu.CompilerParams(vmem_limit_bytes=VMEM_LIMIT),
    )(*queries, *keys, *values)


def cross_back_kernel(part, splits, *refs):
    q_refs, k_refs, v_refs, grad_refs, dq_refs, dk_refs, dv_refs, dk_sums, dv_sums = (
        refs[splits * i : splits * (i + 1)] for i in range(9)
    )
    first = pl.program_id(0) == 0
    last = pl.program_id(0) == pl.num_programs(0) - 1
    for q_ref, k_ref, v_ref, grad_ref, dq_ref, dk, dv in zip(
        q_refs, k_refs, v_refs, grad_refs, dq_refs, dk_sums, dv_sums
    ):

        @pl.when(first)
        def _():
            dk[...] = jnp.zeros_like(dk)
            dv[...] = jnp.zeros_like(dv)

        fill = dq_ref.shape[1] - part
        if fill:
            dq_ref[:, part:] = jnp.zeros((dq_ref.shape[0], fill), bf16)
        for lanes in head_lanes(part):
            query = q_ref[:, lanes]
            key = k_ref[:, lanes]
            grad = grad_ref[:, lanes]
            scores = dot(query, key, NT) * FACTOR
            weights = jnp.exp(scores - jnp.max(scores, axis=1, keepdims=True))
            probs = weights / jnp.sum(weights, axis=1, keepdims=True)
            grad_probs = dot(grad, v_ref[:, lanes], NT)
            delta = jnp.sum(probs * grad_probs, axis=1, keepdims=True)
            grad_scores = (probs * (grad_probs - delta)).astype(bf16)
            dq_ref[:, lanes] = (dot(grad_scores, key) * FACTOR).astype(bf16)
            dk[:, lanes] += dot(grad_scores, query, TN)
            dv[:, lanes] += dot(probs.astype(bf16), grad, TN)

    @pl.when(last)
    def _():
        for dk_ref, dv_ref, dk, dv in zip(dk_refs, dv_refs, dk_sums, dv_sums):
            dk_ref[...] = (dk[...] * FACTOR).astype(bf16)
            dv_ref[...] = dv[...].astype(bf16)


def cross_back(queries, keys, values, grads, part):
    splits = len(queries)
    rows, width = queries[0].shape
    texts = keys[0].shape[0]
    block = min(512, rows)
    whole = whole_block((texts, width))
    split = pl.BlockSpec((block, width), lambda i: (i, 0))
    out = pl.pallas_call(
        partial(cross_back_kernel, part, splits),
        grid=(rows // block,),
        in_specs=[split] * splits + [whole] * (2 * splits) + [split] * splits,
        out_specs=[split] * splits + [whole] * (2 * splits),
        out_shape=[jax.ShapeDtypeStruct((rows, width), bf16)] * splits
        + [jax.ShapeDtypeStruct((texts, width), bf16)] * (2 * splits),
        scratch_shapes=[pltpu.VMEM((texts, width), f32)] * (2 * splits),
        compiler_params=pltpu.CompilerParams(vmem_limit_bytes=VMEM_LIMIT),
    )(*queries, *keys, *values, *grads)
    return (out[:splits], out[splits : 2 * splits], out[2 * splits :])


def assemble_kernel(plan, count, *refs):
    sources, (sems,) = refs[:count], refs[-1:]
    outs = refs[count:-1]
    copies = [
        pltpu.make_async_copy(
            sources[source].at[:, pl.ds(column, size)],
            outs[place].at[pl.ds(row, sources[source].shape[0]), :],
            sems.at[number],
        )
        for number, (source, column, size, place, row) in enumerate(plan)
    ]
    for copy in copies:
        copy.start()
    for copy in copies:
        copy.wait()


def assemble(stacks, columns):
    sources = [piece for stack in stacks for piece in stack]
    plan, shapes, base = [], [], 0
    for stack in stacks:
        offset = 0
        for size in columns:
            row = 0
            for number, piece in enumerate(stack):
                plan.append((base + number, offset, size, len(shapes), row))
                row += piece.shape[0]
            shapes.append(jax.ShapeDtypeStruct((row, size), piece.dtype))
            offset += size
        base += len(stack)
    anywhere = pl.BlockSpec(memory_space=pl.ANY)
    out = pl.pallas_call(
        partial(assemble_kernel, plan, len(sources)),
        in_specs=[anywhere] * len(sources),
        out_specs=[anywhere] * len(shapes),
        out_shape=shapes,
        scratch_shapes=[pltpu.SemaphoreType.DMA((len(plan),))],
    )(*sources)
    out = list(out)
    return [out[place : place + len(columns)] for place in range(0, len(out), len(columns))]


def with_others(piece, axes):
    return [piece] + [send_xor(piece, axes, step) for step in range(1, lax.axis_size(axes))]


def gather(shard, columns, tensor_first):
    start = jnp.concatenate(with_others(shard, "lat"))
    if tensor_first and lax.axis_size("tensor") * lax.axis_size(ROW) <= 8:
        stacks = [with_others(piece, ROW) for piece in with_others(start, "tensor")]
    else:
        half = assemble([with_others(start, ROW)], [start.shape[1]])[0][0]
        stacks = [[piece] for piece in with_others(half, "tensor")]
    stacks = [
        stack + [send_xor(piece, "fsdp", step) for step in range(1, lax.axis_size("fsdp")) for piece in stack]
        for stack in stacks
    ]
    return assemble(stacks, columns)


def kept_sums(left, rights, extra=None):
    cores = lax.axis_size("fsdp")
    half = left.shape[1] // cores
    out = []
    for right in rights:
        sums = []
        for core in range(cores):
            rows = slice(core * half, (core + 1) * half)
            total = dot(left[:, rows], right, TN)
            if extra is not None:
                total += extra[rows]
            sums.append(total)
        total = sums[0]
        for core in range(1, cores):
            total += send_xor(sums[core].astype(bf16), "fsdp", core).astype(f32)
        out.append(total.astype(bf16))
    return out


def sum_pieces(pieces, axes, dtype=bf16):
    total = pieces[0].astype(f32)
    for step in range(1, len(pieces)):
        total += send_xor(pieces[step], axes, step).astype(f32)
    return total.astype(dtype)


def row_blocks(piece, count):
    size = piece.shape[0] // count
    return [piece[place * size : (place + 1) * size] for place in range(count)]


def sum_tensor(parts):
    return [sum_pieces(parts, "tensor")]


def sum_row(parts):
    return [sum_pieces(row_blocks(part, lax.axis_size(ROW)), ROW) for part in parts]


def sum_lat(parts):
    return sum_pieces(row_blocks(parts[0], lax.axis_size("lat")), "lat", f32)


def own_order(share, width):
    cores, lats, rows = (lax.axis_size(axes) for axes in ("fsdp", "lat", ROW))
    place = lax.iota(jnp.int32, width)
    block, rest = place // share, place % share
    lat = jnp.bitwise_xor(block % lats, lax.axis_index("lat"))
    row = jnp.bitwise_xor(block // lats % rows, lax.axis_index(ROW))
    core = jnp.bitwise_xor(block // (lats * rows), lax.axis_index("fsdp"))
    natural = ((core * lats + lat) * rows + row) * share + rest
    return (lax.broadcasted_iota(jnp.int32, (width, width), 0) == natural[None, :]).astype(bf16)


def local(
    latents, text, time_vector, table, w_qkv, w_out, w_cq, w_ckv, w_co, w_up, w_down, cotangent
):
    width = latents.shape[2]
    share = w_cq.shape[0]
    part = w_cq.shape[1]
    inner_part = w_up.shape[1]
    splits = lax.axis_size("tensor")
    ranks = lax.axis_size("hr")
    halves = lax.axis_size("sr")
    edge = part // ranks
    heads = edge // HEAD_DIM
    groups = ranks * splits
    piece_width = -(-(3 * edge + 6) // LANES) * LANES
    wide = -(-part // LANES) * LANES
    slot = lax.axis_index("lat")
    rank = lax.axis_index("hr")

    def padded(values):
        return jnp.pad(values, ((0, 0), (0, wide - part)))

    latents_got = exchange(partial(pick, latents), "lat")
    shard_qkv = jnp.transpose(w_qkv.reshape(share, 3, ranks, edge), (2, 0, 1, 3)).reshape(
        ranks, share, 3 * edge
    )
    fill = jnp.pad(table.T, ((0, 0), (0, piece_width - 3 * edge - 6)))
    qkv_full = [
        gather(jnp.concatenate((shard_qkv[place], fill), axis=1), [piece_width], place % 2 == 0)
        for place in range(ranks)
    ]
    mid_shard = jnp.concatenate(
        [padded(piece) for piece in (w_out.T, w_ckv[:, 0], w_ckv[:, 1], w_cq, w_co.T)], axis=1
    )
    mid_shard, qkv_full[0][0][0] = tie(mid_shard, qkv_full[0][0][0])
    mid_full = gather(mid_shard, [wide] * 5, False)
    out_full, key_full, val_full, cq_full, co_full = (
        [full[place] for full in mid_full] for place in range(5)
    )
    up_shard, down_shard, out_full[0] = lax.optimization_barrier((w_up, w_down.T, out_full[0]))
    up_full = [full[0] for full in gather(up_shard, [inner_part], False)]
    down_full = [full[0] for full in gather(down_shard, [inner_part], True)]

    turn = own_order(share, width)
    residual = dot(jnp.concatenate(latents_got, axis=0), turn)
    grad_three = dot(jnp.concatenate(exchange(partial(pick, cotangent), "lat"), axis=0), turn)
    rows = residual.shape[0]
    caption = dot(pick(text, slot), turn).astype(bf16)
    table_full = qkv_full[0][0][0][:, 3 * edge : 3 * edge + 6]
    modulate = table_full.T.astype(f32) + dot(pick(time_vector, slot).reshape(6, width), turn)
    shift_one, scale_one, gate_one, shift_two, scale_two, gate_two = (
        modulate[row : row + 1] for row in range(6)
    )

    normed_one, inverse_one = norm_parts(residual)
    hidden_one = (normed_one * (1.0 + scale_one) + shift_one).astype(bf16)
    mixed = [None] * groups
    for split in range(splits):
        pieces = [dot(hidden_one, full[split][0]).astype(bf16) for full in qkv_full]
        for other in range(ranks):
            step = other * splits + split
            piece = choose(pieces, jnp.bitwise_xor(rank, other))
            mixed[step] = send_xor(piece, HEAD_GROUP, step) if step else piece
    for step in range(1, halves):
        mixed += [send_xor(piece, "sr", step) for piece in mixed[:groups]]
    att_low, att_wide, logsum = attend(mixed, groups, heads)

    def by_split(pieces, split):
        own = [pieces[other * splits + split] for other in range(ranks)]
        return [choose(own, jnp.bitwise_xor(rank, place)) for place in range(ranks)]

    att_back = give_back(att_low, HEAD_GROUP)
    att = [
        padded(jnp.concatenate(by_split(att_back, split), axis=1)) for split in range(splits)
    ]

    out_one = sum(dot(att[split], out_full[split], NT) for split in range(splits))
    after_one = residual + gate_one * out_one
    mid_low = after_one.astype(bf16)
    cross_q = [dot(mid_low, full).astype(bf16) for full in cq_full]
    cross_k = [dot(caption, full).astype(bf16) for full in key_full]
    cross_v = [dot(caption, full).astype(bf16) for full in val_full]
    cross_low = cross(cross_q, cross_k, cross_v, part)
    out_two = sum(dot(cross_low[split], co_full[split], NT) for split in range(splits))
    after_two = after_one + out_two
    normed_two, inverse_two = norm_parts(after_two)
    hidden_two = (normed_two * (1.0 + scale_two) + shift_two).astype(bf16)
    inner = [dot(hidden_two, up_full[split]) for split in range(splits)]
    active = [jax.nn.gelu(values, approximate=True).astype(bf16) for values in inner]
    out_three = sum(dot(active[split], down_full[split], NT) for split in range(splits))
    result = dot((after_two + gate_two * out_three).astype(bf16), turn, NT).astype(bf16)
    result_back = in_order(give_back(list(result.reshape(latents.shape)), "lat"), "lat")

    grad_gate_two = jnp.sum(grad_three * out_three, axis=0)
    grad_z = (gate_two * grad_three).astype(bf16)
    grad_inner = []
    for split in range(splits):
        grad_active = dot(grad_z, down_full[split])
        _, pull = jax.vjp(partial(jax.nn.gelu, approximate=True), inner[split])
        grad_inner.append(pull(grad_active)[0].astype(bf16))
    down_sums = kept_sums(grad_z, active)
    up_sums = kept_sums(hidden_two, grad_inner)
    grad_hidden_two = sum(dot(grad_inner[split], up_full[split], NT) for split in range(splits))
    grad_shift_two = jnp.sum(grad_hidden_two, axis=0)
    grad_scale_two = jnp.sum(grad_hidden_two * normed_two, axis=0)
    grad_two = grad_three + norm_back(grad_hidden_two * (1.0 + scale_two), normed_two, inverse_two)

    grad_out_two = grad_two.astype(bf16)
    grad_cross = [dot(grad_out_two, full).astype(bf16) for full in co_full]
    (grad_cross[0], down_sums, up_sums) = lax.optimization_barrier(
        (grad_cross[0], down_sums, up_sums)
    )
    down_sums, up_sums = sum_tensor(down_sums), sum_row(up_sums)
    grad_cq, grad_ck, grad_cv = cross_back(cross_q, cross_k, cross_v, grad_cross, part)
    grad_one = grad_two + sum(dot(grad_cq[split], cq_full[split], NT) for split in range(splits))
    text_terms = sum(
        dot(grad_ck[split], key_full[split], NT) + dot(grad_cv[split], val_full[split], NT)
        for split in range(splits)
    )

    grad_gate_one = jnp.sum(grad_one * out_one, axis=0)
    grad_out_one = (gate_one * grad_one).astype(bf16)
    grad_att = [dot(grad_out_one, full).astype(bf16) for full in out_full]
    grad_heads = [None] * groups
    for split in range(splits):
        cuts = [grad_att[split][:, place * edge : (place + 1) * edge] for place in range(ranks)]
        for other in range(ranks):
            step = other * splits + split
            piece = choose(cuts, jnp.bitwise_xor(rank, other))
            grad_heads[step] = send_xor(piece, HEAD_GROUP, step) if step else piece
    mid_sums = [
        kept_sums(left, rights)
        for left, rights in (
            (caption, grad_ck),
            (caption, grad_cv),
            (mid_low, grad_cq),
            (grad_out_two, cross_low),
            (grad_out_one, att),
        )
    ]
    (grad_heads[0], down_sums, up_sums, mid_sums) = lax.optimization_barrier(
        (grad_heads[0], down_sums, up_sums, mid_sums)
    )
    down_sums, up_sums = sum_row(down_sums), sum_tensor(up_sums)
    orders = [(sum_tensor, sum_row), (sum_row, sum_tensor)]
    mid_sums = [orders[place % 2][0](sums) for place, sums in enumerate(mid_sums)]
    grad_mix = list(attend_back(mixed, groups, grad_heads, att_wide, logsum, heads))
    (grad_mix[0], down_sums, up_sums, mid_sums) = lax.optimization_barrier(
        (grad_mix[0], down_sums, up_sums, mid_sums)
    )
    for step in range(1, halves):
        for place in range(groups):
            more = send_xor(grad_mix[step * groups + place], "sr", step)
            grad_mix[place] = (grad_mix[place].astype(f32) + more.astype(f32)).astype(bf16)
    grad_proj = give_back(grad_mix[:groups], HEAD_GROUP)
    grad_proj = [by_split(grad_proj, split) for split in range(splits)]
    mid_sums = [orders[place % 2][1](sums) for place, sums in enumerate(mid_sums)]
    grad_hidden_one = sum(
        dot(grad_proj[split][place], qkv_full[place][split][0], NT)
        for place in range(ranks)
        for split in range(splits)
    )
    grad_shift_one = jnp.sum(grad_hidden_one, axis=0)
    grad_scale_one = jnp.sum(grad_hidden_one * normed_one, axis=0)
    grad_latents = grad_one + norm_back(
        grad_hidden_one * (1.0 + scale_one), normed_one, inverse_one
    )
    grad_latents = dot(grad_latents.astype(bf16), turn, NT).astype(bf16).reshape(latents.shape)
    grad_latents = in_order(give_back(list(grad_latents), "lat"), "lat")

    time_terms = jnp.stack(
        (
            grad_shift_one,
            grad_scale_one,
            grad_gate_one,
            grad_shift_two,
            grad_scale_two,
            grad_gate_two,
        )
    )
    table_terms = jnp.pad(time_terms.T, ((0, 0), (3 * edge, piece_width - 3 * edge - 6)))
    one_sums = [
        kept_sums(
            hidden_one,
            [grad_proj[split][place] for split in range(splits)],
            table_terms if place == 0 else None,
        )
        for place in range(ranks)
    ]
    one_sums = [orders[place % 2][0](sums) for place, sums in enumerate(one_sums)]
    one_sums = [sum_lat(orders[place % 2][1](sums)) for place, sums in enumerate(one_sums)]
    key_sum, val_sum, cq_sum, co_sum, out_sum = (sum_lat(sums)[:, :part] for sums in mid_sums)
    time_natural = lax.dot_general(
        time_terms, turn.astype(f32), NT, precision=lax.Precision.HIGHEST
    )
    text_natural = dot(text_terms.astype(bf16), turn, NT)
    grad_time = over_latents(plane_sum(time_natural, f32)).reshape(-1, 6 * width)
    grad_text = over_latents(plane_sum(text_natural, bf16).astype(bf16)).astype(f32)
    grad_qkv = jnp.stack(
        [sums[:, : 3 * edge].reshape(share, 3, edge) for sums in one_sums], axis=2
    ).reshape(share, 3, part)
    return (
        result_back,
        grad_latents.astype(f32),
        grad_text,
        grad_time,
        one_sums[0][:, 3 * edge : 3 * edge + 6].T,
        grad_qkv,
        out_sum.T,
        cq_sum,
        jnp.stack((key_sum, val_sum), axis=1),
        co_sum.T,
        sum_lat(up_sums),
        sum_lat(down_sums).T,
    )


def solution(mesh):
    def run(latents, text, time_vector, table, w_qkv, *others):
        fsdp, context, tensor = (mesh.shape[name] for name in ("fsdp", "context", "tensor"))
        lat = latents.shape[0] // fsdp
        group = context // lat
        ranks = math.gcd(group, w_qkv.shape[2] // (tensor * HEAD_DIM))
        sizes = (fsdp, lat, group // ranks, ranks, tensor)
        finer = Mesh(mesh.devices.reshape(sizes), ("fsdp", "lat", "sr", "hr", "tensor"))
        line = ("lat", "sr", "hr")
        shard = ("fsdp",) + line
        tokens = P("fsdp", line + ("tensor",), None)
        by_row = P(shard, "tensor")
        by_row3 = P(shard, None, "tensor")
        by_column = P("tensor", shard)
        weights = (by_row3, by_column, by_row, by_row3, by_column, by_row, by_column)
        return jax.shard_map(
            local,
            mesh=finer,
            in_specs=(tokens, P("fsdp", None, None), P("fsdp", None), P(None, shard))
            + weights
            + (tokens,),
            out_specs=(tokens, tokens, P("fsdp", None, None), P("fsdp", None), P(None, shard))
            + weights,
            check_vma=False,
        )(latents, text, time_vector, table, w_qkv, *others)

    return run
```

profile of v0, /device:TPU:0, one launch (start us, length us, event | category | flops | bytes accessed | tf_op | source)
XLA Modules:
  0.0 2727.8 jit_solution(3339615792815491422)
XLA Ops:
  62.0 126.2 %shard_map.211 = (bf16[1152,896]{1,0:T(8,128)(2,1)}, bf16[1152,896]{1,0:T(8,128)(2,1)}) custom-call(bf16[288,896]{1,0:T(8,128)(2,1)} %copy-done.38, bf16[288,896]{1,0:T(8,128)(2,1)} %copy-done.81, bf16[288,896]{1,0:T(8,128)(2,1)} %copy-done.83, bf16[288,896]{1,0:T(8,128)(2,1)} %copy-done.85, bf16[288,896]{1,0:T(8,128)(2,1)} %copy-done.80, ...), custom_call_target="tpu_custom_call" | custom-call | tf_op jit(solution)/shard_map/pallas_call | solution.py:417
  193.8 27.4 %collective-permute-done.24 = bf16[72,3200]{1,0:T(8,128)(2,1)S(1)} collective-permute-done((bf16[72,3200]{1,0:T(8,128)(2,1)}, bf16[72,3200]{1,0:T(8,128)(2,1)S(1)}, u32[]{:S(2)}, u32[]{:S(2)}) %collective-permute-start.24) | collective-permute-done | bytes 460832 | tf_op jit(solution)/shard_map/ppermute | solution.py:49
  231.6 40.3 %collective-permute-done.27.refs_1_ = bf16[288,3200]{1,0:T(8,128)(2,1)} collective-permute-done((bf16[288,3200]{1,0:T(8,128)(2,1)S(1)}, bf16[288,3200]{1,0:T(8,128)(2,1)}, u32[]{:S(2)}, u32[]{:S(2)}) %collective-permute-start.27) | collective-permute-done | bytes 1843232 | tf_op jit(solution)/shard_map/ppermute | solution.py:49
  272.0 112.8 %shard_map.215.refs_0_ = bf16[576,3200]{1,0:T(8,128)(2,1)} custom-call(bf16[288,3200]{1,0:T(8,128)(2,1)} %copy-done.28, bf16[288,3200]{1,0:T(8,128)(2,1)} %collective-permute-done.27.refs_1_), custom_call_target="tpu_custom_call" | custom-call | tf_op jit(solution)/shard_map/pallas_call | solution.py:417
  397.9 67.6 %collective-permute-done.29.refs_2_ = bf16[576,3200]{1,0:T(8,128)(2,1)} collective-permute-done((bf16[576,3200]{1,0:T(8,128)(2,1)}, bf16[576,3200]{1,0:T(8,128)(2,1)}, u32[]{:S(2)}, u32[]{:S(2)}) %collective-permute-start.29) | collective-permute-done | bytes 3686432 | tf_op jit(solution)/shard_map/ppermute | solution.py:49
  466.8 32.4 %shard_map.212.refs_0_ = bf16[576,896]{1,0:T(8,128)(2,1)} custom-call(bf16[288,896]{1,0:T(8,128)(2,1)} %copy-done.37, bf16[288,896]{1,0:T(8,128)(2,1)} %copy-done.79), custom_call_target="tpu_custom_call" | custom-call | tf_op jit(solution)/shard_map/pallas_call | solution.py:417
  505.8 19.0 collective-permute-done.18.refs_2_
  533.2 126.2 %shard_map.213 = (bf16[1152,896]{1,0:T(8,128)(2,1)}, bf16[1152,896]{1,0:T(8,128)(2,1)}) custom-call(bf16[576,896]{1,0:T(8,128)(2,1)} %shard_map.212.refs_0_, bf16[576,896]{1,0:T(8,128)(2,1)} %copy-done.61, bf16[576,896]{1,0:T(8,128)(2,1)} %copy-done.60, bf16[576,896]{1,0:T(8,128)(2,1)} %collective-permute-done.19.refs_3_), custom_call_target="tpu_custom_call" | custom-call | tf_op jit(solution)/shard_map/pallas_call | solution.py:417
  672.2 448.0 %shard_map.216 = (bf16[1152,640]{1,0:T(8,128)(2,1)}, bf16[1152,640]{1,0:T(8,128)(2,1)}, bf16[1152,640]{1,0:T(8,128)(2,1)}, bf16[1152,640]{1,0:T(8,128)(2,1)}, bf...) custom-call(bf16[576,3200]{1,0:T(8,128)(2,1)} %shard_map.215.refs_0_, ...), custom_call_target="tpu_custom_call" | custom-call | tf_op jit(solution)/shard_map/pallas_call | solution.py:417
  1131.4 15.1 collective-permute-done.34
  1158.2 15.4 collective-permute-start.54
  1175.1 32.2 %shard_map.214 = (bf16[512,288]{1,0:T(8,128)(2,1)}, bf16[512,288]{1,0:T(8,128)(2,1)}, bf16[512,288]{1,0:T(8,128)(2,1)}, bf16[512,288]{1,0:T(8,128)(2,1)}, f32[4,2048,72]{2,1,0:T(8,128)}, /*index=5*/f32[8,2048]{1,0:T(8,128)}) custom-call(bf16[512,896]{1,0:T(8,128)(2,1)} %get-tuple-element.234.refs_0_, bf16[512,896]{1,0:T(8,128)(2,1)} %collective-permute-done.20.refs_1_, ...), custom_call_target="tpu_custom_call" | custom-call | flops 17179869184 | bytes 7340032 | tf_op jit(solution)/shard_map/pallas_call | solution.py:159
  1227.4 81.5 %shard_map.218.refs_0_ = bf16[576,2304]{1,0:T(8,128)(2,1)} custom-call(bf16[288,2304]{1,0:T(8,128)(2,1)} %copy-done.34, bf16[288,2304]{1,0:T(8,128)(2,1)} %collective-permute-done.36.refs_1_), custom_call_target="tpu_custom_call" | custom-call | tf_op jit(solution)/shard_map/pallas_call | solution.py:417
  1323.3 60.6 %collective-permute-done.46.refs_4_ = bf16[288,2304]{1,0:T(8,128)(2,1)} collective-permute-done((bf16[288,2304]{1,0:T(8,128)(2,1)}, bf16[288,2304]{1,0:T(8,128)(2,1)}, u32[]{:S(2)}, u32[]{:S(2)}) %collective-permute-start.46) | collective-permute-done | bytes 1327136 | tf_op jit(solution)/shard_map/ppermute | solution.py:49
  1391.1 11.9 shard_map.217
  1414.2 322.8 %shard_map.220 = (bf16[1152,2304]{1,0:T(8,128)(2,1)}, bf16[1152,2304]{1,0:T(8,128)(2,1)}) custom-call(bf16[288,2304]{1,0:T(8,128)(2,1)} %constant_dynamic-update-slice_fusion.8.refs_0_, bf16[288,2304]{1,0:T(8,128)(2,1)} %collective-permute-done.43.refs_1_, bf16[288,2304]{1,0:T(8,128)(2,1)} %collective-permute-done.44.refs_2_, bf16[288,2304]{1,0:T(8,128)(2,1)} %copy-done.54, ...), custom_call_target="tpu_custom_call" | custom-call | tf_op jit(solution)/shard_map/pallas_call | solution.py:417
  1737.0 322.8 %shard_map.219 = (bf16[1152,2304]{1,0:T(8,128)(2,1)}, bf16[1152,2304]{1,0:T(8,128)(2,1)}) custom-call(bf16[576,2304]{1,0:T(8,128)(2,1)} %shard_map.218.refs_0_, bf16[576,2304]{1,0:T(8,128)(2,1)} %collective-permute-done.37.refs_1_, bf16[576,2304]{1,0:T(8,128)(2,1)} %collective-permute-done.38.refs_2_, bf16[576,2304]{1,0:T(8,128)(2,1)} %collective-permute-done.39.refs_3_), custom_call_target="tpu_custom_call" | custom-call | tf_op jit(solution)/shard_map/pallas_call | solution.py:417
  2130.4 15.7 collective-permute-done.51
  2168.7 18.8 shard_map.221
  2233.1 12.8 collective-permute-done.95
  2263.7 20.7 collective-permute-done.62
  2287.3 25.6 collective-permute-done.61
  2333.3 57.9 %shard_map.222 = (bf16[512,896]{1,0:T(8,128)(2,1)}, bf16[512,896]{1,0:T(8,128)(2,1)}, bf16[512,896]{1,0:T(8,128)(2,1)}, bf16[512,896]{1,0:T(8,128)(2,1)}) custom-call(bf16[512,896]{1,0:T(8,128)(2,1)} %get-tuple-element.234.refs_0_, bf16[512,896]{1,0:T(8,128)(2,1)} %collective-permute-done.20.refs_1_, bf16[512,896]{1,0:T(8,128)(2,1)} %collective-permute-done.21.refs_2_, ...), custom_call_target="tpu_custom_call" | custom-call | flops 42949672960 | bytes 14680064 | tf_op jit(solution)/shard_map/pallas_call | solution.py:263
  2413.5 13.4 collective-permute-done.85
  2428.7 18.7 collective-permute-done.86
  2447.4 18.9 collective-permute-done.87
  2475.7 16.7 collective-permute-done.78
  2547.3 12.2 collective-permute-done.89
  2561.1 14.5 collective-permute-start.139
  2579.4 23.6 collective-permute-done.139
  2606.0 12.8 collective-permute-done.142
  2683.4 10.0 collective-permute-done.105
  (792 shorter events, 570.1 us)
Async XLA Ops:
  384.8 80.7 %collective-permute-start.29 = (bf16[576,3200]{1,0:T(8,128)(2,1)}, bf16[576,3200]{1,0:T(8,128)(2,1)}, u32[]{:S(2)}, u32[]{:S(2)}) collective-permute-start(bf16[576,3200]{1,0:T(8,128)(2,1)} %shard_map.215.refs_0_), channel_id=1, source_target_pairs={{0,1},{1,0},{2,3},{3,2},{4,5},{5,4},{6,7},{7,6},{8,9},{9,8},{10,11... | collective-permute-start | bytes 11059208 | tf_op jit(solution)/shard_map/ppermute | solution.py:49
  389.5 109.6 %collective-permute-start = (bf16[128,1152]{1,0:T(8,128)(2,1)}, bf16[128,1152]{1,0:T(8,128)(2,1)}, u32[]{:S(2)}, u32[]{:S(2)}) collective-permute-start(bf16[128,1152]{1,0:T(8,128)(2,1)} %get-tuple-element.252), channel_id=1, source_target_pairs={{0,4},{4,0},{8,12},{12,8},{1,5},{5,1},{9,13},{13,9},{2,6},{6,2},{1... | collective-permute-start | bytes 884744 | tf_op jit(solution)/shard_map/ppermute | solution.py:49
  389.5 109.7 %collective-permute-start.2 = (bf16[128,1152]{1,0:T(8,128)(2,1)}, bf16[128,1152]{1,0:T(8,128)(2,1)}, u32[]{:S(2)}, u32[]{:S(2)}) collective-permute-start(bf16[128,1152]{1,0:T(8,128)(2,1)} %get-tuple-element.253), channel_id=1, source_target_pairs={{0,12},{4,8},{8,4},{12,0},{1,13},{5,9},{9,5},{13,1},{2,14},{6,10},... | collective-permute-start | bytes 884744 | tf_op jit(solution)/shard_map/ppermute | solution.py:49
  390.8 109.4 %collective-permute-start.1 = (bf16[128,1152]{1,0:T(8,128)(2,1)}, bf16[128,1152]{1,0:T(8,128)(2,1)}, u32[]{:S(2)}, u32[]{:S(2)}) collective-permute-start(bf16[128,1152]{1,0:T(8,128)(2,1)} %get-tuple-element.254), channel_id=1, source_target_pairs={{0,8},{4,12},{8,0},{12,4},{1,9},{5,13},{9,1},{13,5},{2,10},{6,14},... | collective-permute-start | bytes 884744 | tf_op jit(solution)/shard_map/ppermute | solution.py:49
  397.9 273.8 %collective-permute-start.28 = (bf16[576,3200]{1,0:T(8,128)(2,1)}, bf16[576,3200]{1,0:T(8,128)(2,1)}, u32[]{:S(2)}, u32[]{:S(2)}) collective-permute-start(bf16[576,3200]{1,0:T(8,128)(2,1)} %shard_map.215.refs_0_), channel_id=1, source_target_pairs={{0,16},{16,0},{1,17},{17,1},{2,18},{18,2},{3,19},{19,3},{4,20},{20... | collective-permute-start | bytes 11059208 | tf_op jit(solution)/shard_map/ppermute | solution.py:49
  465.5 206.7 %collective-permute-start.30 = (bf16[576,3200]{1,0:T(8,128)(2,1)}, bf16[576,3200]{1,0:T(8,128)(2,1)}, u32[]{:S(2)}, u32[]{:S(2)}) collective-permute-start(bf16[576,3200]{1,0:T(8,128)(2,1)} %collective-permute-done.29.refs_2_), channel_id=1, source_target_pairs={{0,16},{16,0},{1,17},{17,1},{2,18},{18,2},{3,19},{19,3},{4,20},{20... | collective-permute-start | bytes 11059208 | tf_op jit(solution)/shard_map/ppermute | solution.py:49
  499.2 708.7 %collective-permute-start.53 = (bf16[128,1152]{1,0:T(8,128)(2,1)}, bf16[128,1152]{1,0:T(8,128)(2,1)}, u32[]{:S(2)}, u32[]{:S(2)}) collective-permute-start(bf16[128,1152]{1,0:T(8,128)(2,1)} %get-tuple-element.245), channel_id=1, source_target_pairs={{0,4},{4,0},{8,12},{12,8},{1,5},{5,1},{9,13},{13,9},{2,6},{6,2},{1... | collective-permute-start | bytes 884744 | tf_op jit(solution)/shard_map/ppermute | solution.py:49
  665.9 492.3 %collective-permute-start.22 = (bf16[512,896]{1,0:T(8,128)(2,1)}, bf16[512,896]{1,0:T(8,128)(2,1)}, u32[]{:S(2)}, u32[]{:S(2)}) collective-permute-start(bf16[512,896]{1,0:T(8,128)(2,1)} %get-tuple-element.231), channel_id=1, source_target_pairs={{0,3},{1,2},{2,1},{3,0},{4,7},{5,6},{6,5},{7,4},{8,11},{9,10},{10,... | collective-permute-start | bytes 2752520 | tf_op jit(solution)/shard_map/ppermute | solution.py:49
  667.7 505.9 %collective-permute-start.20 = (bf16[512,896]{1,0:T(8,128)(2,1)}, bf16[512,896]{1,0:T(8,128)(2,1)}, u32[]{:S(2)}, u32[]{:S(2)}) collective-permute-start(bf16[512,896]{1,0:T(8,128)(2,1)} %get-tuple-element.232), channel_id=1, source_target_pairs={{0,1},{1,0},{2,3},{3,2},{4,5},{5,4},{6,7},{7,6},{8,9},{9,8},{10,11... | collective-permute-start | bytes 2752520 | tf_op jit(solution)/shard_map/ppermute | solution.py:49
  671.6 503.4 %collective-permute-start.21 = (bf16[512,896]{1,0:T(8,128)(2,1)}, bf16[512,896]{1,0:T(8,128)(2,1)}, u32[]{:S(2)}, u32[]{:S(2)}) collective-permute-start(bf16[512,896]{1,0:T(8,128)(2,1)} %get-tuple-element.233), channel_id=1, source_target_pairs={{0,2},{1,3},{2,0},{3,1},{4,6},{5,7},{6,4},{7,5},{8,10},{9,11},{10,... | collective-permute-start | bytes 2752520 | tf_op jit(solution)/shard_map/ppermute | solution.py:49
  1221.2 92.0 %collective-permute-start.42 = (bf16[72,2304]{1,0:T(8,128)(2,1)}, bf16[72,2304]{1,0:T(8,128)(2,1)}, u32[]{:S(2)}, u32[]{:S(2)}) collective-permute-start(bf16[72,2304]{1,0:T(8,128)(2,1)} %bitcast.11), channel_id=1, source_target_pairs={{0,12},{4,8},{8,4},{12,0},{1,13},{5,9},{9,5},{13,1},{2,14},{6,10},... | collective-permute-start | bytes 995336 | tf_op jit(solution)/shard_map/ppermute | solution.py:49
  1223.2 88.3 %collective-permute-start.41 = (bf16[72,2304]{1,0:T(8,128)(2,1)}, bf16[72,2304]{1,0:T(8,128)(2,1)}, u32[]{:S(2)}, u32[]{:S(2)}) collective-permute-start(bf16[72,2304]{1,0:T(8,128)(2,1)} %bitcast.11), channel_id=1, source_target_pairs={{0,8},{4,12},{8,0},{12,4},{1,9},{5,13},{9,1},{13,5},{2,10},{6,14},... | collective-permute-start | bytes 995336 | tf_op jit(solution)/shard_map/ppermute | solution.py:49
  1223.2 86.5 %collective-permute-start.40 = (bf16[72,2304]{1,0:T(8,128)(2,1)}, bf16[72,2304]{1,0:T(8,128)(2,1)}, u32[]{:S(2)}, u32[]{:S(2)}) collective-permute-start(bf16[72,2304]{1,0:T(8,128)(2,1)} %bitcast.11), channel_id=1, source_target_pairs={{0,4},{4,0},{8,12},{12,8},{1,5},{5,1},{9,13},{13,9},{2,6},{6,2},{1... | collective-permute-start | bytes 995336 | tf_op jit(solution)/shard_map/ppermute | solution.py:49
  1308.9 78.6 %collective-permute-start.38 = (bf16[576,2304]{1,0:T(8,128)(2,1)}, bf16[576,2304]{1,0:T(8,128)(2,1)}, u32[]{:S(2)}, u32[]{:S(2)}) collective-permute-start(bf16[576,2304]{1,0:T(8,128)(2,1)} %shard_map.218.refs_0_), channel_id=1, source_target_pairs={{0,1},{1,0},{2,3},{3,2},{4,5},{5,4},{6,7},{7,6},{8,9},{9,8},{10,11... | collective-permute-start | bytes 7962632 | tf_op jit(solution)/shard_map/ppermute | solution.py:49
  1315.1 68.8 %collective-permute-start.46 = (bf16[288,2304]{1,0:T(8,128)(2,1)}, bf16[288,2304]{1,0:T(8,128)(2,1)}, u32[]{:S(2)}, u32[]{:S(2)}) collective-permute-start(bf16[288,2304]{1,0:T(8,128)(2,1)} %constant_dynamic-update-slice_fusion.8.refs_0_), channel_id=1, source_target_pairs={{0,1},{1,0},{2,3},{3,2},{4,5},{5,4},{6,7},{7,6},{8,9},{9,8},{10,11... | collective-permute-start | bytes 3981320 | tf_op jit(solution)/shard_map/ppermute | solution.py:49
  1322.6 83.3 %collective-permute-start.44 = (bf16[288,2304]{1,0:T(8,128)(2,1)}, bf16[288,2304]{1,0:T(8,128)(2,1)}, u32[]{:S(2)}, u32[]{:S(2)}) collective-permute-start(bf16[288,2304]{1,0:T(8,128)(2,1)} %constant_dynamic-update-slice_fusion.8.refs_0_), channel_id=1, source_target_pairs={{0,16},{16,0},{1,17},{17,1},{2,18},{18,2},{3,19},{19,3},{4,20},{20... | collective-permute-start | bytes 3981320 | tf_op jit(solution)/shard_map/ppermute | solution.py:49
  1322.7 83.3 %collective-permute-start.43 = (bf16[288,2304]{1,0:T(8,128)(2,1)}, bf16[288,2304]{1,0:T(8,128)(2,1)}, u32[]{:S(2)}, u32[]{:S(2)}) collective-permute-start(bf16[288,2304]{1,0:T(8,128)(2,1)} %constant_dynamic-update-slice_fusion.8.refs_0_), channel_id=1, source_target_pairs={{0,2},{2,0},{1,3},{3,1},{4,6},{6,4},{5,7},{7,5},{8,10},{10,8},{9,1... | collective-permute-start | bytes 3981320 | tf_op jit(solution)/shard_map/ppermute | solution.py:49
  1387.5 349.4 %collective-permute-start.37 = (bf16[576,2304]{1,0:T(8,128)(2,1)}, bf16[576,2304]{1,0:T(8,128)(2,1)}, u32[]{:S(2)}, u32[]{:S(2)}) collective-permute-start(bf16[576,2304]{1,0:T(8,128)(2,1)} %shard_map.218.refs_0_), channel_id=1, source_target_pairs={{0,16},{16,0},{1,17},{17,1},{2,18},{18,2},{3,19},{19,3},{4,20},{20... | collective-permute-start | bytes 7962632 | tf_op jit(solution)/shard_map/ppermute | solution.py:49
  1387.5 349.4 %collective-permute-start.39 = (bf16[576,2304]{1,0:T(8,128)(2,1)}, bf16[576,2304]{1,0:T(8,128)(2,1)}, u32[]{:S(2)}, u32[]{:S(2)}) collective-permute-start(bf16[576,2304]{1,0:T(8,128)(2,1)} %collective-permute-done.38.refs_2_), channel_id=1, source_target_pairs={{0,16},{16,0},{1,17},{17,1},{2,18},{18,2},{3,19},{19,3},{4,20},{20... | collective-permute-start | bytes 7962632 | tf_op jit(solution)/shard_map/ppermute | solution.py:49
  2088.5 68.5 %collective-permute-start.57 = (bf16[576,2304]{1,0:T(8,128)(2,1)}, bf16[576,2304]{1,0:T(8,128)(2,1)}, u32[]{:S(2)}, u32[]{:S(2)}) collective-permute-start(bf16[576,2304]{1,0:T(8,128)(2,1)} %convolution_convert_fusion.2), channel_id=1, source_target_pairs={{0,16},{16,0},{1,17},{17,1},{2,18},{18,2},{3,19},{19,3},{4,20},{20... | collective-permute-start | bytes 7962632 | tf_op jit(solution)/shard_map/ppermute | solution.py:49
  2256.6 66.8 %collective-permute-start.75 = (bf16[512,288]{1,0:T(8,128)(2,1)S(1)}, bf16[512,288]{1,0:T(8,128)(2,1)S(1)}, u32[]{:S(2)}, u32[]{:S(2)}) collective-permute-start(bf16[512,288]{1,0:T(8,128)(2,1)S(1)} %get-tuple-element.263), channel_id=1, source_target_pairs={{0,3},{1,2},{2,1},{3,0},{4,7},{5,6},{6,5},{7,4},{8,11},{9,10},{10,... | collective-permute-start | bytes 884744 | tf_op jit(solution)/shard_map/ppermute | solution.py:49
  2260.4 70.5 %collective-permute-start.73 = (bf16[512,288]{1,0:T(8,128)(2,1)S(1)}, bf16[512,288]{1,0:T(8,128)(2,1)S(1)}, u32[]{:S(2)}, u32[]{:S(2)}) collective-permute-start(bf16[512,288]{1,0:T(8,128)(2,1)S(1)} %get-tuple-element.264), channel_id=1, source_target_pairs={{0,1},{1,0},{2,3},{3,2},{4,5},{5,4},{6,7},{7,6},{8,9},{9,8},{10,11... | collective-permute-start | bytes 884744 | tf_op jit(solution)/shard_map/ppermute | solution.py:49
  2317.9 73.5 %collective-permute-start.84 = (bf16[288,640]{1,0:T(8,128)(2,1)}, bf16[288,640]{1,0:T(8,128)(2,1)}, u32[]{:S(2)}, u32[]{:S(2)}) collective-permute-start(bf16[288,640]{1,0:T(8,128)(2,1)} %slice.377), channel_id=1, source_target_pairs={{0,2},{2,0},{1,3},{3,1},{4,6},{6,4},{5,7},{7,5},{8,10},{10,8},{9,1... | collective-permute-start | bytes 1105928 | tf_op jit(solution)/shard_map/ppermute | solution.py:49
  2318.5 75.8 %collective-permute-start.83 = (bf16[288,640]{1,0:T(8,128)(2,1)}, bf16[288,640]{1,0:T(8,128)(2,1)}, u32[]{:S(2)}, u32[]{:S(2)}) collective-permute-start(bf16[288,640]{1,0:T(8,128)(2,1)} %slice.375), channel_id=1, source_target_pairs={{0,2},{2,0},{1,3},{3,1},{4,6},{6,4},{5,7},{7,5},{8,10},{10,8},{9,1... | collective-permute-start | bytes 1105928 | tf_op jit(solution)/shard_map/ppermute | solution.py:49
  2323.4 73.8 %collective-permute-start.81 = (bf16[288,640]{1,0:T(8,128)(2,1)}, bf16[288,640]{1,0:T(8,128)(2,1)}, u32[]{:S(2)}, u32[]{:S(2)}) collective-permute-start(bf16[288,640]{1,0:T(8,128)(2,1)} %slice.373), channel_id=1, source_target_pairs={{0,2},{2,0},{1,3},{3,1},{4,6},{6,4},{5,7},{7,5},{8,10},{10,8},{9,1... | collective-permute-start | bytes 1105928 | tf_op jit(solution)/shard_map/ppermute | solution.py:49
  2330.9 70.0 %collective-permute-start.80 = (bf16[288,640]{1,0:T(8,128)(2,1)S(1)}, bf16[288,640]{1,0:T(8,128)(2,1)}, u32[]{:S(2)}, u32[]{:S(2)}) collective-permute-start(bf16[288,640]{1,0:T(8,128)(2,1)S(1)} %slice.371), channel_id=1, source_target_pairs={{0,2},{2,0},{1,3},{3,1},{4,6},{6,4},{5,7},{7,5},{8,10},{10,8},{9,1... | collective-permute-start | bytes 1105928 | tf_op jit(solution)/shard_map/ppermute | solution.py:49
  2331.6 72.1 %collective-permute-start.79 = (bf16[576,640]{1,0:T(8,128)(2,1)S(1)}, bf16[576,640]{1,0:T(8,128)(2,1)}, u32[]{:S(2)}, u32[]{:S(2)}) collective-permute-start(bf16[576,640]{1,0:T(8,128)(2,1)S(1)} %add_convert_fusion.31), channel_id=1, source_target_pairs={{0,1},{1,0},{2,3},{3,2},{4,5},{5,4},{6,7},{7,6},{8,9},{9,8},{10,11... | collective-permute-start | bytes 2211848 | tf_op jit(solution)/shard_map/ppermute | solution.py:49
  2400.9 65.4 %collective-permute-start.87 = (bf16[512,896]{1,0:T(8,128)(2,1)S(1)}, bf16[512,896]{1,0:T(8,128)(2,1)S(1)}, u32[]{:S(2)}, u32[]{:S(2)}) collective-permute-start(bf16[512,896]{1,0:T(8,128)(2,1)S(1)} %copy-done.123), channel_id=1, source_target_pairs={{0,1},{1,0},{2,3},{3,2},{4,5},{5,4},{6,7},{7,6},{8,9},{9,8},{10,11... | collective-permute-start | bytes 2752520 | tf_op jit(solution)/shard_map/ppermute | solution.py:49
  2403.7 90.1 %collective-permute-start.76 = (bf16[512,896]{1,0:T(8,128)(2,1)S(1)}, bf16[512,896]{1,0:T(8,128)(2,1)S(1)}, u32[]{:S(2)}, u32[]{:S(2)}) collective-permute-start(bf16[512,896]{1,0:T(8,128)(2,1)S(1)} %copy-done.122), channel_id=1, source_target_pairs={{0,2},{1,3},{2,0},{3,1},{4,6},{5,7},{6,4},{7,5},{8,10},{9,11},{10,... | collective-permute-start | bytes 2752520 | tf_op jit(solution)/shard_map/ppermute | solution.py:49
  2426.9 65.5 %collective-permute-start.78 = (bf16[288,2304]{1,0:T(8,128)(2,1)}, bf16[288,2304]{1,0:T(8,128)(2,1)S(1)}, u32[]{:S(2)}, u32[]{:S(2)}) collective-permute-start(bf16[288,2304]{1,0:T(8,128)(2,1)} %add_convert_fusion.7), channel_id=1, source_target_pairs={{0,1},{1,0},{2,3},{3,2},{4,5},{5,4},{6,7},{7,6},{8,9},{9,8},{10,11... | collective-permute-start | bytes 3981320 | tf_op jit(solution)/shard_map/ppermute | solution.py:49
  2468.4 188.2 %collective-permute-start.112 = (bf16[576,896]{1,0:T(8,128)(2,1)}, bf16[576,896]{1,0:T(8,128)(2,1)}, u32[]{:S(2)}, u32[]{:S(2)}) collective-permute-start(bf16[576,896]{1,0:T(8,128)(2,1)} %convolution_convert_fusion.4), channel_id=1, source_target_pairs={{0,16},{16,0},{1,17},{17,1},{2,18},{18,2},{3,19},{19,3},{4,20},{20... | collective-permute-start | bytes 3096584 | tf_op jit(solution)/shard_map/ppermute | solution.py:49
  2525.4 95.7 %collective-permute-start.126 = (bf16[288,640]{1,0:T(8,128)(2,1)S(1)}, bf16[288,640]{1,0:T(8,128)(2,1)S(1)}, u32[]{:S(2)}, u32[]{:S(2)}) collective-permute-start(bf16[288,640]{1,0:T(8,128)(2,1)S(1)} %slice.414), channel_id=1, source_target_pairs={{0,2},{2,0},{1,3},{3,1},{4,6},{6,4},{5,7},{7,5},{8,10},{10,8},{9,1... | collective-permute-start | bytes 1105928 | tf_op jit(solution)/shard_map/ppermute | solution.py:49
  (263 other events, 9095.1 us)
where the time goes:
time: 2740 us; the launch traced here: 2730 us
  Pallas kernels  1690 us (62%)
  waiting for transfers between devices  581 us (21%)
  matrix products  184 us (7%)
  starting transfers between devices  180 us (7%)
  local copies, waits for them, and re-layouts  50 us (2%)
  other arithmetic  36.2 us (1%)
    pallas_call x8, Pallas kernels, assemble(): pl.pallas_call(partial(assemble_kernel, plan, len(sources)), in_specs=[an...  1570 us
    ppermute x144, waiting for transfers between devices, send_xor(): lax.ppermute(piece, axes, [(rank, rank ^ step) for rank in range(size)])  581 us
    ppermute x144, starting transfers between devices, send_xor(): lax.ppermute(piece, axes, [(rank, rank ^ step) for rank in range(size)])  180 us
    dot_general x78, matrix products, dot(): return lax.dot_general(left, right, dims, preferred_element_type=f32)  180 us
    pallas_call x1, Pallas kernels, attend_back(): pl.pallas_call(partial(attend_back_kernel, heads, min(512, total), len(pi...  57.9 us
  transfers between devices with their start and end apart: 144, of which 52 were waited for; matrix products, arithmetic and copies ran while one was open for 8% of the time, Pallas kernels for 41%

commit v1 on v0

--- a/solution.py
+++ b/solution.py
@@ -417,9 +417,10 @@
     out = pl.pallas_call(
         partial(assemble_kernel, plan, len(sources)),
         in_specs=[anywhere] * len(sources),
-        out_specs=[anywhere] * len(shapes),
+        out_specs=[pl.BlockSpec(memory_space=pltpu.VMEM)] * len(shapes),
         out_shape=shapes,
         scratch_shapes=[pltpu.SemaphoreType.DMA((len(plan),))],
+        compiler_params=pltpu.CompilerParams(vmem_limit_bytes=VMEM_LIMIT),
     )(*sources)
     out = list(out)
     return [out[place : place + len(columns)] for place in range(0, len(out), len(columns))]
@@ -436,11 +437,12 @@
     else:
         half = assemble([with_others(start, ROW)], [start.shape[1]])[0][0]
         stacks = [[piece] for piece in with_others(half, "tensor")]
+    token = stacks[0][-1]
     stacks = [
         stack + [send_xor(piece, "fsdp", step) for step in range(1, lax.axis_size("fsdp")) for piece in stack]
         for stack in stacks
     ]
-    return assemble(stacks, columns)
+    return assemble(stacks, columns), token
 
 
 def kept_sums(left, rights, extra=None):
@@ -523,21 +525,24 @@
         ranks, share, 3 * edge
     )
     fill = jnp.pad(table.T, ((0, 0), (0, piece_width - 3 * edge - 6)))
-    qkv_full = [
+    qkv_got = [
         gather(jnp.concatenate((shard_qkv[place], fill), axis=1), [piece_width], place % 2 == 0)
         for place in range(ranks)
     ]
     mid_shard = jnp.concatenate(
         [padded(piece) for piece in (w_out.T, w_ckv[:, 0], w_ckv[:, 1], w_cq, w_co.T)], axis=1
     )
-    mid_shard, qkv_full[0][0][0] = tie(mid_shard, qkv_full[0][0][0])
-    mid_full = gather(mid_shard, [wide] * 5, False)
+    qkv_full = [full for full, _ in qkv_got]
+    mid_shard = lax.optimization_barrier([mid_shard] + [token for _, token in qkv_got])[0]
+    mid_full, token = gather(mid_shard, [wide] * 5, False)
     out_full, key_full, val_full, cq_full, co_full = (
         [full[place] for full in mid_full] for place in range(5)
     )
-    up_shard, down_shard, out_full[0] = lax.optimization_barrier((w_up, w_down.T, out_full[0]))
-    up_full = [full[0] for full in gather(up_shard, [inner_part], False)]
-    down_full = [full[0] for full in gather(down_shard, [inner_part], True)]
+    up_shard, down_shard, _ = lax.optimization_barrier((w_up, w_down.T, token))
+    up_got, token = gather(up_shard, [inner_part], False)
+    down_got, other_token = gather(down_shard, [inner_part], True)
+    up_full, down_full = ([full[0] for full in got] for got in (up_got, down_got))
+    cotangent, _, _ = lax.optimization_barrier((cotangent, token, other_token))
 
     turn = own_order(share, width)
     residual = dot(jnp.concatenate(latents_got, axis=0), turn)
@@ -636,8 +641,8 @@
             (grad_out_one, att),
         )
     ]
-    (grad_heads[0], down_sums, up_sums, mid_sums) = lax.optimization_barrier(
-        (grad_heads[0], down_sums, up_sums, mid_sums)
+    (grad_heads[0], down_sums, up_sums, mid_sums, result_back) = lax.optimization_barrier(
+        (grad_heads[0], down_sums, up_sums, mid_sums, result_back)
     )
     down_sums, up_sums = sum_row(down_sums), sum_tensor(up_sums)
     orders = [(sum_tensor, sum_row), (sum_row, sum_tensor)]
@@ -653,6 +658,10 @@
     grad_proj = give_back(grad_mix[:groups], HEAD_GROUP)
     grad_proj = [by_split(grad_proj, split) for split in range(splits)]
     mid_sums = [orders[place % 2][1](sums) for place, sums in enumerate(mid_sums)]
+    up_sum, down_sum = sum_lat(up_sums), sum_lat(down_sums)
+    (grad_proj, mid_sums, up_sum, down_sum) = lax.optimization_barrier(
+        (grad_proj, mid_sums, up_sum, down_sum)
+    )
     grad_hidden_one = sum(
         dot(grad_proj[split][place], qkv_full[place][split][0], NT)
         for place in range(ranks)
@@ -708,8 +717,8 @@
         cq_sum,
         jnp.stack((key_sum, val_sum), axis=1),
         co_sum.T,
-        sum_lat(up_sums),
-        sum_lat(down_sums).T,
+        up_sum,
+        down_sum.T,
     )
 
 

time: 2740 us -> 1220 us (0.45)
  Pallas kernels: 1690 us -> 165 us
  waiting for transfers between devices: 581 us -> 641 us
    pallas_call x8, Pallas kernels: 1570 us -> 44.6 us  [assemble(): pl.pallas_call(partial(assemble_kernel, plan, len(sources)), in_specs=[an...]
    ppermute x144, waiting for transfers between devices: 581 us -> 641 us  [send_xor(): lax.ppermute(piece, axes, [(rank, rank ^ step) for rank in range(size)])]
  transfers between devices with their start and end apart: 144 -> 144, of which waited for: 52 -> 56; matrix products, arithmetic and copies ran while one was open for 8% -> 13% of each run, Pallas kernels for 41% -> 10%
where the time goes in v1:
time: 1220 us; the launch traced here: 1210 us
  waiting for transfers between devices  641 us (53%)
  matrix products  176 us (14%)
  Pallas kernels  165 us (14%)
  starting transfers between devices  162 us (13%)
  other arithmetic  32.6 us (3%)
  local copies, waits for them, and re-layouts  31.6 us (3%)
    ppermute x144, waiting for transfers between devices, send_xor(): lax.ppermute(piece, axes, [(rank, rank ^ step) for rank in range(size)])  641 us
    dot_general x78, matrix products, dot(): return lax.dot_general(left, right, dims, preferred_element_type=f32)  174 us
    ppermute x144, starting transfers between devices, send_xor(): lax.ppermute(piece, axes, [(rank, rank ^ step) for rank in range(size)])  162 us
    pallas_call x1, Pallas kernels, attend_back(): pl.pallas_call(partial(attend_back_kernel, heads, min(512, total), len(pi...  57.8 us
    pallas_call x8, Pallas kernels, assemble(): pl.pallas_call(partial(assemble_kernel, plan, len(sources)), in_specs=[an...  44.6 us
    pallas_call x1, Pallas kernels, attend(): pl.pallas_call(partial(attend_kernel, heads, len(pieces), own), grid=(row...  32.4 us
  transfers between devices with their start and end apart: 144, of which 56 were waited for; matrix products, arithmetic and copies ran while one was open for 13% of the time, Pallas kernels for 10%

profile of v1, /device:TPU:0, one launch (start us, length us, event | category | flops | bytes accessed | tf_op | source)
XLA Modules:
  0.0 1211.9 jit_solution(1930117540369525210)
XLA Ops:
  45.4 11.5 collective-permute-done.30
  71.4 16.4 %collective-permute-done.14 = bf16[72,3200]{1,0:T(8,128)(2,1)S(1)} collective-permute-done((bf16[72,3200]{1,0:T(8,128)(2,1)S(1)}, bf16[72,3200]{1,0:T(8,128)(2,1)S(1)}, u32[]{:S(2)}, u32[]{:S(2)}) %collective-permute-start.14) | collective-permute-done | bytes 460832 | tf_op jit(solution)/shard_map/ppermute | solution.py:49
  89.6 20.6 %collective-permute-done.15 = bf16[72,3200]{1,0:T(8,128)(2,1)S(1)} collective-permute-done((bf16[72,3200]{1,0:T(8,128)(2,1)S(1)}, bf16[72,3200]{1,0:T(8,128)(2,1)S(1)}, u32[]{:S(2)}, u32[]{:S(2)}) %collective-permute-start.15) | collective-permute-done | bytes 460832 | tf_op jit(solution)/shard_map/ppermute | solution.py:49
  142.4 31.7 %collective-permute-done.17.refs_1_ = bf16[288,3200]{1,0:T(8,128)(2,1)S(1)} collective-permute-done((bf16[288,3200]{1,0:T(8,128)(2,1)S(1)}, bf16[288,3200]{1,0:T(8,128)(2,1)S(1)}, u32[]{:S(2)}, u32[]{:S(2)}) %collective-permute-start.17) | collective-permute-done | bytes 1843232 | tf_op jit(solution)/shard_map/ppermute | solution.py:49
  183.5 13.2 %collective-permute-done.18 = bf16[72,2304]{1,0:T(8,128)(2,1)S(1)} collective-permute-done((bf16[72,2304]{1,0:T(8,128)(2,1)}, bf16[72,2304]{1,0:T(8,128)(2,1)S(1)}, u32[]{:S(2)}, u32[]{:S(2)}) %collective-permute-start.18) | collective-permute-done | bytes 331808 | tf_op jit(solution)/shard_map/ppermute | solution.py:49
  197.7 16.4 %collective-permute-done.19 = bf16[72,2304]{1,0:T(8,128)(2,1)S(1)} collective-permute-done((bf16[72,2304]{1,0:T(8,128)(2,1)}, bf16[72,2304]{1,0:T(8,128)(2,1)S(1)}, u32[]{:S(2)}, u32[]{:S(2)}) %collective-permute-start.19) | collective-permute-done | bytes 331808 | tf_op jit(solution)/shard_map/ppermute | solution.py:49
  214.1 9.9 collective-permute-done.22
  224.6 16.3 %collective-permute-done.23 = bf16[72,2304]{1,0:T(8,128)(2,1)S(1)} collective-permute-done((bf16[72,2304]{1,0:T(8,128)(2,1)S(1)}, bf16[72,2304]{1,0:T(8,128)(2,1)S(1)}, u32[]{:S(2)}, u32[]{:S(2)}) %collective-permute-start.23) | collective-permute-done | bytes 331808 | tf_op jit(solution)/shard_map/ppermute | solution.py:49
  242.7 9.8 collective-permute-done.24
  255.5 32.4 %shard_map.216 = (bf16[512,288]{1,0:T(8,128)(2,1)}, bf16[512,288]{1,0:T(8,128)(2,1)}, bf16[512,288]{1,0:T(8,128)(2,1)}, bf16[512,288]{1,0:T(8,128)(2,1)}, f32[4,2048,72]{2,1,0:T(8,128)}, /*index=5*/f32[8,2048]{1,0:T(8,128)}) custom-call(bf16[512,896]{1,0:T(8,128)(2,1)} %get-tuple-element.256.refs_0_, bf16[512,896]{1,0:T(8,128)(2,1)} %collective-permute-done.35.refs_1_, ...), custom_call_target="tpu_custom_call" | custom-call | flops 17179869184 | bytes 7340032 | tf_op jit(solution)/shard_map/pallas_call | solution.py:159
  290.0 30.1 %collective-permute-done.38 = bf16[512,288]{1,0:T(8,128)(2,1)S(1)} collective-permute-done((bf16[512,288]{1,0:T(8,128)(2,1)}, bf16[512,288]{1,0:T(8,128)(2,1)S(1)}, u32[]{:S(2)}, u32[]{:S(2)}) %collective-permute-start.38) | collective-permute-done | bytes 294944 | tf_op jit(solution)/shard_map/ppermute | solution.py:49
  326.0 44.5 %collective-permute-done.42 = bf16[512,288]{1,0:T(8,128)(2,1)S(1)} collective-permute-done((bf16[512,288]{1,0:T(8,128)(2,1)}, bf16[512,288]{1,0:T(8,128)(2,1)S(1)}, u32[]{:S(2)}, u32[]{:S(2)}) %collective-permute-start.42) | collective-permute-done | bytes 294944 | tf_op jit(solution)/shard_map/ppermute | solution.py:49
  374.5 62.2 %collective-permute-done.43 = bf16[512,288]{1,0:T(8,128)(2,1)S(1)} collective-permute-done((bf16[512,288]{1,0:T(8,128)(2,1)}, bf16[512,288]{1,0:T(8,128)(2,1)S(1)}, u32[]{:S(2)}, u32[]{:S(2)}) %collective-permute-start.43) | collective-permute-done | bytes 294944 | tf_op jit(solution)/shard_map/ppermute | solution.py:49
  449.7 14.0 %collective-permute-done.27 = bf16[128,1152]{1,0:T(8,128)(2,1)S(1)} collective-permute-done((bf16[128,1152]{1,0:T(8,128)(2,1)S(1)}, bf16[128,1152]{1,0:T(8,128)(2,1)S(1)}, u32[]{:S(2)}, u32[]{:S(2)}) %collective-permute-start.27) | collective-permute-done | bytes 294944 | tf_op jit(solution)/shard_map/ppermute | solution.py:49
  511.7 10.7 shard_map.217
  537.0 11.6 shard_map.218
  627.6 16.2 %collective-permute-done.71 = bf16[128,1152]{1,0:T(8,128)(2,1)S(1)} collective-permute-done((bf16[128,1152]{1,0:T(8,128)(2,1)S(1)}, bf16[128,1152]{1,0:T(8,128)(2,1)S(1)}, u32[]{:S(2)}, u32[]{:S(2)}) %collective-permute-start.71) | collective-permute-done | bytes 294944 | tf_op jit(solution)/shard_map/ppermute | solution.py:49
  663.8 18.7 %shard_map.221 = (bf16[512,640]{1,0:T(8,128)(2,1)}, bf16[512,640]{1,0:T(8,128)(2,1)}, bf16[120,640]{1,0:T(8,128)(2,1)}, bf16[120,640]{1,0:T(8,128)(2,1)}, bf16[1...) custom-call(bf16[512,640]{1,0:T(8,128)(2,1)} %convolution_convert_fusion.25.refs_0_, ...), custom_call_target="tpu_custom_call" | custom-call | tf_op jit(solution)/shard_map/pallas_call | solution.py:373
  727.1 12.4 %collective-permute-done.106 = bf16[120,1152]{1,0:T(8,128)(2,1)S(1)} collective-permute-done((bf16[120,1152]{1,0:T(8,128)(2,1)S(1)}, bf16[120,1152]{1,0:T(8,128)(2,1)S(1)}, u32[]{:S(2)}, u32[]{:S(2)}) %collective-permute-start.106) | collective-permute-done | bytes 276512 | tf_op jit(solution)/shard_map/ppermute | solution.py:49
  756.9 21.0 %collective-permute-done.59 = bf16[288,2304]{1,0:T(8,128)(2,1)S(1)} collective-permute-done((bf16[288,2304]{1,0:T(8,128)(2,1)S(1)}, bf16[288,2304]{1,0:T(8,128)(2,1)S(1)}, u32[]{:S(2)}, u32[]{:S(2)}) %collective-permute-start.59) | collective-permute-done | bytes 1327136 | tf_op jit(solution)/shard_map/ppermute | solution.py:49
  779.6 26.8 %collective-permute-done.58 = bf16[288,2304]{1,0:T(8,128)(2,1)S(1)} collective-permute-done((bf16[288,2304]{1,0:T(8,128)(2,1)S(1)}, bf16[288,2304]{1,0:T(8,128)(2,1)S(1)}, u32[]{:S(2)}, u32[]{:S(2)}) %collective-permute-start.58) | collective-permute-done | bytes 1327136 | tf_op jit(solution)/shard_map/ppermute | solution.py:49
  826.6 57.8 %shard_map.222 = (bf16[512,896]{1,0:T(8,128)(2,1)}, bf16[512,896]{1,0:T(8,128)(2,1)}, bf16[512,896]{1,0:T(8,128)(2,1)}, bf16[512,896]{1,0:T(8,128)(2,1)}) custom-call(bf16[512,896]{1,0:T(8,128)(2,1)} %get-tuple-element.256.refs_0_, bf16[512,896]{1,0:T(8,128)(2,1)} %collective-permute-done.35.refs_1_, bf16[512,896]{1,0:T(8,128)(2,1)} %collective-permute-done.36.refs_2_, ...), custom_call_target="tpu_custom_call" | custom-call | flops 42949672960 | bytes 14680064 | tf_op jit(solution)/shard_map/pallas_call | solution.py:263
  905.1 14.9 %collective-permute-done.85 = bf16[576,640]{1,0:T(8,128)(2,1)S(1)} collective-permute-done((bf16[576,640]{1,0:T(8,128)(2,1)}, bf16[576,640]{1,0:T(8,128)(2,1)S(1)}, u32[]{:S(2)}, u32[]{:S(2)}) %collective-permute-start.85) | collective-permute-done | bytes 737312 | tf_op jit(solution)/shard_map/ppermute | solution.py:49
  920.8 19.0 %collective-permute-done.86 = bf16[512,896]{1,0:T(8,128)(2,1)S(1)} collective-permute-done((bf16[512,896]{1,0:T(8,128)(2,1)S(1)}, bf16[512,896]{1,0:T(8,128)(2,1)S(1)}, u32[]{:S(2)}, u32[]{:S(2)}) %collective-permute-start.86) | collective-permute-done | bytes 917536 | tf_op jit(solution)/shard_map/ppermute | solution.py:49
  939.8 19.6 %collective-permute-done.87 = bf16[512,896]{1,0:T(8,128)(2,1)S(1)} collective-permute-done((bf16[512,896]{1,0:T(8,128)(2,1)S(1)}, bf16[512,896]{1,0:T(8,128)(2,1)S(1)}, u32[]{:S(2)}, u32[]{:S(2)}) %collective-permute-start.87) | collective-permute-done | bytes 917536 | tf_op jit(solution)/shard_map/ppermute | solution.py:49
  959.9 25.6 %collective-permute-done.78 = bf16[288,2304]{1,0:T(8,128)(2,1)S(1)} collective-permute-done((bf16[288,2304]{1,0:T(8,128)(2,1)S(1)}, bf16[288,2304]{1,0:T(8,128)(2,1)S(1)}, u32[]{:S(2)}, u32[]{:S(2)}) %collective-permute-start.78) | collective-permute-done | bytes 1327136 | tf_op jit(solution)/shard_map/ppermute | solution.py:49
  994.3 9.7 collective-permute-done.93
  1009.1 22.6 %collective-permute-done.94 = bf16[72,2304]{1,0:T(8,128)(2,1)S(1)} collective-permute-done((bf16[72,2304]{1,0:T(8,128)(2,1)S(1)}, bf16[72,2304]{1,0:T(8,128)(2,1)S(1)}, u32[]{:S(2)}, u32[]{:S(2)}) %collective-permute-start.94) | collective-permute-done | bytes 331808 | tf_op jit(solution)/shard_map/ppermute | solution.py:49
  1035.2 10.6 collective-permute-done.97
  1128.7 15.1 %collective-permute-done.100 = bf16[128,1152]{1,0:T(8,128)(2,1)S(1)} collective-permute-done((bf16[128,1152]{1,0:T(8,128)(2,1)S(1)}, bf16[128,1152]{1,0:T(8,128)(2,1)S(1)}, u32[]{:S(2)}, u32[]{:S(2)}) %collective-permute-start.100) | collective-permute-done | bytes 294944 | tf_op jit(solution)/shard_map/ppermute | solution.py:49
  1162.2 10.9 collective-permute-done.116
  1173.9 9.6 collective-permute-done.125
  (790 shorter events, 546.6 us)
Async XLA Ops:
  39.3 50.2 %collective-permute-start.4 = (bf16[288,896]{1,0:T(8,128)(2,1)S(1)}, bf16[288,896]{1,0:T(8,128)(2,1)}, u32[]{:S(2)}, u32[]{:S(2)}) collective-permute-start(bf16[288,896]{1,0:T(8,128)(2,1)S(1)} %get-tuple-element.325.refs_0_), channel_id=1, source_target_pairs={{0,16},{16,0},{1,17},{17,1},{2,18},{18,2},{3,19},{19,3},{4,20},{20... | collective-permute-start | bytes 1548296 | tf_op jit(solution)/shard_map/ppermute | solution.py:49
  111.4 62.7 %collective-permute-start.17 = (bf16[288,3200]{1,0:T(8,128)(2,1)S(1)}, bf16[288,3200]{1,0:T(8,128)(2,1)S(1)}, u32[]{:S(2)}, u32[]{:S(2)}) collective-permute-start(bf16[288,3200]{1,0:T(8,128)(2,1)S(1)} %constant_dynamic-update-slice_fusion.refs_0_), channel_id=1, source_target_pairs={{0,2},{2,0},{1,3},{3,1},{4,6},{6,4},{5,7},{7,5},{8,10},{10,8},{9,1... | collective-permute-start | bytes 5529608 | tf_op jit(solution)/shard_map/ppermute | solution.py:49
  134.5 120.4 %collective-permute-start.37 = (bf16[512,896]{1,0:T(8,128)(2,1)}, bf16[512,896]{1,0:T(8,128)(2,1)}, u32[]{:S(2)}, u32[]{:S(2)}) collective-permute-start(bf16[512,896]{1,0:T(8,128)(2,1)} %get-tuple-element.253), channel_id=1, source_target_pairs={{0,3},{1,2},{2,1},{3,0},{4,7},{5,6},{6,5},{7,4},{8,11},{9,10},{10,... | collective-permute-start | bytes 2752520 | tf_op jit(solution)/shard_map/ppermute | solution.py:49
  137.4 118.1 %collective-permute-start.35 = (bf16[512,896]{1,0:T(8,128)(2,1)}, bf16[512,896]{1,0:T(8,128)(2,1)}, u32[]{:S(2)}, u32[]{:S(2)}) collective-permute-start(bf16[512,896]{1,0:T(8,128)(2,1)} %get-tuple-element.254), channel_id=1, source_target_pairs={{0,1},{1,0},{2,3},{3,2},{4,5},{5,4},{6,7},{7,6},{8,9},{9,8},{10,11... | collective-permute-start | bytes 2752520 | tf_op jit(solution)/shard_map/ppermute | solution.py:49
  142.3 113.2 %collective-permute-start.36 = (bf16[512,896]{1,0:T(8,128)(2,1)}, bf16[512,896]{1,0:T(8,128)(2,1)}, u32[]{:S(2)}, u32[]{:S(2)}) collective-permute-start(bf16[512,896]{1,0:T(8,128)(2,1)} %get-tuple-element.255), channel_id=1, source_target_pairs={{0,2},{1,3},{2,0},{3,1},{4,6},{5,7},{6,4},{7,5},{8,10},{9,11},{10,... | collective-permute-start | bytes 2752520 | tf_op jit(solution)/shard_map/ppermute | solution.py:49
  179.2 74.0 %collective-permute-start.20 = (bf16[72,2304]{1,0:T(8,128)(2,1)}, bf16[72,2304]{1,0:T(8,128)(2,1)S(1)}, u32[]{:S(2)}, u32[]{:S(2)}) collective-permute-start(bf16[72,2304]{1,0:T(8,128)(2,1)} %param.21), channel_id=1, source_target_pairs={{0,12},{4,8},{8,4},{12,0},{1,13},{5,9},{9,5},{13,1},{2,14},{6,10},... | collective-permute-start | bytes 995336 | tf_op jit(solution)/shard_map/ppermute | solution.py:49
  252.5 219.5 %collective-permute-start.40 = (bf16[576,3200]{1,0:T(8,128)(2,1)}, bf16[576,3200]{1,0:T(8,128)(2,1)}, u32[]{:S(2)}, u32[]{:S(2)}) collective-permute-start(bf16[576,3200]{1,0:T(8,128)(2,1)} %shard_map.213.refs_0_), channel_id=1, source_target_pairs={{0,1},{1,0},{2,3},{3,2},{4,5},{5,4},{6,7},{7,6},{8,9},{9,8},{10,11... | collective-permute-start | bytes 11059208 | tf_op jit(solution)/shard_map/ppermute | solution.py:49
  253.3 118.7 %collective-permute-start.25 = (bf16[288,2304]{1,0:T(8,128)(2,1)S(1)}, bf16[288,2304]{1,0:T(8,128)(2,1)}, u32[]{:S(2)}, u32[]{:S(2)}) collective-permute-start(bf16[288,2304]{1,0:T(8,128)(2,1)S(1)} %constant_dynamic-update-slice_fusion.8.refs_0_), channel_id=1, source_target_pairs={{0,2},{2,0},{1,3},{3,1},{4,6},{6,4},{5,7},{7,5},{8,10},{10,8},{9,1... | collective-permute-start | bytes 3981320 | tf_op jit(solution)/shard_map/ppermute | solution.py:49
  254.9 66.6 %collective-permute-start.21 = (bf16[288,2304]{1,0:T(8,128)(2,1)S(1)}, bf16[288,2304]{1,0:T(8,128)(2,1)S(1)}, u32[]{:S(2)}, u32[]{:S(2)}) collective-permute-start(bf16[288,2304]{1,0:T(8,128)(2,1)S(1)} %constant_dynamic-update-slice_fusion.4.refs_0_), channel_id=1, source_target_pairs={{0,2},{2,0},{1,3},{3,1},{4,6},{6,4},{5,7},{7,5},{8,10},{10,8},{9,1... | collective-permute-start | bytes 3981320 | tf_op jit(solution)/shard_map/ppermute | solution.py:49
  289.5 149.7 %collective-permute-start.46 = (bf16[288,2304]{1,0:T(8,128)(2,1)S(1)}, bf16[288,2304]{1,0:T(8,128)(2,1)}, u32[]{:S(2)}, u32[]{:S(2)}) collective-permute-start(bf16[288,2304]{1,0:T(8,128)(2,1)S(1)} %constant_dynamic-update-slice_fusion.8.refs_0_), channel_id=1, source_target_pairs={{0,1},{1,0},{2,3},{3,2},{4,5},{5,4},{6,7},{7,6},{8,9},{9,8},{10,11... | collective-permute-start | bytes 3981320 | tf_op jit(solution)/shard_map/ppermute | solution.py:49
  320.1 50.4 %collective-permute-start.42 = (bf16[512,288]{1,0:T(8,128)(2,1)}, bf16[512,288]{1,0:T(8,128)(2,1)S(1)}, u32[]{:S(2)}, u32[]{:S(2)}) collective-permute-start(bf16[512,288]{1,0:T(8,128)(2,1)} %get-tuple-element.104), channel_id=1, source_target_pairs={{0,3},{1,2},{2,1},{3,0},{4,7},{5,6},{6,5},{7,4},{8,11},{9,10},{10,... | collective-permute-start | bytes 884744 | tf_op jit(solution)/shard_map/ppermute | solution.py:49
  321.6 121.5 %collective-permute-start.44 = (bf16[288,2304]{1,0:T(8,128)(2,1)S(1)}, bf16[288,2304]{1,0:T(8,128)(2,1)S(1)}, u32[]{:S(2)}, u32[]{:S(2)}) collective-permute-start(bf16[288,2304]{1,0:T(8,128)(2,1)S(1)} %constant_dynamic-update-slice_fusion.8.refs_0_), channel_id=1, source_target_pairs={{0,16},{16,0},{1,17},{17,1},{2,18},{18,2},{3,19},{19,3},{4,20},{20... | collective-permute-start | bytes 3981320 | tf_op jit(solution)/shard_map/ppermute | solution.py:49
  370.5 105.6 %collective-permute-start.51 = (bf16[576,2304]{1,0:T(8,128)(2,1)}, bf16[576,2304]{1,0:T(8,128)(2,1)}, u32[]{:S(2)}, u32[]{:S(2)}) collective-permute-start(bf16[576,2304]{1,0:T(8,128)(2,1)} %shard_map.214.refs_0_), channel_id=1, source_target_pairs={{0,1},{1,0},{2,3},{3,2},{4,5},{5,4},{6,7},{7,6},{8,9},{9,8},{10,11... | collective-permute-start | bytes 7962632 | tf_op jit(solution)/shard_map/ppermute | solution.py:49
  372.0 64.8 %collective-permute-start.43 = (bf16[512,288]{1,0:T(8,128)(2,1)}, bf16[512,288]{1,0:T(8,128)(2,1)S(1)}, u32[]{:S(2)}, u32[]{:S(2)}) collective-permute-start(bf16[512,288]{1,0:T(8,128)(2,1)} %get-tuple-element.105), channel_id=1, source_target_pairs={{0,1},{1,0},{2,3},{3,2},{4,5},{5,4},{6,7},{7,6},{8,9},{9,8},{10,11... | collective-permute-start | bytes 884744 | tf_op jit(solution)/shard_map/ppermute | solution.py:49
  579.1 74.0 %collective-permute-start.54 = (bf16[576,2304]{1,0:T(8,128)(2,1)}, bf16[576,2304]{1,0:T(8,128)(2,1)S(1)}, u32[]{:S(2)}, u32[]{:S(2)}) collective-permute-start(bf16[576,2304]{1,0:T(8,128)(2,1)} %convolution_convert_fusion.2), channel_id=1, source_target_pairs={{0,16},{16,0},{1,17},{17,1},{2,18},{18,2},{3,19},{19,3},{4,20},{20... | collective-permute-start | bytes 7962632 | tf_op jit(solution)/shard_map/ppermute | solution.py:49
  579.2 69.6 %collective-permute-start.56 = (bf16[576,2304]{1,0:T(8,128)(2,1)S(1)}, bf16[576,2304]{1,0:T(8,128)(2,1)}, u32[]{:S(2)}, u32[]{:S(2)}) collective-permute-start(bf16[576,2304]{1,0:T(8,128)(2,1)S(1)} %convolution_convert_fusion), channel_id=1, source_target_pairs={{0,16},{16,0},{1,17},{17,1},{2,18},{18,2},{3,19},{19,3},{4,20},{20... | collective-permute-start | bytes 7962632 | tf_op jit(solution)/shard_map/ppermute | solution.py:49
  747.7 60.5 %collective-permute-start.57 = (bf16[576,2304]{1,0:T(8,128)(2,1)S(1)}, bf16[576,2304]{1,0:T(8,128)(2,1)S(1)}, u32[]{:S(2)}, u32[]{:S(2)}) collective-permute-start(bf16[576,2304]{1,0:T(8,128)(2,1)S(1)} %copy-done.103), channel_id=1, source_target_pairs={{0,1},{1,0},{2,3},{3,2},{4,5},{5,4},{6,7},{7,6},{8,9},{9,8},{10,11... | collective-permute-start | bytes 7962632 | tf_op jit(solution)/shard_map/ppermute | solution.py:49
  749.9 67.0 %collective-permute-start.75 = (bf16[512,288]{1,0:T(8,128)(2,1)S(1)}, bf16[512,288]{1,0:T(8,128)(2,1)S(1)}, u32[]{:S(2)}, u32[]{:S(2)}) collective-permute-start(bf16[512,288]{1,0:T(8,128)(2,1)S(1)} %get-tuple-element.285), channel_id=1, source_target_pairs={{0,3},{1,2},{2,1},{3,0},{4,7},{5,6},{6,5},{7,4},{8,11},{9,10},{10,... | collective-permute-start | bytes 884744 | tf_op jit(solution)/shard_map/ppermute | solution.py:49
  752.8 53.6 %collective-permute-start.58 = (bf16[288,2304]{1,0:T(8,128)(2,1)S(1)}, bf16[288,2304]{1,0:T(8,128)(2,1)S(1)}, u32[]{:S(2)}, u32[]{:S(2)}) collective-permute-start(bf16[288,2304]{1,0:T(8,128)(2,1)S(1)} %slice.355), channel_id=1, source_target_pairs={{0,2},{2,0},{1,3},{3,1},{4,6},{6,4},{5,7},{7,5},{8,10},{10,8},{9,1... | collective-permute-start | bytes 3981320 | tf_op jit(solution)/shard_map/ppermute | solution.py:49
  754.5 69.8 %collective-permute-start.73 = (bf16[512,288]{1,0:T(8,128)(2,1)S(1)}, bf16[512,288]{1,0:T(8,128)(2,1)S(1)}, u32[]{:S(2)}, u32[]{:S(2)}) collective-permute-start(bf16[512,288]{1,0:T(8,128)(2,1)S(1)} %get-tuple-element.286), channel_id=1, source_target_pairs={{0,1},{1,0},{2,3},{3,2},{4,5},{5,4},{6,7},{7,6},{8,9},{9,8},{10,11... | collective-permute-start | bytes 884744 | tf_op jit(solution)/shard_map/ppermute | solution.py:49
  812.0 72.5 %collective-permute-start.84 = (bf16[288,640]{1,0:T(8,128)(2,1)}, bf16[288,640]{1,0:T(8,128)(2,1)}, u32[]{:S(2)}, u32[]{:S(2)}) collective-permute-start(bf16[288,640]{1,0:T(8,128)(2,1)} %slice.377), channel_id=1, source_target_pairs={{0,2},{2,0},{1,3},{3,1},{4,6},{6,4},{5,7},{7,5},{8,10},{10,8},{9,1... | collective-permute-start | bytes 1105928 | tf_op jit(solution)/shard_map/ppermute | solution.py:49
  812.7 73.8 %collective-permute-start.83 = (bf16[288,640]{1,0:T(8,128)(2,1)}, bf16[288,640]{1,0:T(8,128)(2,1)S(1)}, u32[]{:S(2)}, u32[]{:S(2)}) collective-permute-start(bf16[288,640]{1,0:T(8,128)(2,1)} %slice.375), channel_id=1, source_target_pairs={{0,2},{2,0},{1,3},{3,1},{4,6},{6,4},{5,7},{7,5},{8,10},{10,8},{9,1... | collective-permute-start | bytes 1105928 | tf_op jit(solution)/shard_map/ppermute | solution.py:49
  816.9 72.7 %collective-permute-start.81 = (bf16[288,640]{1,0:T(8,128)(2,1)}, bf16[288,640]{1,0:T(8,128)(2,1)}, u32[]{:S(2)}, u32[]{:S(2)}) collective-permute-start(bf16[288,640]{1,0:T(8,128)(2,1)} %slice.373), channel_id=1, source_target_pairs={{0,2},{2,0},{1,3},{3,1},{4,6},{6,4},{5,7},{7,5},{8,10},{10,8},{9,1... | collective-permute-start | bytes 1105928 | tf_op jit(solution)/shard_map/ppermute | solution.py:49
  824.2 67.7 %collective-permute-start.80 = (bf16[288,640]{1,0:T(8,128)(2,1)}, bf16[288,640]{1,0:T(8,128)(2,1)}, u32[]{:S(2)}, u32[]{:S(2)}) collective-permute-start(bf16[288,640]{1,0:T(8,128)(2,1)} %slice.371), channel_id=1, source_target_pairs={{0,2},{2,0},{1,3},{3,1},{4,6},{6,4},{5,7},{7,5},{8,10},{10,8},{9,1... | collective-permute-start | bytes 1105928 | tf_op jit(solution)/shard_map/ppermute | solution.py:49
  825.0 67.9 %collective-permute-start.79 = (bf16[576,640]{1,0:T(8,128)(2,1)}, bf16[576,640]{1,0:T(8,128)(2,1)}, u32[]{:S(2)}, u32[]{:S(2)}) collective-permute-start(bf16[576,640]{1,0:T(8,128)(2,1)} %add_convert_fusion.31), channel_id=1, source_target_pairs={{0,1},{1,0},{2,3},{3,2},{4,5},{5,4},{6,7},{7,6},{8,9},{9,8},{10,11... | collective-permute-start | bytes 2211848 | tf_op jit(solution)/shard_map/ppermute | solution.py:49
  889.6 50.2 %collective-permute-start.86 = (bf16[512,896]{1,0:T(8,128)(2,1)S(1)}, bf16[512,896]{1,0:T(8,128)(2,1)S(1)}, u32[]{:S(2)}, u32[]{:S(2)}) collective-permute-start(bf16[512,896]{1,0:T(8,128)(2,1)S(1)} %copy-done.113), channel_id=1, source_target_pairs={{0,3},{1,2},{2,1},{3,0},{4,7},{5,6},{6,5},{7,4},{8,11},{9,10},{10,... | collective-permute-start | bytes 2752520 | tf_op jit(solution)/shard_map/ppermute | solution.py:49
  892.0 67.4 %collective-permute-start.87 = (bf16[512,896]{1,0:T(8,128)(2,1)S(1)}, bf16[512,896]{1,0:T(8,128)(2,1)S(1)}, u32[]{:S(2)}, u32[]{:S(2)}) collective-permute-start(bf16[512,896]{1,0:T(8,128)(2,1)S(1)} %copy-done.112), channel_id=1, source_target_pairs={{0,1},{1,0},{2,3},{3,2},{4,5},{5,4},{6,7},{7,6},{8,9},{9,8},{10,11... | collective-permute-start | bytes 2752520 | tf_op jit(solution)/shard_map/ppermute | solution.py:49
  892.9 66.6 %collective-permute-start.77 = (bf16[288,2304]{1,0:T(8,128)(2,1)S(1)}, bf16[288,2304]{1,0:T(8,128)(2,1)S(1)}, u32[]{:S(2)}, u32[]{:S(2)}) collective-permute-start(bf16[288,2304]{1,0:T(8,128)(2,1)S(1)} %slice.369), channel_id=1, source_target_pairs={{0,2},{2,0},{1,3},{3,1},{4,6},{6,4},{5,7},{7,5},{8,10},{10,8},{9,1... | collective-permute-start | bytes 3981320 | tf_op jit(solution)/shard_map/ppermute | solution.py:49
  904.2 89.6 %collective-permute-start.76 = (bf16[512,896]{1,0:T(8,128)(2,1)S(1)}, bf16[512,896]{1,0:T(8,128)(2,1)S(1)}, u32[]{:S(2)}, u32[]{:S(2)}) collective-permute-start(bf16[512,896]{1,0:T(8,128)(2,1)S(1)} %copy-done.111), channel_id=1, source_target_pairs={{0,2},{1,3},{2,0},{3,1},{4,6},{5,7},{6,4},{7,5},{8,10},{9,11},{10,... | collective-permute-start | bytes 2752520 | tf_op jit(solution)/shard_map/ppermute | solution.py:49
  920.0 65.5 %collective-permute-start.78 = (bf16[288,2304]{1,0:T(8,128)(2,1)S(1)}, bf16[288,2304]{1,0:T(8,128)(2,1)S(1)}, u32[]{:S(2)}, u32[]{:S(2)}) collective-permute-start(bf16[288,2304]{1,0:T(8,128)(2,1)S(1)} %add_convert_fusion.7), channel_id=1, source_target_pairs={{0,1},{1,0},{2,3},{3,2},{4,5},{5,4},{6,7},{7,6},{8,9},{9,8},{10,11... | collective-permute-start | bytes 3981320 | tf_op jit(solution)/shard_map/ppermute | solution.py:49
  992.0 56.2 %collective-permute-start.92 = (bf16[288,640]{1,0:T(8,128)(2,1)S(1)}, bf16[288,640]{1,0:T(8,128)(2,1)S(1)}, u32[]{:S(2)}, u32[]{:S(2)}) collective-permute-start(bf16[288,640]{1,0:T(8,128)(2,1)S(1)} %slice.383), channel_id=1, source_target_pairs={{0,2},{2,0},{1,3},{3,1},{4,6},{6,4},{5,7},{7,5},{8,10},{10,8},{9,1... | collective-permute-start | bytes 1105928 | tf_op jit(solution)/shard_map/ppermute | solution.py:49
  993.8 55.3 %collective-permute-start.90 = (bf16[288,640]{1,0:T(8,128)(2,1)S(1)}, bf16[288,640]{1,0:T(8,128)(2,1)S(1)}, u32[]{:S(2)}, u32[]{:S(2)}) collective-permute-start(bf16[288,640]{1,0:T(8,128)(2,1)S(1)} %slice.381), channel_id=1, source_target_pairs={{0,2},{2,0},{1,3},{3,1},{4,6},{6,4},{5,7},{7,5},{8,10},{10,8},{9,1... | collective-permute-start | bytes 1105928 | tf_op jit(solution)/shard_map/ppermute | solution.py:49
  (262 other events, 5333.4 us)

commit v2 on v0

--- a/solution.py
+++ b/solution.py
@@ -24,6 +24,7 @@
 TN = (((0,), (0,)), ((), ()))
 
 ROW = ("sr", "hr")
+EVERY = ("tensor", "fsdp", "lat", "sr", "hr")
 PLANE = ("sr", "hr", "tensor")
 HEAD_GROUP = ("hr", "tensor")
 
@@ -384,63 +385,85 @@
 
 
 def assemble_kernel(plan, count, *refs):
-    sources, (sems,) = refs[:count], refs[-1:]
-    outs = refs[count:-1]
-    copies = [
-        pltpu.make_async_copy(
-            sources[source].at[:, pl.ds(column, size)],
-            outs[place].at[pl.ds(row, sources[source].shape[0]), :],
-            sems.at[number],
+    sources, outs, sems = refs[:count], refs[count:-1], refs[-1]
+    copies = []
+    for number, (source, start, rows, column, size, place, row, shift) in enumerate(plan):
+        copies.append(
+            pltpu.make_async_copy(
+                sources[source].at[pl.ds(start, rows), pl.ds(column, size)],
+                outs[place].at[pl.ds(row, rows), pl.ds(shift, size)],
+                sems.at[number],
+            )
         )
-        for number, (source, column, size, place, row) in enumerate(plan)
-    ]
     for copy in copies:
         copy.start()
     for copy in copies:
         copy.wait()
 
 
-def assemble(stacks, columns):
+def lay(sources, plan, shapes):
+    anywhere = pl.BlockSpec(memory_space=pl.ANY)
+    return list(
+        pl.pallas_call(
+            partial(assemble_kernel, plan, len(sources)),
+            in_specs=[anywhere] * len(sources),
+            out_specs=[pl.BlockSpec(memory_space=pltpu.VMEM)] * len(shapes),
+            out_shape=[jax.ShapeDtypeStruct(shape, bf16) for shape in shapes],
+            scratch_shapes=[pltpu.SemaphoreType.DMA((len(plan),))],
+            compiler_params=pltpu.CompilerParams(vmem_limit_bytes=VMEM_LIMIT),
+        )(*sources)
+    )
+
+
+def assemble(stacks):
     sources = [piece for stack in stacks for piece in stack]
-    plan, shapes, base = [], [], 0
+    plan, shapes = [], []
     for stack in stacks:
-        offset = 0
-        for size in columns:
-            row = 0
-            for number, piece in enumerate(stack):
-                plan.append((base + number, offset, size, len(shapes), row))
-                row += piece.shape[0]
-            shapes.append(jax.ShapeDtypeStruct((row, size), piece.dtype))
-            offset += size
-        base += len(stack)
-    anywhere = pl.BlockSpec(memory_space=pl.ANY)
-    out = pl.pallas_call(
-        partial(assemble_kernel, plan, len(sources)),
-        in_specs=[anywhere] * len(sources),
-        out_specs=[anywhere] * len(shapes),
-        out_shape=shapes,
-        scratch_shapes=[pltpu.SemaphoreType.DMA((len(plan),))],
-    )(*sources)
-    out = list(out)
-    return [out[place : place + len(columns)] for place in range(0, len(out), len(columns))]
+        row, width = 0, stack[0].shape[1]
+        for piece in stack:
+            plan.append((len(plan), 0, piece.shape[0], 0, width, len(shapes), row, 0))
+            row += piece.shape[0]
+        shapes.append((row, width))
+    return lay(sources, plan, shapes)
+
+
+def cut(source, rows, columns):
+    grid = [
+        (place, row) for place in range(source.shape[1] // columns) for row in range(source.shape[0] // rows)
+    ]
+    plan = [
+        (0, row * rows, rows, place * columns, columns, number, 0, 0)
+        for number, (place, row) in enumerate(grid)
+    ]
+    out = lay([source], plan, [(rows, columns)] * len(grid))
+    count = source.shape[0] // rows
+    return [out[place : place + count] for place in range(0, len(out), count)]
 
 
 def with_others(piece, axes):
     return [piece] + [send_xor(piece, axes, step) for step in range(1, lax.axis_size(axes))]
 
 
-def gather(shard, columns, tensor_first):
+def gather(shard, tensor_first):
     start = jnp.concatenate(with_others(shard, "lat"))
     if tensor_first and lax.axis_size("tensor") * lax.axis_size(ROW) <= 8:
         stacks = [with_others(piece, ROW) for piece in with_others(start, "tensor")]
     else:
-        half = assemble([with_others(start, ROW)], [start.shape[1]])[0][0]
+        half = assemble([with_others(start, ROW)])[0]
         stacks = [[piece] for piece in with_others(half, "tensor")]
-    stacks = [
-        stack + [send_xor(piece, "fsdp", step) for step in range(1, lax.axis_size("fsdp")) for piece in stack]
-        for stack in stacks
-    ]
-    return assemble(stacks, columns)
+    cores = range(1, lax.axis_size("fsdp"))
+    return assemble(
+        [stack + [send_xor(piece, "fsdp", step) for step in cores for piece in stack] for stack in stacks]
+    )
+
+
+def gather_all(shard):
+    return lax.all_gather(shard, EVERY, axis=shard.ndim - 2, tiled=True)
+
+
+def scatter_all(pieces):
+    pack = assemble([pieces])[0]
+    return lax.psum_scatter(pack, EVERY, scatter_dimension=0, tiled=True).astype(f32)
 
 
 def kept_sums(left, rights, extra=None):
@@ -519,42 +542,38 @@
         return jnp.pad(values, ((0, 0), (0, wide - part)))
 
     latents_got = exchange(partial(pick, latents), "lat")
+    mid_shard = jnp.concatenate(
+        [padded(piece) for piece in (w_out.T, w_ckv[:, 0], w_ckv[:, 1], w_cq, w_co.T)], axis=1
+    )
+    mid_full = gather_all(mid_shard)
+    two_full = gather_all(jnp.stack((w_up, w_down.T)))
     shard_qkv = jnp.transpose(w_qkv.reshape(share, 3, ranks, edge), (2, 0, 1, 3)).reshape(
         ranks, share, 3 * edge
     )
     fill = jnp.pad(table.T, ((0, 0), (0, piece_width - 3 * edge - 6)))
     qkv_full = [
-        gather(jnp.concatenate((shard_qkv[place], fill), axis=1), [piece_width], place % 2 == 0)
+        gather(jnp.concatenate((shard_qkv[place], fill), axis=1), place % 2 == 0)
         for place in range(ranks)
     ]
-    mid_shard = jnp.concatenate(
-        [padded(piece) for piece in (w_out.T, w_ckv[:, 0], w_ckv[:, 1], w_cq, w_co.T)], axis=1
-    )
-    mid_shard, qkv_full[0][0][0] = tie(mid_shard, qkv_full[0][0][0])
-    mid_full = gather(mid_shard, [wide] * 5, False)
-    out_full, key_full, val_full, cq_full, co_full = (
-        [full[place] for full in mid_full] for place in range(5)
-    )
-    up_shard, down_shard, out_full[0] = lax.optimization_barrier((w_up, w_down.T, out_full[0]))
-    up_full = [full[0] for full in gather(up_shard, [inner_part], False)]
-    down_full = [full[0] for full in gather(down_shard, [inner_part], True)]
 
     turn = own_order(share, width)
-    residual = dot(jnp.concatenate(latents_got, axis=0), turn)
-    grad_three = dot(jnp.concatenate(exchange(partial(pick, cotangent), "lat"), axis=0), turn)
+    residual = jnp.concatenate(latents_got, axis=0).astype(f32)
+    cotangent, _ = tie(cotangent, qkv_full[0][0])
+    grad_three = jnp.concatenate(exchange(partial(pick, cotangent), "lat"), axis=0).astype(f32)
     rows = residual.shape[0]
-    caption = dot(pick(text, slot), turn).astype(bf16)
-    table_full = qkv_full[0][0][0][:, 3 * edge : 3 * edge + 6]
-    modulate = table_full.T.astype(f32) + dot(pick(time_vector, slot).reshape(6, width), turn)
+    caption = pick(text, slot)
+    table_full = dot(qkv_full[0][0][:, 3 * edge : 3 * edge + 6].T, turn, NT)
+    modulate = table_full + pick(time_vector, slot).astype(f32).reshape(6, width)
     shift_one, scale_one, gate_one, shift_two, scale_two, gate_two = (
         modulate[row : row + 1] for row in range(6)
     )
 
     normed_one, inverse_one = norm_parts(residual)
     hidden_one = (normed_one * (1.0 + scale_one) + shift_one).astype(bf16)
+    hidden_one = dot(hidden_one, turn).astype(bf16)
     mixed = [None] * groups
     for split in range(splits):
-        pieces = [dot(hidden_one, full[split][0]).astype(bf16) for full in qkv_full]
+        pieces = [dot(hidden_one, full[split]).astype(bf16) for full in qkv_full]
         for other in range(ranks):
             step = other * splits + split
             piece = choose(pieces, jnp.bitwise_xor(rank, other))
@@ -568,9 +587,20 @@
         return [choose(own, jnp.bitwise_xor(rank, place)) for place in range(ranks)]
 
     att_back = give_back(att_low, HEAD_GROUP)
-    att = [
+    att_own = [
         padded(jnp.concatenate(by_split(att_back, split), axis=1)) for split in range(splits)
     ]
+    col = lax.axis_index("tensor")
+
+    def from_own(pieces):
+        return [choose(pieces, jnp.bitwise_xor(col, place)) for place in range(splits)]
+
+    att = from_own(att_own)
+    out_full, key_full, val_full, cq_full, co_full = cut(mid_full, width, wide)
+    up_full, down_full = (
+        [two_full[place, split * width : (split + 1) * width] for split in range(splits)]
+        for place in range(2)
+    )
 
     out_one = sum(dot(att[split], out_full[split], NT) for split in range(splits))
     after_one = residual + gate_one * out_one
@@ -586,7 +616,7 @@
     inner = [dot(hidden_two, up_full[split]) for split in range(splits)]
     active = [jax.nn.gelu(values, approximate=True).astype(bf16) for values in inner]
     out_three = sum(dot(active[split], down_full[split], NT) for split in range(splits))
-    result = dot((after_two + gate_two * out_three).astype(bf16), turn, NT).astype(bf16)
+    result = (after_two + gate_two * out_three).astype(bf16)
     result_back = in_order(give_back(list(result.reshape(latents.shape)), "lat"), "lat")
 
     grad_gate_two = jnp.sum(grad_three * out_three, axis=0)
@@ -596,8 +626,8 @@
         grad_active = dot(grad_z, down_full[split])
         _, pull = jax.vjp(partial(jax.nn.gelu, approximate=True), inner[split])
         grad_inner.append(pull(grad_active)[0].astype(bf16))
-    down_sums = kept_sums(grad_z, active)
-    up_sums = kept_sums(hidden_two, grad_inner)
+    down_sum = scatter_all([dot(grad_z, piece, TN).astype(bf16) for piece in active])
+    up_sum = scatter_all([dot(hidden_two, piece, TN).astype(bf16) for piece in grad_inner])
     grad_hidden_two = sum(dot(grad_inner[split], up_full[split], NT) for split in range(splits))
     grad_shift_two = jnp.sum(grad_hidden_two, axis=0)
     grad_scale_two = jnp.sum(grad_hidden_two * normed_two, axis=0)
@@ -605,10 +635,6 @@
 
     grad_out_two = grad_two.astype(bf16)
     grad_cross = [dot(grad_out_two, full).astype(bf16) for full in co_full]
-    (grad_cross[0], down_sums, up_sums) = lax.optimization_barrier(
-        (grad_cross[0], down_sums, up_sums)
-    )
-    down_sums, up_sums = sum_tensor(down_sums), sum_row(up_sums)
     grad_cq, grad_ck, grad_cv = cross_back(cross_q, cross_k, cross_v, grad_cross, part)
     grad_one = grad_two + sum(dot(grad_cq[split], cq_full[split], NT) for split in range(splits))
     text_terms = sum(
@@ -618,7 +644,7 @@
 
     grad_gate_one = jnp.sum(grad_one * out_one, axis=0)
     grad_out_one = (gate_one * grad_one).astype(bf16)
-    grad_att = [dot(grad_out_one, full).astype(bf16) for full in out_full]
+    grad_att = from_own([dot(grad_out_one, full).astype(bf16) for full in out_full])
     grad_heads = [None] * groups
     for split in range(splits):
         cuts = [grad_att[split][:, place * edge : (place + 1) * edge] for place in range(ranks)]
@@ -626,26 +652,24 @@
             step = other * splits + split
             piece = choose(cuts, jnp.bitwise_xor(rank, other))
             grad_heads[step] = send_xor(piece, HEAD_GROUP, step) if step else piece
+    caption_turn = dot(caption, turn).astype(bf16)
     mid_sums = [
         kept_sums(left, rights)
         for left, rights in (
-            (caption, grad_ck),
-            (caption, grad_cv),
-            (mid_low, grad_cq),
-            (grad_out_two, cross_low),
-            (grad_out_one, att),
+            (caption_turn, from_own(grad_ck)),
+            (caption_turn, from_own(grad_cv)),
+            (dot(mid_low, turn).astype(bf16), from_own(grad_cq)),
+            (dot(grad_out_two, turn).astype(bf16), from_own(cross_low)),
+            (dot(grad_out_one, turn).astype(bf16), att_own),
         )
     ]
-    (grad_heads[0], down_sums, up_sums, mid_sums) = lax.optimization_barrier(
-        (grad_heads[0], down_sums, up_sums, mid_sums)
-    )
-    down_sums, up_sums = sum_row(down_sums), sum_tensor(up_sums)
+    (grad_heads[0], mid_sums, result_back, down_sum) = lax.optimization_barrier(
+        (grad_heads[0], mid_sums, result_back, down_sum)
+    )
     orders = [(sum_tensor, sum_row), (sum_row, sum_tensor)]
     mid_sums = [orders[place % 2][0](sums) for place, sums in enumerate(mid_sums)]
     grad_mix = list(attend_back(mixed, groups, grad_heads, att_wide, logsum, heads))
-    (grad_mix[0], down_sums, up_sums, mid_sums) = lax.optimization_barrier(
-        (grad_mix[0], down_sums, up_sums, mid_sums)
-    )
+    (grad_mix[0], mid_sums) = tie(grad_mix[0], mid_sums)
     for step in range(1, halves):
         for place in range(groups):
             more = send_xor(grad_mix[step * groups + place], "sr", step)
@@ -653,17 +677,21 @@
     grad_proj = give_back(grad_mix[:groups], HEAD_GROUP)
     grad_proj = [by_split(grad_proj, split) for split in range(splits)]
     mid_sums = [orders[place % 2][1](sums) for place, sums in enumerate(mid_sums)]
+    text_sum = plane_sum(text_terms, bf16)
+    (grad_proj, mid_sums, text_sum) = lax.optimization_barrier((grad_proj, mid_sums, text_sum))
     grad_hidden_one = sum(
-        dot(grad_proj[split][place], qkv_full[place][split][0], NT)
+        dot(grad_proj[split][place], qkv_full[place][split], NT)
         for place in range(ranks)
         for split in range(splits)
     )
+    grad_hidden_one = dot(grad_hidden_one.astype(bf16), turn, NT)
     grad_shift_one = jnp.sum(grad_hidden_one, axis=0)
     grad_scale_one = jnp.sum(grad_hidden_one * normed_one, axis=0)
     grad_latents = grad_one + norm_back(
         grad_hidden_one * (1.0 + scale_one), normed_one, inverse_one
     )
-    grad_latents = dot(grad_latents.astype(bf16), turn, NT).astype(bf16).reshape(latents.shape)
+    grad_latents = grad_latents.astype(bf16).reshape(latents.shape)
+    grad_latents, up_sum = tie(grad_latents, up_sum)
     grad_latents = in_order(give_back(list(grad_latents), "lat"), "lat")
 
     time_terms = jnp.stack(
@@ -676,7 +704,10 @@
             grad_gate_two,
         )
     )
-    table_terms = jnp.pad(time_terms.T, ((0, 0), (3 * edge, piece_width - 3 * edge - 6)))
+    time_turn = lax.dot_general(
+        time_terms, turn.astype(f32), NN, precision=lax.Precision.HIGHEST
+    )
+    table_terms = jnp.pad(time_turn.T, ((0, 0), (3 * edge, piece_width - 3 * edge - 6)))
     one_sums = [
         kept_sums(
             hidden_one,
@@ -688,12 +719,8 @@
     one_sums = [orders[place % 2][0](sums) for place, sums in enumerate(one_sums)]
     one_sums = [sum_lat(orders[place % 2][1](sums)) for place, sums in enumerate(one_sums)]
     key_sum, val_sum, cq_sum, co_sum, out_sum = (sum_lat(sums)[:, :part] for sums in mid_sums)
-    time_natural = lax.dot_general(
-        time_terms, turn.astype(f32), NT, precision=lax.Precision.HIGHEST
-    )
-    text_natural = dot(text_terms.astype(bf16), turn, NT)
-    grad_time = over_latents(plane_sum(time_natural, f32)).reshape(-1, 6 * width)
-    grad_text = over_latents(plane_sum(text_natural, bf16).astype(bf16)).astype(f32)
+    grad_time = over_latents(plane_sum(time_terms, f32)).reshape(-1, 6 * width)
+    grad_text = over_latents(text_sum.astype(bf16)).astype(f32)
     grad_qkv = jnp.stack(
         [sums[:, : 3 * edge].reshape(share, 3, edge) for sums in one_sums], axis=2
     ).reshape(share, 3, part)
@@ -708,8 +735,8 @@
         cq_sum,
         jnp.stack((key_sum, val_sum), axis=1),
         co_sum.T,
-        sum_lat(up_sums),
-        sum_lat(down_sums).T,
+        up_sum,
+        down_sum.T,
     )
 
 

time: 2740 us -> 971 us (0.35)
  Pallas kernels: 1690 us -> 159 us
  waiting for transfers between devices: 581 us -> 373 us
  starting transfers between devices: 180 us -> 149 us
    pallas_call x8 -> x6, Pallas kernels: 1570 us -> 37.7 us  [lay(): pl.pallas_call(partial(assemble_kernel, plan, len(sources)), in_specs=[an...]
    ppermute x144 -> x105, waiting for transfers between devices: 581 us -> 270 us  [send_xor(): lax.ppermute(piece, axes, [(rank, rank ^ step) for rank in range(size)])]
    reduce_scatter x0 -> x2, waiting for transfers between devices: none -> 67.5 us  [scatter_all(): lax.psum_scatter(pack, EVERY, scatter_dimension=0, tiled=True).astype(f32)]
    all_gather x0 -> x2, waiting for transfers between devices: none -> 35.8 us  [gather_all(): return lax.all_gather(shard, EVERY, axis=shard.ndim - 2, tiled=True)]
    ppermute x144 -> x105, starting transfers between devices: 180 us -> 149 us  [send_xor(): lax.ppermute(piece, axes, [(rank, rank ^ step) for rank in range(size)])]
    dot_general x78 -> x74, matrix products: 180 us -> 188 us  [dot(): return lax.dot_general(left, right, dims, preferred_element_type=f32)]
  transfers between devices with their start and end apart: 144 -> 109, of which waited for: 52 -> 48; matrix products, arithmetic and copies ran while one was open for 8% -> 21% of each run, Pallas kernels for 41% -> 16%
where the time goes in v2:
time: 971 us; the launch traced here: 960 us
  waiting for transfers between devices  373 us (38%)
  matrix products  191 us (20%)
  Pallas kernels  159 us (16%)
  starting transfers between devices  149 us (15%)
  other arithmetic  41.1 us (4%)
  local copies, waits for them, and re-layouts  29.9 us (3%)
  between operations  16.2 us (2%)
    ppermute x105, waiting for transfers between devices, send_xor(): lax.ppermute(piece, axes, [(rank, rank ^ step) for rank in range(size)])  270 us
    dot_general x74, matrix products, dot(): return lax.dot_general(left, right, dims, preferred_element_type=f32)  188 us
    ppermute x105, starting transfers between devices, send_xor(): lax.ppermute(piece, axes, [(rank, rank ^ step) for rank in range(size)])  149 us
    reduce_scatter x2, waiting for transfers between devices, scatter_all(): lax.psum_scatter(pack, EVERY, scatter_dimension=0, tiled=True).astype(f32)  67.5 us
    pallas_call x1, Pallas kernels, attend_back(): pl.pallas_call(partial(attend_back_kernel, heads, min(512, total), len(pi...  58.4 us
    pallas_call x6, Pallas kernels, lay(): pl.pallas_call(partial(assemble_kernel, plan, len(sources)), in_specs=[an...  37.7 us
    all_gather x2, waiting for transfers between devices, gather_all(): return lax.all_gather(shard, EVERY, axis=shard.ndim - 2, tiled=True)  35.8 us
    pallas_call x1, Pallas kernels, attend(): pl.pallas_call(partial(attend_kernel, heads, len(pieces), own), grid=(row...  32.9 us
  transfers between devices with their start and end apart: 109, of which 48 were waited for; matrix products, arithmetic and copies ran while one was open for 21% of the time, Pallas kernels for 16%

profile of v2, /device:TPU:0, one launch (start us, length us, event | category | flops | bytes accessed | tf_op | source)
XLA Modules:
  0.0 960.4 jit_solution(15645322445272275587)
XLA Ops:
  30.3 11.3 %collective-permute-done.17 = bf16[72,896]{1,0:T(8,128)(2,1)S(1)} collective-permute-done((bf16[72,896]{1,0:T(8,128)(2,1)S(1)}, bf16[72,896]{1,0:T(8,128)(2,1)S(1)}, u32[]{:S(2)}, u32[]{:S(2)}) %collective-permute-start.17) | collective-permute-done | bytes 129056 | tf_op jit(solution)/shard_map/ppermute | solution.py:50
  48.2 10.2 %collective-permute-done.19.refs_1_ = bf16[288,896]{1,0:T(8,128)(2,1)S(1)} collective-permute-done((bf16[288,896]{1,0:T(8,128)(2,1)S(1)}, bf16[288,896]{1,0:T(8,128)(2,1)S(1)}, u32[]{:S(2)}, u32[]{:S(2)}) %collective-permute-start.19) | collective-permute-done | bytes 516128 | tf_op jit(solution)/shard_map/ppermute | solution.py:50
  64.5 15.8 %collective-permute-start.13 = (bf16[128,1152]{1,0:T(8,128)(2,1)S(1)}, bf16[128,1152]{1,0:T(8,128)(2,1)S(1)}, u32[]{:S(2)}, u32[]{:S(2)}) collective-permute-start(bf16[128,1152]{1,0:T(8,128)(2,1)S(1)} %get-tuple-element.228), channel_id=1, source_target_pairs={{0,4},{4,0},{8,12},{12,8},{1,5},{5,1},{9,13},{13,9},{2,6},{6,2},{1... | collective-permute-start | bytes 884744 | tf_op jit(solution)/shard_map/ppermute | solution.py:50
  83.0 13.9 %collective-permute-done.13 = bf16[128,1152]{1,0:T(8,128)(2,1)S(1)} collective-permute-done((bf16[128,1152]{1,0:T(8,128)(2,1)S(1)}, bf16[128,1152]{1,0:T(8,128)(2,1)S(1)}, u32[]{:S(2)}, u32[]{:S(2)}) %collective-permute-start.13) | collective-permute-done | bytes 294944 | tf_op jit(solution)/shard_map/ppermute | solution.py:50
  100.0 9.7 %collective-permute-done.14 = bf16[128,1152]{1,0:T(8,128)(2,1)S(1)} collective-permute-done((bf16[128,1152]{1,0:T(8,128)(2,1)S(1)}, bf16[128,1152]{1,0:T(8,128)(2,1)S(1)}, u32[]{:S(2)}, u32[]{:S(2)}) %collective-permute-start.14) | collective-permute-done | bytes 294944 | tf_op jit(solution)/shard_map/ppermute | solution.py:50
  146.5 15.4 %collective-permute-done.23.refs_1_ = bf16[512,896]{1,0:T(8,128)(2,1)S(1)} collective-permute-done((bf16[512,896]{1,0:T(8,128)(2,1)S(1)}, bf16[512,896]{1,0:T(8,128)(2,1)S(1)}, u32[]{:S(2)}, u32[]{:S(2)}) %collective-permute-start.23) | collective-permute-done | bytes 917536 | tf_op jit(solution)/shard_map/ppermute | solution.py:50
  161.9 23.2 %collective-permute-done.25.refs_3_ = bf16[512,896]{1,0:T(8,128)(2,1)S(1)} collective-permute-done((bf16[512,896]{1,0:T(8,128)(2,1)S(1)}, bf16[512,896]{1,0:T(8,128)(2,1)S(1)}, u32[]{:S(2)}, u32[]{:S(2)}) %collective-permute-start.25) | collective-permute-done | bytes 917536 | tf_op jit(solution)/shard_map/ppermute | solution.py:50
  192.2 32.9 %shard_map.214 = (bf16[512,288]{1,0:T(8,128)(2,1)}, bf16[512,288]{1,0:T(8,128)(2,1)}, bf16[512,288]{1,0:T(8,128)(2,1)}, bf16[512,288]{1,0:T(8,128)(2,1)}, f32[4,2048,72]{2,1,0:T(8,128)}, /*index=5*/f32[8,2048]{1,0:T(8,128)}) custom-call(bf16[512,896]{1,0:T(8,128)(2,1)} %get-tuple-element.214.refs_0_, bf16[512,896]{1,0:T(8,128)(2,1)} %copy-done.106, ...), custom_call_target="tpu_custom_call" | custom-call | flops 17179869184 | bytes 7340032 | tf_op jit(solution)/shard_map/pallas_call | solution.py:160
  247.5 10.9 %shard_map.215 = (bf16[1152,640]{1,0:T(8,128)(2,1)}, bf16[1152,640]{1,0:T(8,128)(2,1)}, bf16[1152,640]{1,0:T(8,128)(2,1)}, bf16[1152,640]{1,0:T(8,128)(2,1)}, bf...) custom-call(bf16[2304,3200]{1,0:T(8,128)(2,1)} %all-gather.3.cloned., ...), custom_call_target="tpu_custom_call" | custom-call | tf_op jit(solution)/shard_map/pallas_call | solution.py:407
  273.5 11.6 %shard_map.216 = (bf16[512,640]{1,0:T(8,128)(2,1)}, bf16[512,640]{1,0:T(8,128)(2,1)}) custom-call(bf16[512,640]{1,0:T(8,128)(2,1)} %convolution_convert_fusion.25.refs_0_, bf16[512,640]{1,0:T(8,128)(2,1)} %convolution_convert_fusion.24.refs_1_, bf16[120,640]{1,0:T(8,128)(2,1)} %convolution_convert_fusion.29.refs_2_, ...), custom_call_target="tpu_custom_call" | custom-call | tf_op jit(solution)/shard_map/pallas_call | solution.py:318
  291.1 35.8 %all-gather.5.cloned.1.call-done = bf16[2,2304,2304]{2,1,0:T(8,128)(2,1)} async-done(((bf16[2,72,2304]{2,1,0:T(8,128)(2,1)}), bf16[2,2304,2304]{2,1,0:T(8,128)(2,1)}) %all-gather.5.cloned.1.call-update) | async-done | bytes 21233680 | tf_op jit(solution)/shard_map/all_gather | solution.py:461
  333.1 7.5 fusion.25
  340.6 7.1 convolution_convert_fusion.2.refs_1_
  354.6 8.0 shard_map.218
  367.6 9.2 fusion.14
  390.6 7.7 multiply_reduce_fusion
  398.3 8.7 fusion.22
  407.0 9.4 fusion.70
  420.9 18.7 %shard_map.217 = (bf16[512,640]{1,0:T(8,128)(2,1)}, bf16[512,640]{1,0:T(8,128)(2,1)}, bf16[120,640]{1,0:T(8,128)(2,1)}, bf16[120,640]{1,0:T(8,128)(2,1)}, bf16[1...) custom-call(bf16[512,640]{1,0:T(8,128)(2,1)} %convolution_convert_fusion.25.refs_0_, ...), custom_call_target="tpu_custom_call" | custom-call | tf_op jit(solution)/shard_map/pallas_call | solution.py:374
  458.3 8.1 shard_map.220
  546.9 58.4 %shard_map.219 = (bf16[512,896]{1,0:T(8,128)(2,1)}, bf16[512,896]{1,0:T(8,128)(2,1)}, bf16[512,896]{1,0:T(8,128)(2,1)}, bf16[512,896]{1,0:T(8,128)(2,1)}) custom-call(bf16[512,896]{1,0:T(8,128)(2,1)} %get-tuple-element.214.refs_0_, bf16[512,896]{1,0:T(8,128)(2,1)} %copy-done.106, bf16[512,896]{1,0:T(8,128)(2,1)} %copy-done.108, ...), custom_call_target="tpu_custom_call" | custom-call | flops 42949672960 | bytes 14680064 | tf_op jit(solution)/shard_map/pallas_call | solution.py:264
  606.0 67.5 %reduce-scatter.5.cloned.1.call-done = bf16[72,2304]{1,0:T(8,128)(2,1)} async-done(((bf16[2304,2304]{1,0:T(8,128)(2,1)}), bf16[72,2304]{1,0:T(8,128)(2,1)}) %reduce-scatter.5.cloned.1.call-update) | async-done | bytes 331792 | tf_op jit(solution)/shard_map/reduce_scatter | solution.py:466
  689.9 8.7 collective-permute-done.46
  701.1 17.3 %collective-permute-done.53 = bf16[512,896]{1,0:T(8,128)(2,1)S(1)} collective-permute-done((bf16[512,896]{1,0:T(8,128)(2,1)S(1)}, bf16[512,896]{1,0:T(8,128)(2,1)S(1)}, u32[]{:S(2)}, u32[]{:S(2)}) %collective-permute-start.53) | collective-permute-done | bytes 917536 | tf_op jit(solution)/shard_map/ppermute | solution.py:50
  719.9 18.2 %collective-permute-done.54 = bf16[512,896]{1,0:T(8,128)(2,1)S(1)} collective-permute-done((bf16[512,896]{1,0:T(8,128)(2,1)S(1)}, bf16[512,896]{1,0:T(8,128)(2,1)S(1)}, u32[]{:S(2)}, u32[]{:S(2)}) %collective-permute-start.54) | collective-permute-done | bytes 917536 | tf_op jit(solution)/shard_map/ppermute | solution.py:50
  764.1 9.0 fusion.67
  800.6 12.4 %collective-permute-start.102 = (bf16[72,640]{1,0:T(8,128)(2,1)S(1)}, bf16[72,640]{1,0:T(8,128)(2,1)S(1)}, u32[]{:S(2)}, u32[]{:S(2)}) collective-permute-start(bf16[72,640]{1,0:T(8,128)(2,1)S(1)} %get-tuple-element.255), channel_id=1, source_target_pairs={{0,4},{4,0},{8,12},{12,8},{1,5},{5,1},{9,13},{13,9},{2,6},{6,2},{1... | collective-permute-start | bytes 276488 | tf_op jit(solution)/shard_map/ppermute | solution.py:50
  872.5 15.0 %collective-permute-done.64 = bf16[128,1152]{1,0:T(8,128)(2,1)S(1)} collective-permute-done((bf16[128,1152]{1,0:T(8,128)(2,1)S(1)}, bf16[128,1152]{1,0:T(8,128)(2,1)S(1)}, u32[]{:S(2)}, u32[]{:S(2)}) %collective-permute-start.64) | collective-permute-done | bytes 294944 | tf_op jit(solution)/shard_map/ppermute | solution.py:50
  895.7 7.5 collective-permute-done.85
  906.0 10.2 %collective-permute-done.77 = bf16[576,896]{1,0:T(8,128)(2,1)S(1)} collective-permute-done((bf16[576,896]{1,0:T(8,128)(2,1)S(1)}, bf16[576,896]{1,0:T(8,128)(2,1)S(1)}, u32[]{:S(2)}, u32[]{:S(2)}) %collective-permute-start.77) | collective-permute-done | bytes 1032224 | tf_op jit(solution)/shard_map/ppermute | solution.py:50
  917.6 8.9 collective-permute-done.86
  940.1 10.4 %collective-permute-done.80 = bf16[72,896]{1,0:T(8,128)(2,1)S(1)} collective-permute-done((bf16[72,896]{1,0:T(8,128)(2,1)S(1)}, bf16[72,896]{1,0:T(8,128)(2,1)S(1)}, u32[]{:S(2)}, u32[]{:S(2)}) %collective-permute-start.80) | collective-permute-done | bytes 129056 | tf_op jit(solution)/shard_map/ppermute | solution.py:50
  (661 shorter events, 425.3 us)
Async XLA Ops:
  7.2 240.3 %all-gather.3.cloned.1.call-start = ((), (), s32[]{:S(2)}) async-start(), calls=%async_computation.2 | async-start | bytes 15206400 | tf_op jit(solution)/shard_map/all_gather | solution.py:461
  12.4 314.5 %all-gather.5.cloned.1.call-start = ((), (), s32[]{:S(2)}) async-start(), calls=%async_computation.3 | async-start | bytes 21897216 | tf_op jit(solution)/shard_map/all_gather | solution.py:461
  13.4 516.3 %reduce-scatter.3.cloned.1.call-start = ((), (), s32[]{:S(2)}) async-start(), calls=%async_computation.4 | async-start | bytes 10948608 | tf_op jit(solution)/shard_map/reduce_scatter | solution.py:466
  46.7 35.8 %collective-permute-start.6 = (bf16[288,896]{1,0:T(8,128)(2,1)}, bf16[288,896]{1,0:T(8,128)(2,1)}, u32[]{:S(2)}, u32[]{:S(2)}) collective-permute-start(bf16[288,896]{1,0:T(8,128)(2,1)} %get-tuple-element.279.refs_0_), channel_id=1, source_target_pairs={{0,1},{1,0},{2,3},{3,2},{4,5},{5,4},{6,7},{7,6},{8,9},{9,8},{10,11... | collective-permute-start | bytes 1548296 | tf_op jit(solution)/shard_map/ppermute | solution.py:50
  61.4 50.7 %collective-permute-start.21 = (bf16[576,896]{1,0:T(8,128)(2,1)}, bf16[576,896]{1,0:T(8,128)(2,1)}, u32[]{:S(2)}, u32[]{:S(2)}) collective-permute-start(bf16[576,896]{1,0:T(8,128)(2,1)} %shard_map.212.refs_0_), channel_id=1, source_target_pairs={{0,1},{1,0},{2,3},{3,2},{4,5},{5,4},{6,7},{7,6},{8,9},{9,8},{10,11... | collective-permute-start | bytes 3096584 | tf_op jit(solution)/shard_map/ppermute | solution.py:50
  64.5 32.4 %collective-permute-start.13 = (bf16[128,1152]{1,0:T(8,128)(2,1)S(1)}, bf16[128,1152]{1,0:T(8,128)(2,1)S(1)}, u32[]{:S(2)}, u32[]{:S(2)}) collective-permute-start(bf16[128,1152]{1,0:T(8,128)(2,1)S(1)} %get-tuple-element.228), channel_id=1, source_target_pairs={{0,4},{4,0},{8,12},{12,8},{1,5},{5,1},{9,13},{13,9},{2,6},{6,2},{1... | collective-permute-start | bytes 884744 | tf_op jit(solution)/shard_map/ppermute | solution.py:50
  81.0 29.7 %collective-permute-start.3 = (bf16[288,896]{1,0:T(8,128)(2,1)}, bf16[288,896]{1,0:T(8,128)(2,1)}, u32[]{:S(2)}, u32[]{:S(2)}) collective-permute-start(bf16[288,896]{1,0:T(8,128)(2,1)} %get-tuple-element.279.refs_0_), channel_id=1, source_target_pairs={{0,2},{2,0},{1,3},{3,1},{4,6},{6,4},{5,7},{7,5},{8,10},{10,8},{9,1... | collective-permute-start | bytes 1548296 | tf_op jit(solution)/shard_map/ppermute | solution.py:50
  138.8 46.4 %collective-permute-start.25 = (bf16[512,896]{1,0:T(8,128)(2,1)S(1)}, bf16[512,896]{1,0:T(8,128)(2,1)S(1)}, u32[]{:S(2)}, u32[]{:S(2)}) collective-permute-start(bf16[512,896]{1,0:T(8,128)(2,1)S(1)} %get-tuple-element.211), channel_id=1, source_target_pairs={{0,3},{1,2},{2,1},{3,0},{4,7},{5,6},{6,5},{7,4},{8,11},{9,10},{10,... | collective-permute-start | bytes 2752520 | tf_op jit(solution)/shard_map/ppermute | solution.py:50
  143.7 47.6 %collective-permute-start.24 = (bf16[512,896]{1,0:T(8,128)(2,1)S(1)}, bf16[512,896]{1,0:T(8,128)(2,1)S(1)}, u32[]{:S(2)}, u32[]{:S(2)}) collective-permute-start(bf16[512,896]{1,0:T(8,128)(2,1)S(1)} %get-tuple-element.213), channel_id=1, source_target_pairs={{0,2},{1,3},{2,0},{3,1},{4,6},{5,7},{6,4},{7,5},{8,10},{9,11},{10,... | collective-permute-start | bytes 2752520 | tf_op jit(solution)/shard_map/ppermute | solution.py:50
  229.8 110.8 %collective-permute-start.10 = (bf16[128,1152]{1,0:T(8,128)(2,1)}, bf16[128,1152]{1,0:T(8,128)(2,1)}, u32[]{:S(2)}, u32[]{:S(2)}) collective-permute-start(bf16[128,1152]{1,0:T(8,128)(2,1)} %get-tuple-element.226), channel_id=1, source_target_pairs={{0,4},{4,0},{8,12},{12,8},{1,5},{5,1},{9,13},{13,9},{2,6},{6,2},{1... | collective-permute-start | bytes 884744 | tf_op jit(solution)/shard_map/ppermute | solution.py:50
  236.1 104.5 %collective-permute-start.11 = (bf16[128,1152]{1,0:T(8,128)(2,1)}, bf16[128,1152]{1,0:T(8,128)(2,1)}, u32[]{:S(2)}, u32[]{:S(2)}) collective-permute-start(bf16[128,1152]{1,0:T(8,128)(2,1)} %get-tuple-element.225), channel_id=1, source_target_pairs={{0,8},{4,12},{8,0},{12,4},{1,9},{5,13},{9,1},{13,5},{2,10},{6,14},... | collective-permute-start | bytes 884744 | tf_op jit(solution)/shard_map/ppermute | solution.py:50
  238.5 102.2 %collective-permute-start.12 = (bf16[128,1152]{1,0:T(8,128)(2,1)}, bf16[128,1152]{1,0:T(8,128)(2,1)}, u32[]{:S(2)}, u32[]{:S(2)}) collective-permute-start(bf16[128,1152]{1,0:T(8,128)(2,1)} %get-tuple-element.224), channel_id=1, source_target_pairs={{0,12},{4,8},{8,4},{12,0},{1,13},{5,9},{9,5},{13,1},{2,14},{6,10},... | collective-permute-start | bytes 884744 | tf_op jit(solution)/shard_map/ppermute | solution.py:50
  362.7 310.8 %reduce-scatter.5.cloned.1.call-start = ((), (), s32[]{:S(2)}) async-start(), calls=%async_computation.5 | async-start | bytes 10948608 | tf_op jit(solution)/shard_map/reduce_scatter | solution.py:466
  444.7 46.3 %collective-permute-start.60 = (bf16[120,1152]{1,0:T(8,128)(2,1)S(1)}, bf16[120,1152]{1,0:T(8,128)(2,1)}, u32[]{:S(2)}, u32[]{:S(2)}) collective-permute-start(bf16[120,1152]{1,0:T(8,128)(2,1)S(1)} %fusion.58), channel_id=1, source_target_pairs={{0,1},{1,0},{2,3},{3,2},{4,5},{5,4},{6,7},{7,6},{8,9},{9,8},{10,11... | collective-permute-start | bytes 829448 | tf_op jit(solution)/shard_map/ppermute | solution.py:50
  444.9 49.0 %collective-permute-start.61 = (bf16[120,1152]{1,0:T(8,128)(2,1)S(1)}, bf16[120,1152]{1,0:T(8,128)(2,1)}, u32[]{:S(2)}, u32[]{:S(2)}) collective-permute-start(bf16[120,1152]{1,0:T(8,128)(2,1)S(1)} %fusion.58), channel_id=1, source_target_pairs={{0,2},{1,3},{2,0},{3,1},{4,6},{5,7},{6,4},{7,5},{8,10},{9,11},{10,... | collective-permute-start | bytes 829448 | tf_op jit(solution)/shard_map/ppermute | solution.py:50
  446.4 47.5 %collective-permute-start.62 = (bf16[120,1152]{1,0:T(8,128)(2,1)S(1)}, bf16[120,1152]{1,0:T(8,128)(2,1)}, u32[]{:S(2)}, u32[]{:S(2)}) collective-permute-start(bf16[120,1152]{1,0:T(8,128)(2,1)S(1)} %fusion.58), channel_id=1, source_target_pairs={{0,3},{1,2},{2,1},{3,0},{4,7},{5,6},{6,5},{7,4},{8,11},{9,10},{10,... | collective-permute-start | bytes 829448 | tf_op jit(solution)/shard_map/ppermute | solution.py:50
  468.9 34.5 %collective-permute-start.40 = (bf16[128,1152]{1,0:T(8,128)(2,1)S(1)}, bf16[128,1152]{1,0:T(8,128)(2,1)S(1)}, u32[]{:S(2)}, u32[]{:S(2)}) collective-permute-start(bf16[128,1152]{1,0:T(8,128)(2,1)S(1)} %get-tuple-element.221), channel_id=1, source_target_pairs={{0,8},{4,12},{8,0},{12,4},{1,9},{5,13},{9,1},{13,5},{2,10},{6,14},... | collective-permute-start | bytes 884744 | tf_op jit(solution)/shard_map/ppermute | solution.py:50
  493.9 34.1 %collective-permute-start.37 = (bf16[576,640]{1,0:T(8,128)(2,1)S(1)}, bf16[576,640]{1,0:T(8,128)(2,1)S(1)}, u32[]{:S(2)}, u32[]{:S(2)}) collective-permute-start(bf16[576,640]{1,0:T(8,128)(2,1)S(1)} %convolution_convert_fusion.11), channel_id=1, source_target_pairs={{0,16},{16,0},{1,17},{17,1},{2,18},{18,2},{3,19},{19,3},{4,20},{20... | collective-permute-start | bytes 2211848 | tf_op jit(solution)/shard_map/ppermute | solution.py:50
  531.5 154.2 %collective-permute-start.52 = (bf16[576,640]{1,0:T(8,128)(2,1)}, bf16[576,640]{1,0:T(8,128)(2,1)}, u32[]{:S(2)}, u32[]{:S(2)}) collective-permute-start(bf16[576,640]{1,0:T(8,128)(2,1)} %add_convert_fusion.12), channel_id=1, source_target_pairs={{0,1},{1,0},{2,3},{3,2},{4,5},{5,4},{6,7},{7,6},{8,9},{9,8},{10,11... | collective-permute-start | bytes 2211848 | tf_op jit(solution)/shard_map/ppermute | solution.py:50
  534.7 140.8 %collective-permute-start.51 = (bf16[288,640]{1,0:T(8,128)(2,1)}, bf16[288,640]{1,0:T(8,128)(2,1)}, u32[]{:S(2)}, u32[]{:S(2)}) collective-permute-start(bf16[288,640]{1,0:T(8,128)(2,1)} %slice.321), channel_id=1, source_target_pairs={{0,2},{2,0},{1,3},{3,1},{4,6},{6,4},{5,7},{7,5},{8,10},{10,8},{9,1... | collective-permute-start | bytes 1105928 | tf_op jit(solution)/shard_map/ppermute | solution.py:50
  537.0 141.3 %collective-permute-start.50 = (bf16[288,640]{1,0:T(8,128)(2,1)}, bf16[288,640]{1,0:T(8,128)(2,1)S(1)}, u32[]{:S(2)}, u32[]{:S(2)}) collective-permute-start(bf16[288,640]{1,0:T(8,128)(2,1)} %slice.319), channel_id=1, source_target_pairs={{0,2},{2,0},{1,3},{3,1},{4,6},{6,4},{5,7},{7,5},{8,10},{10,8},{9,1... | collective-permute-start | bytes 1105928 | tf_op jit(solution)/shard_map/ppermute | solution.py:50
  542.5 146.1 %collective-permute-start.49 = (bf16[576,640]{1,0:T(8,128)(2,1)}, bf16[576,640]{1,0:T(8,128)(2,1)}, u32[]{:S(2)}, u32[]{:S(2)}) collective-permute-start(bf16[576,640]{1,0:T(8,128)(2,1)} %add_convert_fusion.16), channel_id=1, source_target_pairs={{0,1},{1,0},{2,3},{3,2},{4,5},{5,4},{6,7},{7,6},{8,9},{9,8},{10,11... | collective-permute-start | bytes 2211848 | tf_op jit(solution)/shard_map/ppermute | solution.py:50
  546.4 134.7 %collective-permute-start.48 = (bf16[288,640]{1,0:T(8,128)(2,1)}, bf16[288,640]{1,0:T(8,128)(2,1)}, u32[]{:S(2)}, u32[]{:S(2)}) collective-permute-start(bf16[288,640]{1,0:T(8,128)(2,1)} %slice.317), channel_id=1, source_target_pairs={{0,2},{2,0},{1,3},{3,1},{4,6},{6,4},{5,7},{7,5},{8,10},{10,8},{9,1... | collective-permute-start | bytes 1105928 | tf_op jit(solution)/shard_map/ppermute | solution.py:50
  681.1 37.2 %collective-permute-start.53 = (bf16[512,896]{1,0:T(8,128)(2,1)S(1)}, bf16[512,896]{1,0:T(8,128)(2,1)S(1)}, u32[]{:S(2)}, u32[]{:S(2)}) collective-permute-start(bf16[512,896]{1,0:T(8,128)(2,1)S(1)} %copy-done.111), channel_id=1, source_target_pairs={{0,3},{1,2},{2,1},{3,0},{4,7},{5,6},{6,5},{7,4},{8,11},{9,10},{10,... | collective-permute-start | bytes 2752520 | tf_op jit(solution)/shard_map/ppermute | solution.py:50
  684.1 53.9 %collective-permute-start.54 = (bf16[512,896]{1,0:T(8,128)(2,1)S(1)}, bf16[512,896]{1,0:T(8,128)(2,1)S(1)}, u32[]{:S(2)}, u32[]{:S(2)}) collective-permute-start(bf16[512,896]{1,0:T(8,128)(2,1)S(1)} %copy-done.110), channel_id=1, source_target_pairs={{0,1},{1,0},{2,3},{3,2},{4,5},{5,4},{6,7},{7,6},{8,9},{9,8},{10,11... | collective-permute-start | bytes 2752520 | tf_op jit(solution)/shard_map/ppermute | solution.py:50
  685.7 53.5 %collective-permute-start.45 = (bf16[512,896]{1,0:T(8,128)(2,1)S(1)}, bf16[512,896]{1,0:T(8,128)(2,1)S(1)}, u32[]{:S(2)}, u32[]{:S(2)}) collective-permute-start(bf16[512,896]{1,0:T(8,128)(2,1)S(1)} %copy-done.109), channel_id=1, source_target_pairs={{0,2},{1,3},{2,0},{3,1},{4,6},{5,7},{6,4},{7,5},{8,10},{9,11},{10,... | collective-permute-start | bytes 2752520 | tf_op jit(solution)/shard_map/ppermute | solution.py:50
  698.9 42.6 %collective-permute-start.59 = (bf16[288,640]{1,0:T(8,128)(2,1)S(1)}, bf16[288,640]{1,0:T(8,128)(2,1)S(1)}, u32[]{:S(2)}, u32[]{:S(2)}) collective-permute-start(bf16[288,640]{1,0:T(8,128)(2,1)S(1)} %slice.327), channel_id=1, source_target_pairs={{0,2},{2,0},{1,3},{3,1},{4,6},{6,4},{5,7},{7,5},{8,10},{10,8},{9,1... | collective-permute-start | bytes 1105928 | tf_op jit(solution)/shard_map/ppermute | solution.py:50
  699.5 49.7 %collective-permute-start.58 = (bf16[288,640]{1,0:T(8,128)(2,1)S(1)}, bf16[288,640]{1,0:T(8,128)(2,1)S(1)}, u32[]{:S(2)}, u32[]{:S(2)}) collective-permute-start(bf16[288,640]{1,0:T(8,128)(2,1)S(1)} %add_convert_fusion.31), channel_id=1, source_target_pairs={{0,1},{1,0},{2,3},{3,2},{4,5},{5,4},{6,7},{7,6},{8,9},{9,8},{10,11... | collective-permute-start | bytes 1105928 | tf_op jit(solution)/shard_map/ppermute | solution.py:50
  786.6 74.1 %collective-permute-start.66 = (bf16[120,1152]{1,0:T(8,128)(2,1)S(1)}, bf16[120,1152]{1,0:T(8,128)(2,1)S(1)}, u32[]{:S(2)}, u32[]{:S(2)}) collective-permute-start(bf16[120,1152]{1,0:T(8,128)(2,1)S(1)} %copy-done.47), channel_id=1, source_target_pairs={{0,12},{4,8},{8,4},{12,0},{1,13},{5,9},{9,5},{13,1},{2,14},{6,10},... | collective-permute-start | bytes 829448 | tf_op jit(solution)/shard_map/ppermute | solution.py:50
  789.1 74.0 %collective-permute-start.67 = (bf16[120,1152]{1,0:T(8,128)(2,1)S(1)}, bf16[120,1152]{1,0:T(8,128)(2,1)S(1)}, u32[]{:S(2)}, u32[]{:S(2)}) collective-permute-start(bf16[120,1152]{1,0:T(8,128)(2,1)S(1)} %copy-done.47), channel_id=1, source_target_pairs={{0,8},{4,12},{8,0},{12,4},{1,9},{5,13},{9,1},{13,5},{2,10},{6,14},... | collective-permute-start | bytes 829448 | tf_op jit(solution)/shard_map/ppermute | solution.py:50
  857.0 30.7 %collective-permute-start.84 = (bf16[576,896]{1,0:T(8,128)(2,1)S(1)}, bf16[576,896]{1,0:T(8,128)(2,1)S(1)}, u32[]{:S(2)}, u32[]{:S(2)}) collective-permute-start(bf16[576,896]{1,0:T(8,128)(2,1)S(1)} %copy-done.105), channel_id=1, source_target_pairs={{0,16},{16,0},{1,17},{17,1},{2,18},{18,2},{3,19},{19,3},{4,20},{20... | collective-permute-start | bytes 3096584 | tf_op jit(solution)/shard_map/ppermute | solution.py:50
  860.0 29.6 %collective-permute-start.76 = (bf16[576,896]{1,0:T(8,128)(2,1)S(1)}, bf16[576,896]{1,0:T(8,128)(2,1)S(1)}, u32[]{:S(2)}, u32[]{:S(2)}) collective-permute-start(bf16[576,896]{1,0:T(8,128)(2,1)S(1)} %add_convert_fusion.6), channel_id=1, source_target_pairs={{0,16},{16,0},{1,17},{17,1},{2,18},{18,2},{3,19},{19,3},{4,20},{20... | collective-permute-start | bytes 3096584 | tf_op jit(solution)/shard_map/ppermute | solution.py:50
  (211 other events, 3062.5 us)
Sparse Core Ops, SparseCore 0:
  12.5 146.0 all-gather.2
  162.1 164.7 all-gather.4
  362.8 163.8 reduce-scatter.2
  532.7 140.8 reduce-scatter.4

commit v3 on v2

--- a/solution.py
+++ b/solution.py
@@ -452,37 +452,18 @@
         half = assemble([with_others(start, ROW)])[0]
         stacks = [[piece] for piece in with_others(half, "tensor")]
     cores = range(1, lax.axis_size("fsdp"))
-    return assemble(
-        [stack + [send_xor(piece, "fsdp", step) for step in cores for piece in stack] for stack in stacks]
-    )
+    stacks = [
+        stack + [send_xor(piece, "fsdp", step) for step in cores for piece in stack] for stack in stacks
+    ]
+    return assemble(stacks), start
 
 
 def gather_all(shard):
     return lax.all_gather(shard, EVERY, axis=shard.ndim - 2, tiled=True)
 
 
-def scatter_all(pieces):
-    pack = assemble([pieces])[0]
+def scatter_all(pack):
     return lax.psum_scatter(pack, EVERY, scatter_dimension=0, tiled=True).astype(f32)
-
-
-def kept_sums(left, rights, extra=None):
-    cores = lax.axis_size("fsdp")
-    half = left.shape[1] // cores
-    out = []
-    for right in rights:
-        sums = []
-        for core in range(cores):
-            rows = slice(core * half, (core + 1) * half)
-            total = dot(left[:, rows], right, TN)
-            if extra is not None:
-                total += extra[rows]
-            sums.append(total)
-        total = sums[0]
-        for core in range(1, cores):
-            total += send_xor(sums[core].astype(bf16), "fsdp", core).astype(f32)
-        out.append(total.astype(bf16))
-    return out
 
 
 def sum_pieces(pieces, axes, dtype=bf16):
@@ -492,21 +473,38 @@
     return total.astype(dtype)
 
 
-def row_blocks(piece, count):
-    size = piece.shape[0] // count
-    return [piece[place * size : (place + 1) * size] for place in range(count)]
-
-
-def sum_tensor(parts):
-    return [sum_pieces(parts, "tensor")]
-
-
-def sum_row(parts):
-    return [sum_pieces(row_blocks(part, lax.axis_size(ROW)), ROW) for part in parts]
-
-
-def sum_lat(parts):
-    return sum_pieces(row_blocks(parts[0], lax.axis_size("lat")), "lat", f32)
+def sum_blocks(pack, axes, dtype=bf16):
+    count = lax.axis_size(axes)
+    size = pack.shape[0] // count
+    blocks = [pack[place * size : (place + 1) * size] for place in range(count)]
+    return sum_pieces(blocks, axes, dtype)
+
+
+def pack_for(first, grads):
+    splits, cores, ranks = (lax.axis_size(axes) for axes in ("tensor", "fsdp", ROW))
+    rows, columns = grads[0][0].shape
+    size = rows // cores // ranks
+    plan = []
+    for piece, row in enumerate(grads):
+        for split in range(splits):
+            for core in range(cores):
+                for rank in range(ranks):
+                    place = split * ranks + rank if first == "tensor" else rank * splits + split
+                    source = (piece * splits + split, (core * ranks + rank) * size, size, 0, columns)
+                    plan.append(source + (core, place * size, piece * columns))
+    sources = [values for row in grads for values in row]
+    return lay(sources, plan, [(splits * rows // cores, columns * len(grads))] * cores)
+
+
+def pack_grid(grads):
+    rows, columns = grads[0][0].shape
+    count = len(grads[0])
+    plan = [
+        (place * count + row, 0, rows, 0, columns, 0, row * rows, place * columns)
+        for place in range(len(grads))
+        for row in range(count)
+    ]
+    return lay([values for row in grads for values in row], plan, [(rows * count, columns * len(grads))])[0]
 
 
 def own_order(share, width):
@@ -545,16 +543,18 @@
     mid_shard = jnp.concatenate(
         [padded(piece) for piece in (w_out.T, w_ckv[:, 0], w_ckv[:, 1], w_cq, w_co.T)], axis=1
     )
-    mid_full = gather_all(mid_shard)
-    two_full = gather_all(jnp.stack((w_up, w_down.T)))
     shard_qkv = jnp.transpose(w_qkv.reshape(share, 3, ranks, edge), (2, 0, 1, 3)).reshape(
         ranks, share, 3 * edge
     )
     fill = jnp.pad(table.T, ((0, 0), (0, piece_width - 3 * edge - 6)))
-    qkv_full = [
+    qkv_got = [
         gather(jnp.concatenate((shard_qkv[place], fill), axis=1), place % 2 == 0)
         for place in range(ranks)
     ]
+    qkv_full = [full for full, _ in qkv_got]
+    mid_shard = lax.optimization_barrier([mid_shard] + [start for _, start in qkv_got])[0]
+    mid_full = gather_all(mid_shard)
+    two_full = gather_all(jnp.stack((w_up, w_down.T)))
 
     turn = own_order(share, width)
     residual = jnp.concatenate(latents_got, axis=0).astype(f32)
@@ -570,10 +570,10 @@
 
     normed_one, inverse_one = norm_parts(residual)
     hidden_one = (normed_one * (1.0 + scale_one) + shift_one).astype(bf16)
-    hidden_one = dot(hidden_one, turn).astype(bf16)
+    hidden_turn = dot(hidden_one, turn).astype(bf16)
     mixed = [None] * groups
     for split in range(splits):
-        pieces = [dot(hidden_one, full[split]).astype(bf16) for full in qkv_full]
+        pieces = [dot(hidden_turn, full[split]).astype(bf16) for full in qkv_full]
         for other in range(ranks):
             step = other * splits + split
             piece = choose(pieces, jnp.bitwise_xor(rank, other))
@@ -626,8 +626,10 @@
         grad_active = dot(grad_z, down_full[split])
         _, pull = jax.vjp(partial(jax.nn.gelu, approximate=True), inner[split])
         grad_inner.append(pull(grad_active)[0].astype(bf16))
-    down_sum = scatter_all([dot(grad_z, piece, TN).astype(bf16) for piece in active])
-    up_sum = scatter_all([dot(hidden_two, piece, TN).astype(bf16) for piece in grad_inner])
+    down_sum = scatter_all(pack_grid([[dot(grad_z, piece, TN).astype(bf16) for piece in active]]))
+    up_sum = scatter_all(
+        pack_grid([[dot(hidden_two, piece, TN).astype(bf16) for piece in grad_inner]])
+    )
     grad_hidden_two = sum(dot(grad_inner[split], up_full[split], NT) for split in range(splits))
     grad_shift_two = jnp.sum(grad_hidden_two, axis=0)
     grad_scale_two = jnp.sum(grad_hidden_two * normed_two, axis=0)
@@ -653,8 +655,8 @@
             piece = choose(cuts, jnp.bitwise_xor(rank, other))
             grad_heads[step] = send_xor(piece, HEAD_GROUP, step) if step else piece
     caption_turn = dot(caption, turn).astype(bf16)
-    mid_sums = [
-        kept_sums(left, rights)
+    mid_grads = [
+        [dot(left, right, TN).astype(bf16) for right in rights]
         for left, rights in (
             (caption_turn, from_own(grad_ck)),
             (caption_turn, from_own(grad_cv)),
@@ -663,22 +665,27 @@
             (dot(grad_out_one, turn).astype(bf16), att_own),
         )
     ]
-    (grad_heads[0], mid_sums, result_back, down_sum) = lax.optimization_barrier(
-        (grad_heads[0], mid_sums, result_back, down_sum)
-    )
-    orders = [(sum_tensor, sum_row), (sum_row, sum_tensor)]
-    mid_sums = [orders[place % 2][0](sums) for place, sums in enumerate(mid_sums)]
+    pack_a = sum_pieces(pack_for("tensor", mid_grads[:3]), "fsdp")
+    pack_b = sum_pieces(pack_for(ROW, mid_grads[3:]), "fsdp")
+    (grad_heads[0], pack_a, pack_b, result_back) = lax.optimization_barrier(
+        (grad_heads[0], pack_a, pack_b, result_back)
+    )
+    pack_a, pack_b = sum_blocks(pack_a, "tensor"), sum_blocks(pack_b, ROW)
     grad_mix = list(attend_back(mixed, groups, grad_heads, att_wide, logsum, heads))
-    (grad_mix[0], mid_sums) = tie(grad_mix[0], mid_sums)
+    (grad_mix[0], pack_a, pack_b, down_sum) = lax.optimization_barrier(
+        (grad_mix[0], pack_a, pack_b, down_sum)
+    )
     for step in range(1, halves):
         for place in range(groups):
             more = send_xor(grad_mix[step * groups + place], "sr", step)
             grad_mix[place] = (grad_mix[place].astype(f32) + more.astype(f32)).astype(bf16)
     grad_proj = give_back(grad_mix[:groups], HEAD_GROUP)
     grad_proj = [by_split(grad_proj, split) for split in range(splits)]
-    mid_sums = [orders[place % 2][1](sums) for place, sums in enumerate(mid_sums)]
+    pack_a, pack_b = sum_blocks(pack_a, ROW), sum_blocks(pack_b, "tensor")
     text_sum = plane_sum(text_terms, bf16)
-    (grad_proj, mid_sums, text_sum) = lax.optimization_barrier((grad_proj, mid_sums, text_sum))
+    (grad_proj, pack_a, pack_b, text_sum) = lax.optimization_barrier(
+        (grad_proj, pack_a, pack_b, text_sum)
+    )
     grad_hidden_one = sum(
         dot(grad_proj[split][place], qkv_full[place][split], NT)
         for place in range(ranks)
@@ -691,7 +698,6 @@
         grad_hidden_one * (1.0 + scale_one), normed_one, inverse_one
     )
     grad_latents = grad_latents.astype(bf16).reshape(latents.shape)
-    grad_latents, up_sum = tie(grad_latents, up_sum)
     grad_latents = in_order(give_back(list(grad_latents), "lat"), "lat")
 
     time_terms = jnp.stack(
@@ -704,21 +710,25 @@
             grad_gate_two,
         )
     )
-    time_turn = lax.dot_general(
-        time_terms, turn.astype(f32), NN, precision=lax.Precision.HIGHEST
-    )
-    table_terms = jnp.pad(time_turn.T, ((0, 0), (3 * edge, piece_width - 3 * edge - 6)))
+    table_terms = jnp.pad(time_terms.T, ((0, 0), (3 * edge, piece_width - 3 * edge - 6)))
+    one_grads = []
+    for place in range(ranks):
+        rights = from_own([grad_proj[split][place] for split in range(splits)])
+        grads = [dot(hidden_one, right, TN) for right in rights]
+        if place == 0:
+            grads = [grad + table_terms for grad in grads]
+        one_grads.append([grad.astype(bf16) for grad in grads])
+    pack_one, up_sum = tie(pack_grid(one_grads), up_sum)
+    one_sum = scatter_all(pack_one)
     one_sums = [
-        kept_sums(
-            hidden_one,
-            [grad_proj[split][place] for split in range(splits)],
-            table_terms if place == 0 else None,
-        )
-        for place in range(ranks)
+        one_sum[:, place * piece_width : (place + 1) * piece_width] for place in range(ranks)
     ]
-    one_sums = [orders[place % 2][0](sums) for place, sums in enumerate(one_sums)]
-    one_sums = [sum_lat(orders[place % 2][1](sums)) for place, sums in enumerate(one_sums)]
-    key_sum, val_sum, cq_sum, co_sum, out_sum = (sum_lat(sums)[:, :part] for sums in mid_sums)
+    pack_a, pack_b = sum_blocks(pack_a, "lat", f32), sum_blocks(pack_b, "lat", f32)
+    key_sum, val_sum, cq_sum, co_sum, out_sum = (
+        pack[:, place * wide : place * wide + part]
+        for pack, count in ((pack_a, 3), (pack_b, 2))
+        for place in range(count)
+    )
     grad_time = over_latents(plane_sum(time_terms, f32)).reshape(-1, 6 * width)
     grad_text = over_latents(text_sum.astype(bf16)).astype(f32)
     grad_qkv = jnp.stack(

time: 971 us -> 937 us (0.965)
  waiting for transfers between devices: 373 us -> 334 us
  Pallas kernels: 159 us -> 179 us
  starting transfers between devices: 149 us -> 130 us
    ppermute x105 -> x65, waiting for transfers between devices: 270 us -> 244 us  [send_xor(): lax.ppermute(piece, axes, [(rank, rank ^ step) for rank in range(size)])]
    reduce_scatter x2 -> x3, waiting for transfers between devices: 67.5 us -> 45.5 us  [scatter_all(): lax.psum_scatter(pack, EVERY, scatter_dimension=0, tiled=True).astype(f32)]
    pallas_call x6 -> x9, Pallas kernels: 37.7 us -> 58.1 us  [lay(): pl.pallas_call(partial(assemble_kernel, plan, len(sources)), in_specs=[an...]
    ppermute x105 -> x65, starting transfers between devices: 149 us -> 129 us  [send_xor(): lax.ppermute(piece, axes, [(rank, rank ^ step) for rank in range(size)])]
    dot_general x74 -> x60, matrix products: 188 us -> 196 us  [dot(): return lax.dot_general(left, right, dims, preferred_element_type=f32)]
  transfers between devices with their start and end apart: 109 -> 70, of which waited for: 48 -> 29; matrix products, arithmetic and copies ran while one was open for 21% -> 22% of each run, Pallas kernels for 16% -> 18%
where the time goes in v3:
time: 937 us; the launch traced here: 933 us
  waiting for transfers between devices  334 us (36%)
  matrix products  196 us (21%)
  Pallas kernels  179 us (19%)
  starting transfers between devices  130 us (14%)
  other arithmetic  44.8 us (5%)
  local copies, waits for them, and re-layouts  33.5 us (4%)
  between operations  16.1 us (2%)
    ppermute x65, waiting for transfers between devices, send_xor(): lax.ppermute(piece, axes, [(rank, rank ^ step) for rank in range(size)])  244 us
    dot_general x60, matrix products, dot(): return lax.dot_general(left, right, dims, preferred_element_type=f32)  196 us
    ppermute x65, starting transfers between devices, send_xor(): lax.ppermute(piece, axes, [(rank, rank ^ step) for rank in range(size)])  129 us
    pallas_call x9, Pallas kernels, lay(): pl.pallas_call(partial(assemble_kernel, plan, len(sources)), in_specs=[an...  58.1 us
    pallas_call x1, Pallas kernels, attend_back(): pl.pallas_call(partial(attend_back_kernel, heads, min(512, total), len(pi...  57.6 us
    reduce_scatter x3, waiting for transfers between devices, scatter_all(): lax.psum_scatter(pack, EVERY, scatter_dimension=0, tiled=True).astype(f32)  45.5 us
    all_gather x2, waiting for transfers between devices, gather_all(): return lax.all_gather(shard, EVERY, axis=shard.ndim - 2, tiled=True)  44.5 us
    pallas_call x1, Pallas kernels, attend(): pl.pallas_call(partial(attend_kernel, heads, len(pieces), own), grid=(row...  32.7 us
  transfers between devices with their start and end apart: 70, of which 29 were waited for; matrix products, arithmetic and copies ran while one was open for 22% of the time, Pallas kernels for 18%

profile of v3, /device:TPU:0, one launch (start us, length us, event | category | flops | bytes accessed | tf_op | source)
XLA Modules:
  0.0 933.4 jit_solution(17922304662540860512)
XLA Ops:
  26.2 7.9 collective-permute-done.17
  40.3 8.7 collective-permute-done.19.refs_1_
  55.5 9.8 %collective-permute-start.13 = (bf16[128,1152]{1,0:T(8,128)(2,1)S(1)}, bf16[128,1152]{1,0:T(8,128)(2,1)S(1)}, u32[]{:S(2)}, u32[]{:S(2)}) collective-permute-start(bf16[128,1152]{1,0:T(8,128)(2,1)S(1)} %get-tuple-element.218), channel_id=1, source_target_pairs={{0,4},{4,0},{8,12},{12,8},{1,5},{5,1},{9,13},{13,9},{2,6},{6,2},{1... | collective-permute-start | bytes 884744 | tf_op jit(solution)/shard_map/ppermute | solution.py:50
  68.0 11.5 %collective-permute-done.13 = bf16[128,1152]{1,0:T(8,128)(2,1)S(1)} collective-permute-done((bf16[128,1152]{1,0:T(8,128)(2,1)S(1)}, bf16[128,1152]{1,0:T(8,128)(2,1)S(1)}, u32[]{:S(2)}, u32[]{:S(2)}) %collective-permute-start.13) | collective-permute-done | bytes 294944 | tf_op jit(solution)/shard_map/ppermute | solution.py:50
  81.5 14.2 %collective-permute-done.15 = bf16[128,1152]{1,0:T(8,128)(2,1)S(1)} collective-permute-done((bf16[128,1152]{1,0:T(8,128)(2,1)}, bf16[128,1152]{1,0:T(8,128)(2,1)S(1)}, u32[]{:S(2)}, u32[]{:S(2)}) %collective-permute-start.15) | collective-permute-done | bytes 294944 | tf_op jit(solution)/shard_map/ppermute | solution.py:50
  131.4 31.9 %collective-permute-done.23.refs_1_ = bf16[512,896]{1,0:T(8,128)(2,1)S(1)} collective-permute-done((bf16[512,896]{1,0:T(8,128)(2,1)S(1)}, bf16[512,896]{1,0:T(8,128)(2,1)S(1)}, u32[]{:S(2)}, u32[]{:S(2)}) %collective-permute-start.23) | collective-permute-done | bytes 917536 | tf_op jit(solution)/shard_map/ppermute | solution.py:50
  163.4 20.4 %collective-permute-done.25.refs_3_ = bf16[512,896]{1,0:T(8,128)(2,1)S(1)} collective-permute-done((bf16[512,896]{1,0:T(8,128)(2,1)S(1)}, bf16[512,896]{1,0:T(8,128)(2,1)S(1)}, u32[]{:S(2)}, u32[]{:S(2)}) %collective-permute-start.25) | collective-permute-done | bytes 917536 | tf_op jit(solution)/shard_map/ppermute | solution.py:50
  185.0 32.7 %shard_map.214 = (bf16[512,288]{1,0:T(8,128)(2,1)}, bf16[512,288]{1,0:T(8,128)(2,1)}, bf16[512,288]{1,0:T(8,128)(2,1)}, bf16[512,288]{1,0:T(8,128)(2,1)}, f32[4,2048,72]{2,1,0:T(8,128)}, /*index=5*/f32[8,2048]{1,0:T(8,128)}) custom-call(bf16[512,896]{1,0:T(8,128)(2,1)} %get-tuple-element.204.refs_0_, bf16[512,896]{1,0:T(8,128)(2,1)} %copy-done.115, ...), custom_call_target="tpu_custom_call" | custom-call | flops 17179869184 | bytes 7340032 | tf_op jit(solution)/shard_map/pallas_call | solution.py:160
  226.2 13.2 %collective-permute-done.26 = bf16[512,288]{1,0:T(8,128)(2,1)} collective-permute-done((bf16[512,288]{1,0:T(8,128)(2,1)}, bf16[512,288]{1,0:T(8,128)(2,1)}, u32[]{:S(2)}, u32[]{:S(2)}) %collective-permute-start.26) | collective-permute-done | bytes 294944 | tf_op jit(solution)/shard_map/ppermute | solution.py:50
  242.7 12.2 %collective-permute-done.27 = bf16[512,288]{1,0:T(8,128)(2,1)} collective-permute-done((bf16[512,288]{1,0:T(8,128)(2,1)}, bf16[512,288]{1,0:T(8,128)(2,1)}, u32[]{:S(2)}, u32[]{:S(2)}) %collective-permute-start.27) | collective-permute-done | bytes 294944 | tf_op jit(solution)/shard_map/ppermute | solution.py:50
  257.1 10.8 %shard_map.215 = (bf16[1152,640]{1,0:T(8,128)(2,1)}, bf16[1152,640]{1,0:T(8,128)(2,1)}, bf16[1152,640]{1,0:T(8,128)(2,1)}, bf16[1152,640]{1,0:T(8,128)(2,1)}, bf...) custom-call(bf16[2304,3200]{1,0:T(8,128)(2,1)} %all-gather.3.cloned., ...), custom_call_target="tpu_custom_call" | custom-call | tf_op jit(solution)/shard_map/pallas_call | solution.py:407
  282.6 11.8 %shard_map.216 = (bf16[512,640]{1,0:T(8,128)(2,1)}, bf16[512,640]{1,0:T(8,128)(2,1)}) custom-call(bf16[512,640]{1,0:T(8,128)(2,1)} %convolution_convert_fusion.25.refs_0_, bf16[512,640]{1,0:T(8,128)(2,1)} %convolution_convert_fusion.24.refs_1_, bf16[120,640]{1,0:T(8,128)(2,1)} %convolution_convert_fusion.29.refs_2_, ...), custom_call_target="tpu_custom_call" | custom-call | tf_op jit(solution)/shard_map/pallas_call | solution.py:318
  300.3 44.5 %all-gather.5.cloned.1.call-done = bf16[2,2304,2304]{2,1,0:T(8,128)(2,1)} async-done(((bf16[2,72,2304]{2,1,0:T(8,128)(2,1)}), bf16[2,2304,2304]{2,1,0:T(8,128)(2,1)}) %all-gather.5.cloned.1.call-update) | async-done | bytes 21233680 | tf_op jit(solution)/shard_map/all_gather | solution.py:462
  372.4 8.1 shard_map.221
  408.6 8.5 multiply_reduce_fusion
  417.1 8.4 fusion.21
  425.4 10.2 %fusion.68 = (f32[1152]{0:T(1024)}, bf16[512,1152]{1,0:T(8,128)(2,1)}, f32[512,1152]{1,0:T(8,128)S(1)}) fusion(bf16[128,1152]{1,0:T(8,128)(2,1)} %collective-permute-done.12, bf16[128,1152]{1,0:T(8,128)(2,1)} %collective-permute-done.11, bf16[128,1152]{1,0:T(8,128)(2,1)} %collective-permute-done.10, bf16[128,1152]{1,0:T(8,128)(2,1)S(1)} %copy-done.84, ...), kind=kOutput, calls=%fused_computation.113 | convolution fusion | flops 2741500928 | bytes 21845504 | tf_op jit(solution)/shard_map/dot_general | solution.py:33
  440.1 18.7 %shard_map.217 = (bf16[512,640]{1,0:T(8,128)(2,1)}, bf16[512,640]{1,0:T(8,128)(2,1)}, bf16[120,640]{1,0:T(8,128)(2,1)}, bf16[120,640]{1,0:T(8,128)(2,1)}, bf16[1...) custom-call(bf16[512,640]{1,0:T(8,128)(2,1)} %convolution_convert_fusion.25.refs_0_, ...), custom_call_target="tpu_custom_call" | custom-call | tf_op jit(solution)/shard_map/pallas_call | solution.py:374
  469.2 8.5 shard_map.223
  539.9 14.1 %collective-permute-done.32 = bf16[128,1152]{1,0:T(8,128)(2,1)S(1)} collective-permute-done((bf16[128,1152]{1,0:T(8,128)(2,1)S(1)}, bf16[128,1152]{1,0:T(8,128)(2,1)S(1)}, u32[]{:S(2)}, u32[]{:S(2)}) %collective-permute-start.32) | collective-permute-done | bytes 294944 | tf_op jit(solution)/shard_map/ppermute | solution.py:50
  577.7 14.2 %collective-permute-done.35.refs_6_ = bf16[512,288]{1,0:T(8,128)(2,1)S(1)} collective-permute-done((bf16[512,288]{1,0:T(8,128)(2,1)S(1)}, bf16[512,288]{1,0:T(8,128)(2,1)S(1)}, u32[]{:S(2)}, u32[]{:S(2)}) %collective-permute-start.35) | collective-permute-done | bytes 294944 | tf_op jit(solution)/shard_map/ppermute | solution.py:50
  593.2 57.6 %shard_map.220 = (bf16[512,896]{1,0:T(8,128)(2,1)}, bf16[512,896]{1,0:T(8,128)(2,1)}, bf16[512,896]{1,0:T(8,128)(2,1)}, bf16[512,896]{1,0:T(8,128)(2,1)}) custom-call(bf16[512,896]{1,0:T(8,128)(2,1)} %get-tuple-element.204.refs_0_, bf16[512,896]{1,0:T(8,128)(2,1)} %copy-done.115, bf16[512,896]{1,0:T(8,128)(2,1)} %copy-done.117, ...), custom_call_target="tpu_custom_call" | custom-call | flops 42949672960 | bytes 14680064 | tf_op jit(solution)/shard_map/pallas_call | solution.py:264
  675.4 19.0 %collective-permute-done.41 = bf16[512,896]{1,0:T(8,128)(2,1)} collective-permute-done((bf16[512,896]{1,0:T(8,128)(2,1)}, bf16[512,896]{1,0:T(8,128)(2,1)}, u32[]{:S(2)}, u32[]{:S(2)}) %collective-permute-start.41) | collective-permute-done | bytes 917536 | tf_op jit(solution)/shard_map/ppermute | solution.py:50
  697.3 12.5 %reduce-scatter.6.cloned.1.call-done = bf16[72,2304]{1,0:T(8,128)(2,1)} async-done(((bf16[2304,2304]{1,0:T(8,128)(2,1)}), bf16[72,2304]{1,0:T(8,128)(2,1)}) %reduce-scatter.6.cloned.1.call-update) | async-done | bytes 331792 | tf_op jit(solution)/shard_map/reduce_scatter | solution.py:466
  729.5 9.5 %fusion.65 = (f32[1152]{0:T(1024)}, f32[512]{0:T(512)}, f32[512]{0:T(512)}, f32[1152]{0:T(1024)}, f32[512,1152]{1,0:T(8,128)}) fusion(f32[512]{0:T(512)S(1)} %copy-done.103, f32[512]{0:T(512)S(1)} %copy-done.89, bf16[128,1152]{1,0:T(8,128)(2,1)S(1)} %copy-done.22, bf16[128,1152]{1,0:T(8,128)(2,1)S(1)} %copy-done.19, bf16[128,1152]{1,0:T(8,128)(2,1)S(1)} %copy-done.16, ...), kind=kOutput, calls=%fused_computation.110 | convolution fusion | flops 2429629440 | bytes 13625344 | tf_op jit(solution)/shard_map/dot_general | solution.py:33
  778.4 9.1 collective-permute-done.56
  787.5 11.6 %collective-permute-start.59 = (bf16[72,1280]{1,0:T(8,128)(2,1)S(1)}, bf16[72,1280]{1,0:T(8,128)(2,1)S(1)}, u32[]{:S(2)}, u32[]{:S(2)}) collective-permute-start(bf16[72,1280]{1,0:T(8,128)(2,1)S(1)} %get-tuple-element.232), channel_id=1, source_target_pairs={{0,4},{4,0},{8,12},{12,8},{1,5},{5,1},{9,13},{13,9},{2,6},{6,2},{1... | collective-permute-start | bytes 552968 | tf_op jit(solution)/shard_map/ppermute | solution.py:50
  818.0 11.0 %collective-permute-start.52 = (bf16[120,1152]{1,0:T(8,128)(2,1)S(1)}, bf16[120,1152]{1,0:T(8,128)(2,1)S(1)}, u32[]{:S(2)}, u32[]{:S(2)}) collective-permute-start(bf16[120,1152]{1,0:T(8,128)(2,1)S(1)} %copy-done.48), channel_id=1, source_target_pairs={{0,4},{4,0},{8,12},{12,8},{1,5},{5,1},{9,13},{13,9},{2,6},{6,2},{1... | collective-permute-start | bytes 829448 | tf_op jit(solution)/shard_map/ppermute | solution.py:50
  829.0 18.9 %collective-permute-done.63 = bf16[72,1920]{1,0:T(8,128)(2,1)S(1)} collective-permute-done((bf16[72,1920]{1,0:T(8,128)(2,1)S(1)}, bf16[72,1920]{1,0:T(8,128)(2,1)S(1)}, u32[]{:S(2)}, u32[]{:S(2)}) %collective-permute-start.63) | collective-permute-done | bytes 276512 | tf_op jit(solution)/shard_map/ppermute | solution.py:50
  852.4 18.2 %collective-permute-start.48 = (bf16[128,1152]{1,0:T(8,128)(2,1)S(1)}, bf16[128,1152]{1,0:T(8,128)(2,1)S(1)}, u32[]{:S(2)}, u32[]{:S(2)}) collective-permute-start(bf16[128,1152]{1,0:T(8,128)(2,1)S(1)} %get-tuple-element.208), channel_id=1, source_target_pairs={{0,8},{4,12},{8,0},{12,4},{1,9},{5,13},{9,1},{13,5},{2,10},{6,14},... | collective-permute-start | bytes 884744 | tf_op jit(solution)/shard_map/ppermute | solution.py:50
  874.2 13.2 %collective-permute-done.48 = bf16[128,1152]{1,0:T(8,128)(2,1)S(1)} collective-permute-done((bf16[128,1152]{1,0:T(8,128)(2,1)S(1)}, bf16[128,1152]{1,0:T(8,128)(2,1)S(1)}, u32[]{:S(2)}, u32[]{:S(2)}) %collective-permute-start.48) | collective-permute-done | bytes 294944 | tf_op jit(solution)/shard_map/ppermute | solution.py:50
  889.1 32.9 %reduce-scatter.8.cloned.1.call-done = bf16[72,1792]{1,0:T(8,128)(2,1)} async-done(((bf16[2304,1792]{1,0:T(8,128)(2,1)}), bf16[72,1792]{1,0:T(8,128)(2,1)}) %reduce-scatter.8.cloned.1.call-update) | async-done | bytes 258064 | tf_op jit(solution)/shard_map/reduce_scatter | solution.py:466
  (554 shorter events, 383.7 us)
Async XLA Ops:
  7.2 249.9 %all-gather.3.cloned.1.call-start = ((), (), s32[]{:S(2)}) async-start(), calls=%async_computation.3 | async-start | bytes 15206400 | tf_op jit(solution)/shard_map/all_gather | solution.py:462
  35.9 308.9 %all-gather.5.cloned.1.call-start = ((), (), s32[]{:S(2)}) async-start(), calls=%async_computation.4 | async-start | bytes 21897216 | tf_op jit(solution)/shard_map/all_gather | solution.py:462
  36.9 622.5 %reduce-scatter.4.cloned.1.call-start = ((), (), s32[]{:S(2)}) async-start(), calls=%async_computation.5 | async-start | bytes 10948608 | tf_op jit(solution)/shard_map/reduce_scatter | solution.py:466
  51.9 45.2 %collective-permute-start.21 = (bf16[576,896]{1,0:T(8,128)(2,1)}, bf16[576,896]{1,0:T(8,128)(2,1)}, u32[]{:S(2)}, u32[]{:S(2)}) collective-permute-start(bf16[576,896]{1,0:T(8,128)(2,1)} %shard_map.212.refs_0_), channel_id=1, source_target_pairs={{0,1},{1,0},{2,3},{3,2},{4,5},{5,4},{6,7},{7,6},{8,9},{9,8},{10,11... | collective-permute-start | bytes 3096584 | tf_op jit(solution)/shard_map/ppermute | solution.py:50
  123.8 39.5 %collective-permute-start.23 = (bf16[512,896]{1,0:T(8,128)(2,1)S(1)}, bf16[512,896]{1,0:T(8,128)(2,1)S(1)}, u32[]{:S(2)}, u32[]{:S(2)}) collective-permute-start(bf16[512,896]{1,0:T(8,128)(2,1)S(1)} %get-tuple-element.202), channel_id=1, source_target_pairs={{0,1},{1,0},{2,3},{3,2},{4,5},{5,4},{6,7},{7,6},{8,9},{9,8},{10,11... | collective-permute-start | bytes 2752520 | tf_op jit(solution)/shard_map/ppermute | solution.py:50
  124.1 59.6 %collective-permute-start.25 = (bf16[512,896]{1,0:T(8,128)(2,1)S(1)}, bf16[512,896]{1,0:T(8,128)(2,1)S(1)}, u32[]{:S(2)}, u32[]{:S(2)}) collective-permute-start(bf16[512,896]{1,0:T(8,128)(2,1)S(1)} %get-tuple-element.201), channel_id=1, source_target_pairs={{0,3},{1,2},{2,1},{3,0},{4,7},{5,6},{6,5},{7,4},{8,11},{9,10},{10,... | collective-permute-start | bytes 2752520 | tf_op jit(solution)/shard_map/ppermute | solution.py:50
  130.1 53.6 %collective-permute-start.24 = (bf16[512,896]{1,0:T(8,128)(2,1)S(1)}, bf16[512,896]{1,0:T(8,128)(2,1)S(1)}, u32[]{:S(2)}, u32[]{:S(2)}) collective-permute-start(bf16[512,896]{1,0:T(8,128)(2,1)S(1)} %get-tuple-element.203), channel_id=1, source_target_pairs={{0,2},{1,3},{2,0},{3,1},{4,6},{5,7},{6,4},{7,5},{8,10},{9,11},{10,... | collective-permute-start | bytes 2752520 | tf_op jit(solution)/shard_map/ppermute | solution.py:50
  218.2 36.7 %collective-permute-start.27 = (bf16[512,288]{1,0:T(8,128)(2,1)}, bf16[512,288]{1,0:T(8,128)(2,1)}, u32[]{:S(2)}, u32[]{:S(2)}) collective-permute-start(bf16[512,288]{1,0:T(8,128)(2,1)} %get-tuple-element.73), channel_id=1, source_target_pairs={{0,1},{1,0},{2,3},{3,2},{4,5},{5,4},{6,7},{7,6},{8,9},{9,8},{10,11... | collective-permute-start | bytes 884744 | tf_op jit(solution)/shard_map/ppermute | solution.py:50
  219.8 36.3 %collective-permute-start.28 = (bf16[512,288]{1,0:T(8,128)(2,1)}, bf16[512,288]{1,0:T(8,128)(2,1)S(1)}, u32[]{:S(2)}, u32[]{:S(2)}) collective-permute-start(bf16[512,288]{1,0:T(8,128)(2,1)} %get-tuple-element.74), channel_id=1, source_target_pairs={{0,2},{1,3},{2,0},{3,1},{4,6},{5,7},{6,4},{7,5},{8,10},{9,11},{10,... | collective-permute-start | bytes 884744 | tf_op jit(solution)/shard_map/ppermute | solution.py:50
  222.3 136.1 %collective-permute-start.10 = (bf16[128,1152]{1,0:T(8,128)(2,1)}, bf16[128,1152]{1,0:T(8,128)(2,1)}, u32[]{:S(2)}, u32[]{:S(2)}) collective-permute-start(bf16[128,1152]{1,0:T(8,128)(2,1)} %get-tuple-element.216), channel_id=1, source_target_pairs={{0,4},{4,0},{8,12},{12,8},{1,5},{5,1},{9,13},{13,9},{2,6},{6,2},{1... | collective-permute-start | bytes 884744 | tf_op jit(solution)/shard_map/ppermute | solution.py:50
  223.8 134.7 %collective-permute-start.11 = (bf16[128,1152]{1,0:T(8,128)(2,1)}, bf16[128,1152]{1,0:T(8,128)(2,1)}, u32[]{:S(2)}, u32[]{:S(2)}) collective-permute-start(bf16[128,1152]{1,0:T(8,128)(2,1)} %get-tuple-element.215), channel_id=1, source_target_pairs={{0,8},{4,12},{8,0},{12,4},{1,9},{5,13},{9,1},{13,5},{2,10},{6,14},... | collective-permute-start | bytes 884744 | tf_op jit(solution)/shard_map/ppermute | solution.py:50
  239.4 119.1 %collective-permute-start.12 = (bf16[128,1152]{1,0:T(8,128)(2,1)}, bf16[128,1152]{1,0:T(8,128)(2,1)}, u32[]{:S(2)}, u32[]{:S(2)}) collective-permute-start(bf16[128,1152]{1,0:T(8,128)(2,1)} %get-tuple-element.214), channel_id=1, source_target_pairs={{0,12},{4,8},{8,4},{12,0},{1,13},{5,9},{9,5},{13,1},{2,14},{6,10},... | collective-permute-start | bytes 884744 | tf_op jit(solution)/shard_map/ppermute | solution.py:50
  380.5 329.3 %reduce-scatter.6.cloned.1.call-start = ((), (), s32[]{:S(2)}) async-start(), calls=%async_computation.6 | async-start | bytes 10948608 | tf_op jit(solution)/shard_map/reduce_scatter | solution.py:466
  497.3 424.7 %reduce-scatter.8.cloned.1.call-start = ((), (), s32[]{:S(2)}) async-start(), calls=%async_computation.7 | async-start | bytes 8515584 | tf_op jit(solution)/shard_map/reduce_scatter | solution.py:466
  507.3 49.7 %collective-permute-start.30 = (bf16[1152,1280]{1,0:T(8,128)(2,1)}, bf16[1152,1280]{1,0:T(8,128)(2,1)S(1)}, u32[]{:S(2)}, u32[]{:S(2)}) collective-permute-start(bf16[1152,1280]{1,0:T(8,128)(2,1)} %get-tuple-element.98), channel_id=1, source_target_pairs={{0,16},{16,0},{1,17},{17,1},{2,18},{18,2},{3,19},{19,3},{4,20},{20... | collective-permute-start | bytes 8847368 | tf_op jit(solution)/shard_map/ppermute | solution.py:50
  522.7 37.1 %collective-permute-start.29 = (bf16[1152,1920]{1,0:T(8,128)(2,1)}, bf16[1152,1920]{1,0:T(8,128)(2,1)S(1)}, u32[]{:S(2)}, u32[]{:S(2)}) collective-permute-start(bf16[1152,1920]{1,0:T(8,128)(2,1)} %get-tuple-element.96), channel_id=1, source_target_pairs={{0,16},{16,0},{1,17},{17,1},{2,18},{18,2},{3,19},{19,3},{4,20},{20... | collective-permute-start | bytes 13271048 | tf_op jit(solution)/shard_map/ppermute | solution.py:50
  538.4 116.9 %collective-permute-start.44 = (bf16[120,1152]{1,0:T(8,128)(2,1)S(1)}, bf16[120,1152]{1,0:T(8,128)(2,1)S(1)}, u32[]{:S(2)}, u32[]{:S(2)}) collective-permute-start(bf16[120,1152]{1,0:T(8,128)(2,1)S(1)} %fusion.56), channel_id=1, source_target_pairs={{0,1},{1,0},{2,3},{3,2},{4,5},{5,4},{6,7},{7,6},{8,9},{9,8},{10,11... | collective-permute-start | bytes 829448 | tf_op jit(solution)/shard_map/ppermute | solution.py:50
  554.0 109.3 %collective-permute-start.45 = (bf16[120,1152]{1,0:T(8,128)(2,1)S(1)}, bf16[120,1152]{1,0:T(8,128)(2,1)}, u32[]{:S(2)}, u32[]{:S(2)}) collective-permute-start(bf16[120,1152]{1,0:T(8,128)(2,1)S(1)} %fusion.56), channel_id=1, source_target_pairs={{0,2},{1,3},{2,0},{3,1},{4,6},{5,7},{6,4},{7,5},{8,10},{9,11},{10,... | collective-permute-start | bytes 829448 | tf_op jit(solution)/shard_map/ppermute | solution.py:50
  559.8 32.1 %collective-permute-start.35 = (bf16[512,288]{1,0:T(8,128)(2,1)S(1)}, bf16[512,288]{1,0:T(8,128)(2,1)S(1)}, u32[]{:S(2)}, u32[]{:S(2)}) collective-permute-start(bf16[512,288]{1,0:T(8,128)(2,1)S(1)} %get-tuple-element.237), channel_id=1, source_target_pairs={{0,2},{1,3},{2,0},{3,1},{4,6},{5,7},{6,4},{7,5},{8,10},{9,11},{10,... | collective-permute-start | bytes 884744 | tf_op jit(solution)/shard_map/ppermute | solution.py:50
  567.8 96.3 %collective-permute-start.46 = (bf16[120,1152]{1,0:T(8,128)(2,1)S(1)}, bf16[120,1152]{1,0:T(8,128)(2,1)}, u32[]{:S(2)}, u32[]{:S(2)}) collective-permute-start(bf16[120,1152]{1,0:T(8,128)(2,1)S(1)} %fusion.56), channel_id=1, source_target_pairs={{0,3},{1,2},{2,1},{3,0},{4,7},{5,6},{6,5},{7,4},{8,11},{9,10},{10,... | collective-permute-start | bytes 829448 | tf_op jit(solution)/shard_map/ppermute | solution.py:50
  576.2 74.6 %collective-permute-start.39 = (bf16[576,1280]{1,0:T(8,128)(2,1)}, bf16[576,1280]{1,0:T(8,128)(2,1)}, u32[]{:S(2)}, u32[]{:S(2)}) collective-permute-start(bf16[576,1280]{1,0:T(8,128)(2,1)} %slice.166), channel_id=1, source_target_pairs={{0,2},{2,0},{1,3},{3,1},{4,6},{6,4},{5,7},{7,5},{8,10},{10,8},{9,1... | collective-permute-start | bytes 4423688 | tf_op jit(solution)/shard_map/ppermute | solution.py:50
  591.8 64.2 %collective-permute-start.38 = (bf16[576,1920]{1,0:T(8,128)(2,1)}, bf16[576,1920]{1,0:T(8,128)(2,1)}, u32[]{:S(2)}, u32[]{:S(2)}) collective-permute-start(bf16[576,1920]{1,0:T(8,128)(2,1)} %slice.164), channel_id=1, source_target_pairs={{0,1},{1,0},{2,3},{3,2},{4,5},{5,4},{6,7},{7,6},{8,9},{9,8},{10,11... | collective-permute-start | bytes 6635528 | tf_op jit(solution)/shard_map/ppermute | solution.py:50
  655.3 39.1 %collective-permute-start.41 = (bf16[512,896]{1,0:T(8,128)(2,1)}, bf16[512,896]{1,0:T(8,128)(2,1)}, u32[]{:S(2)}, u32[]{:S(2)}) collective-permute-start(bf16[512,896]{1,0:T(8,128)(2,1)} %get-tuple-element.109), channel_id=1, source_target_pairs={{0,1},{1,0},{2,3},{3,2},{4,5},{5,4},{6,7},{7,6},{8,9},{9,8},{10,11... | collective-permute-start | bytes 2752520 | tf_op jit(solution)/shard_map/ppermute | solution.py:50
  656.0 55.8 %collective-permute-start.37 = (bf16[512,896]{1,0:T(8,128)(2,1)}, bf16[512,896]{1,0:T(8,128)(2,1)}, u32[]{:S(2)}, u32[]{:S(2)}) collective-permute-start(bf16[512,896]{1,0:T(8,128)(2,1)} %get-tuple-element.103), channel_id=1, source_target_pairs={{0,2},{1,3},{2,0},{3,1},{4,6},{5,7},{6,4},{7,5},{8,10},{9,11},{10,... | collective-permute-start | bytes 2752520 | tf_op jit(solution)/shard_map/ppermute | solution.py:50
  663.3 51.1 %collective-permute-start.43 = (bf16[288,1280]{1,0:T(8,128)(2,1)}, bf16[288,1280]{1,0:T(8,128)(2,1)}, u32[]{:S(2)}, u32[]{:S(2)}) collective-permute-start(bf16[288,1280]{1,0:T(8,128)(2,1)} %slice.170), channel_id=1, source_target_pairs={{0,1},{1,0},{2,3},{3,2},{4,5},{5,4},{6,7},{7,6},{8,9},{9,8},{10,11... | collective-permute-start | bytes 2211848 | tf_op jit(solution)/shard_map/ppermute | solution.py:50
  667.0 52.2 %collective-permute-start.42 = (bf16[288,1920]{1,0:T(8,128)(2,1)}, bf16[288,1920]{1,0:T(8,128)(2,1)S(1)}, u32[]{:S(2)}, u32[]{:S(2)}) collective-permute-start(bf16[288,1920]{1,0:T(8,128)(2,1)} %slice.168), channel_id=1, source_target_pairs={{0,2},{2,0},{1,3},{3,1},{4,6},{6,4},{5,7},{7,5},{8,10},{10,8},{9,1... | collective-permute-start | bytes 3317768 | tf_op jit(solution)/shard_map/ppermute | solution.py:50
  770.3 102.1 %collective-permute-start.50 = (bf16[120,1152]{1,0:T(8,128)(2,1)S(1)}, bf16[120,1152]{1,0:T(8,128)(2,1)S(1)}, u32[]{:S(2)}, u32[]{:S(2)}) collective-permute-start(bf16[120,1152]{1,0:T(8,128)(2,1)S(1)} %copy-done.48), channel_id=1, source_target_pairs={{0,12},{4,8},{8,4},{12,0},{1,13},{5,9},{9,5},{13,1},{2,14},{6,10},... | collective-permute-start | bytes 829448 | tf_op jit(solution)/shard_map/ppermute | solution.py:50
  773.7 98.8 %collective-permute-start.51 = (bf16[120,1152]{1,0:T(8,128)(2,1)S(1)}, bf16[120,1152]{1,0:T(8,128)(2,1)S(1)}, u32[]{:S(2)}, u32[]{:S(2)}) collective-permute-start(bf16[120,1152]{1,0:T(8,128)(2,1)S(1)} %copy-done.48), channel_id=1, source_target_pairs={{0,8},{4,12},{8,0},{12,4},{1,9},{5,13},{9,1},{13,5},{2,10},{6,14},... | collective-permute-start | bytes 829448 | tf_op jit(solution)/shard_map/ppermute | solution.py:50
  810.6 37.4 %collective-permute-start.63 = (bf16[72,1920]{1,0:T(8,128)(2,1)S(1)}, bf16[72,1920]{1,0:T(8,128)(2,1)S(1)}, u32[]{:S(2)}, u32[]{:S(2)}) collective-permute-start(bf16[72,1920]{1,0:T(8,128)(2,1)S(1)} %get-tuple-element.223), channel_id=1, source_target_pairs={{0,8},{4,12},{8,0},{12,4},{1,9},{5,13},{9,1},{13,5},{2,10},{6,14},... | collective-permute-start | bytes 829448 | tf_op jit(solution)/shard_map/ppermute | solution.py:50
  814.8 37.6 %collective-permute-start.64 = (bf16[72,1920]{1,0:T(8,128)(2,1)S(1)}, bf16[72,1920]{1,0:T(8,128)(2,1)S(1)}, u32[]{:S(2)}, u32[]{:S(2)}) collective-permute-start(bf16[72,1920]{1,0:T(8,128)(2,1)S(1)} %get-tuple-element.222), channel_id=1, source_target_pairs={{0,12},{4,8},{8,4},{12,0},{1,13},{5,9},{9,5},{13,1},{2,14},{6,10},... | collective-permute-start | bytes 829448 | tf_op jit(solution)/shard_map/ppermute | solution.py:50
  818.0 54.4 %collective-permute-start.52 = (bf16[120,1152]{1,0:T(8,128)(2,1)S(1)}, bf16[120,1152]{1,0:T(8,128)(2,1)S(1)}, u32[]{:S(2)}, u32[]{:S(2)}) collective-permute-start(bf16[120,1152]{1,0:T(8,128)(2,1)S(1)} %copy-done.48), channel_id=1, source_target_pairs={{0,4},{4,0},{8,12},{12,8},{1,5},{5,1},{9,13},{13,9},{2,6},{6,2},{1... | collective-permute-start | bytes 829448 | tf_op jit(solution)/shard_map/ppermute | solution.py:50
  852.4 34.9 %collective-permute-start.48 = (bf16[128,1152]{1,0:T(8,128)(2,1)S(1)}, bf16[128,1152]{1,0:T(8,128)(2,1)S(1)}, u32[]{:S(2)}, u32[]{:S(2)}) collective-permute-start(bf16[128,1152]{1,0:T(8,128)(2,1)S(1)} %get-tuple-element.208), channel_id=1, source_target_pairs={{0,8},{4,12},{8,0},{12,4},{1,9},{5,13},{9,1},{13,5},{2,10},{6,14},... | collective-permute-start | bytes 884744 | tf_op jit(solution)/shard_map/ppermute | solution.py:50
  (173 other events, 2538.2 us)
Sparse Core Ops, SparseCore 0:
  36.0 137.8 all-gather.2
  177.3 167.4 all-gather.4
  380.6 140.0 reduce-scatter.3
  526.7 183.1 reduce-scatter.5
  766.3 155.7 reduce-scatter.7

commit v4 on v3

--- a/solution.py
+++ b/solution.py
@@ -552,7 +552,6 @@
         for place in range(ranks)
     ]
     qkv_full = [full for full, _ in qkv_got]
-    mid_shard = lax.optimization_barrier([mid_shard] + [start for _, start in qkv_got])[0]
     mid_full = gather_all(mid_shard)
     two_full = gather_all(jnp.stack((w_up, w_down.T)))
 
@@ -580,6 +579,10 @@
             mixed[step] = send_xor(piece, HEAD_GROUP, step) if step else piece
     for step in range(1, halves):
         mixed += [send_xor(piece, "sr", step) for piece in mixed[:groups]]
+    out_full, key_full, val_full, cq_full, co_full = cut(mid_full, width, wide)
+    cross_k = [dot(caption, full).astype(bf16) for full in key_full]
+    cross_v = [dot(caption, full).astype(bf16) for full in val_full]
+    (mixed[0], cross_k, cross_v) = lax.optimization_barrier((mixed[0], cross_k, cross_v))
     att_low, att_wide, logsum = attend(mixed, groups, heads)
 
     def by_split(pieces, split):
@@ -596,7 +599,6 @@
         return [choose(pieces, jnp.bitwise_xor(col, place)) for place in range(splits)]
 
     att = from_own(att_own)
-    out_full, key_full, val_full, cq_full, co_full = cut(mid_full, width, wide)
     up_full, down_full = (
         [two_full[place, split * width : (split + 1) * width] for split in range(splits)]
         for place in range(2)
@@ -606,8 +608,6 @@
     after_one = residual + gate_one * out_one
     mid_low = after_one.astype(bf16)
     cross_q = [dot(mid_low, full).astype(bf16) for full in cq_full]
-    cross_k = [dot(caption, full).astype(bf16) for full in key_full]
-    cross_v = [dot(caption, full).astype(bf16) for full in val_full]
     cross_low = cross(cross_q, cross_k, cross_v, part)
     out_two = sum(dot(cross_low[split], co_full[split], NT) for split in range(splits))
     after_two = after_one + out_two
@@ -654,15 +654,17 @@
             step = other * splits + split
             piece = choose(cuts, jnp.bitwise_xor(rank, other))
             grad_heads[step] = send_xor(piece, HEAD_GROUP, step) if step else piece
+    lefts = [mid_low, grad_out_two, grad_out_one]
+    lefts, grad_ck, grad_cv, _ = lax.optimization_barrier((lefts, grad_ck, grad_cv, grad_att))
     caption_turn = dot(caption, turn).astype(bf16)
     mid_grads = [
         [dot(left, right, TN).astype(bf16) for right in rights]
         for left, rights in (
             (caption_turn, from_own(grad_ck)),
             (caption_turn, from_own(grad_cv)),
-            (dot(mid_low, turn).astype(bf16), from_own(grad_cq)),
-            (dot(grad_out_two, turn).astype(bf16), from_own(cross_low)),
-            (dot(grad_out_one, turn).astype(bf16), att_own),
+            (dot(lefts[0], turn).astype(bf16), from_own(grad_cq)),
+            (dot(lefts[1], turn).astype(bf16), from_own(cross_low)),
+            (dot(lefts[2], turn).astype(bf16), att_own),
         )
     ]
     pack_a = sum_pieces(pack_for("tensor", mid_grads[:3]), "fsdp")
@@ -681,11 +683,17 @@
             grad_mix[place] = (grad_mix[place].astype(f32) + more.astype(f32)).astype(bf16)
     grad_proj = give_back(grad_mix[:groups], HEAD_GROUP)
     grad_proj = [by_split(grad_proj, split) for split in range(splits)]
+    one_packs = [
+        pack_for(
+            ROW if place % 2 else "tensor",
+            [[dot(hidden_turn, grad_proj[split][place], TN).astype(bf16) for split in range(splits)]],
+        )
+        for place in range(ranks)
+    ]
+    (grad_proj, one_packs) = tie(grad_proj, one_packs)
     pack_a, pack_b = sum_blocks(pack_a, ROW), sum_blocks(pack_b, "tensor")
+    one_packs = [sum_pieces(pack, "fsdp") for pack in one_packs]
     text_sum = plane_sum(text_terms, bf16)
-    (grad_proj, pack_a, pack_b, text_sum) = lax.optimization_barrier(
-        (grad_proj, pack_a, pack_b, text_sum)
-    )
     grad_hidden_one = sum(
         dot(grad_proj[split][place], qkv_full[place][split], NT)
         for place in range(ranks)
@@ -710,26 +718,24 @@
             grad_gate_two,
         )
     )
-    table_terms = jnp.pad(time_terms.T, ((0, 0), (3 * edge, piece_width - 3 * edge - 6)))
-    one_grads = []
-    for place in range(ranks):
-        rights = from_own([grad_proj[split][place] for split in range(splits)])
-        grads = [dot(hidden_one, right, TN) for right in rights]
-        if place == 0:
-            grads = [grad + table_terms for grad in grads]
-        one_grads.append([grad.astype(bf16) for grad in grads])
-    pack_one, up_sum = tie(pack_grid(one_grads), up_sum)
-    one_sum = scatter_all(pack_one)
-    one_sums = [
-        one_sum[:, place * piece_width : (place + 1) * piece_width] for place in range(ranks)
-    ]
+    orders = [("tensor", ROW), (ROW, "tensor")]
+    for stage in range(2):
+        one_packs = [
+            sum_blocks(pack, orders[place % 2][stage]) for place, pack in enumerate(one_packs)
+        ]
+    (one_packs, up_sum) = tie(one_packs, up_sum)
+    one_sums = [sum_blocks(pack, "lat", f32) for pack in one_packs]
     pack_a, pack_b = sum_blocks(pack_a, "lat", f32), sum_blocks(pack_b, "lat", f32)
     key_sum, val_sum, cq_sum, co_sum, out_sum = (
         pack[:, place * wide : place * wide + part]
         for pack, count in ((pack_a, 3), (pack_b, 2))
         for place in range(count)
     )
-    grad_time = over_latents(plane_sum(time_terms, f32)).reshape(-1, 6 * width)
+    grad_time = over_latents(plane_sum(time_terms, f32))
+    grad_table = jnp.sum(grad_time, axis=0)
+    grad_table += send_xor(grad_table, "fsdp", 1)
+    owner = lax.axis_index(("fsdp", "lat", "sr", "hr"))
+    grad_table = lax.dynamic_slice_in_dim(grad_table, owner * share, share, 1)
     grad_text = over_latents(text_sum.astype(bf16)).astype(f32)
     grad_qkv = jnp.stack(
         [sums[:, : 3 * edge].reshape(share, 3, edge) for sums in one_sums], axis=2
@@ -738,8 +744,8 @@
         result_back,
         grad_latents.astype(f32),
         grad_text,
-        grad_time,
-        one_sums[0][:, 3 * edge : 3 * edge + 6].T,
+        grad_time.reshape(-1, 6 * width),
+        grad_table,
         grad_qkv,
         out_sum.T,
         cq_sum,

time: 937 us -> 904 us (0.965)
  waiting for transfers between devices: 334 us -> 299 us
    reduce_scatter x3 -> x2, waiting for transfers between devices: 45.5 us -> 0.01 us  [scatter_all(): lax.psum_scatter(pack, EVERY, scatter_dimension=0, tiled=True).astype(f32)]
    ppermute x65 -> x78, waiting for transfers between devices: 244 us -> 266 us  [send_xor(): lax.ppermute(piece, axes, [(rank, rank ^ step) for rank in range(size)])]
    all_gather x2, waiting for transfers between devices: 44.5 us -> 33.1 us  [gather_all(): return lax.all_gather(shard, EVERY, axis=shard.ndim - 2, tiled=True)]
    ppermute x65 -> x78, starting transfers between devices: 129 us -> 121 us  [send_xor(): lax.ppermute(piece, axes, [(rank, rank ^ step) for rank in range(size)])]
    pallas_call x9 -> x10, Pallas kernels: 58.1 us -> 60 us  [lay(): pl.pallas_call(partial(assemble_kernel, plan, len(sources)), in_specs=[an...]
  transfers between devices with their start and end apart: 70 -> 82, of which waited for: 29 -> 34; matrix products, arithmetic and copies ran while one was open for 22% -> 27% of each run, Pallas kernels for 18% -> 19%
where the time goes in v4:
time: 904 us; the launch traced here: 894 us
  waiting for transfers between devices  299 us (33%)
  matrix products  194 us (21%)
  Pallas kernels  181 us (20%)
  starting transfers between devices  121 us (13%)
  other arithmetic  46.7 us (5%)
  local copies, waits for them, and re-layouts  36.7 us (4%)
  between operations  15.9 us (2%)
    ppermute x78, waiting for transfers between devices, send_xor(): lax.ppermute(piece, axes, [(rank, rank ^ step) for rank in range(size)])  266 us
    dot_general x60, matrix products, dot(): return lax.dot_general(left, right, dims, preferred_element_type=f32)  194 us
    ppermute x78, starting transfers between devices, send_xor(): lax.ppermute(piece, axes, [(rank, rank ^ step) for rank in range(size)])  121 us
    pallas_call x10, Pallas kernels, lay(): pl.pallas_call(partial(assemble_kernel, plan, len(sources)), in_specs=[an...  60 us
    pallas_call x1, Pallas kernels, attend_back(): pl.pallas_call(partial(attend_back_kernel, heads, min(512, total), len(pi...  58.1 us
    all_gather x2, waiting for transfers between devices, gather_all(): return lax.all_gather(shard, EVERY, axis=shard.ndim - 2, tiled=True)  33.1 us
    pallas_call x1, Pallas kernels, attend(): pl.pallas_call(partial(attend_kernel, heads, len(pieces), own), grid=(row...  32.4 us
    pallas_call x1, Pallas kernels, cross_back(): pl.pallas_call(partial(cross_back_kernel, part, splits), grid=(rows // bl...  18.9 us
  transfers between devices with their start and end apart: 82, of which 34 were waited for; matrix products, arithmetic and copies ran while one was open for 27% of the time, Pallas kernels for 19%

profile of v4, /device:TPU:0, one launch (start us, length us, event | category | flops | bytes accessed | tf_op | source)
XLA Modules:
  0.0 894.1 jit_solution(5988158968233266135)
XLA Ops:
  24.2 9.6 %collective-permute-start = (bf16[72,896]{1,0:T(8,128)(2,1)S(1)}, bf16[72,896]{1,0:T(8,128)(2,1)S(1)}, u32[]{:S(2)}, u32[]{:S(2)}) collective-permute-start(bf16[72,896]{1,0:T(8,128)(2,1)S(1)} %get-tuple-element.289), channel_id=1, source_target_pairs={{0,4},{4,0},{8,12},{12,8},{1,5},{5,1},{9,13},{13,9},{2,6},{6,2},{1... | collective-permute-start | bytes 387080 | tf_op jit(solution)/shard_map/ppermute | solution.py:50
  33.8 11.2 %collective-permute-done.17 = bf16[72,896]{1,0:T(8,128)(2,1)S(1)} collective-permute-done((bf16[72,896]{1,0:T(8,128)(2,1)S(1)}, bf16[72,896]{1,0:T(8,128)(2,1)S(1)}, u32[]{:S(2)}, u32[]{:S(2)}) %collective-permute-start.17) | collective-permute-done | bytes 129056 | tf_op jit(solution)/shard_map/ppermute | solution.py:50
  55.5 16.4 %collective-permute-done.19.refs_1_ = bf16[288,896]{1,0:T(8,128)(2,1)S(1)} collective-permute-done((bf16[288,896]{1,0:T(8,128)(2,1)S(1)}, bf16[288,896]{1,0:T(8,128)(2,1)S(1)}, u32[]{:S(2)}, u32[]{:S(2)}) %collective-permute-start.19) | collective-permute-done | bytes 516128 | tf_op jit(solution)/shard_map/ppermute | solution.py:50
  82.8 11.1 %collective-permute-done.15 = bf16[128,1152]{1,0:T(8,128)(2,1)S(1)} collective-permute-done((bf16[128,1152]{1,0:T(8,128)(2,1)S(1)}, bf16[128,1152]{1,0:T(8,128)(2,1)S(1)}, u32[]{:S(2)}, u32[]{:S(2)}) %collective-permute-start.15) | collective-permute-done | bytes 294944 | tf_op jit(solution)/shard_map/ppermute | solution.py:50
  93.9 13.2 %collective-permute-start.13 = (bf16[128,1152]{1,0:T(8,128)(2,1)}, bf16[128,1152]{1,0:T(8,128)(2,1)S(1)}, u32[]{:S(2)}, u32[]{:S(2)}) collective-permute-start(bf16[128,1152]{1,0:T(8,128)(2,1)} %get-tuple-element.248), channel_id=1, source_target_pairs={{0,4},{4,0},{8,12},{12,8},{1,5},{5,1},{9,13},{13,9},{2,6},{6,2},{1... | collective-permute-start | bytes 884744 | tf_op jit(solution)/shard_map/ppermute | solution.py:50
  110.2 14.2 %collective-permute-done.13 = bf16[128,1152]{1,0:T(8,128)(2,1)S(1)} collective-permute-done((bf16[128,1152]{1,0:T(8,128)(2,1)}, bf16[128,1152]{1,0:T(8,128)(2,1)S(1)}, u32[]{:S(2)}, u32[]{:S(2)}) %collective-permute-start.13) | collective-permute-done | bytes 294944 | tf_op jit(solution)/shard_map/ppermute | solution.py:50
  164.4 11.3 %shard_map.214 = (bf16[1152,640]{1,0:T(8,128)(2,1)}, bf16[1152,640]{1,0:T(8,128)(2,1)}, bf16[1152,640]{1,0:T(8,128)(2,1)}, bf16[1152,640]{1,0:T(8,128)(2,1)}, bf...) custom-call(bf16[2304,3200]{1,0:T(8,128)(2,1)} %all-gather.3.cloned., ...), custom_call_target="tpu_custom_call" | custom-call | tf_op jit(solution)/shard_map/pallas_call | solution.py:407
  183.2 25.1 %collective-permute-done.24.refs_2_ = bf16[512,896]{1,0:T(8,128)(2,1)} collective-permute-done((bf16[512,896]{1,0:T(8,128)(2,1)}, bf16[512,896]{1,0:T(8,128)(2,1)}, u32[]{:S(2)}, u32[]{:S(2)}) %collective-permute-start.24) | collective-permute-done | bytes 917536 | tf_op jit(solution)/shard_map/ppermute | solution.py:50
  208.4 32.4 %shard_map.215 = (bf16[512,288]{1,0:T(8,128)(2,1)}, bf16[512,288]{1,0:T(8,128)(2,1)}, bf16[512,288]{1,0:T(8,128)(2,1)}, bf16[512,288]{1,0:T(8,128)(2,1)}, f32[4,2048,72]{2,1,0:T(8,128)}, /*index=5*/f32[8,2048]{1,0:T(8,128)}) custom-call(bf16[512,896]{1,0:T(8,128)(2,1)} %get-tuple-element.91.refs_0_, bf16[512,896]{1,0:T(8,128)(2,1)} %copy-done.108, ...), custom_call_target="tpu_custom_call" | custom-call | flops 17179869184 | bytes 7340032 | tf_op jit(solution)/shard_map/pallas_call | solution.py:160
  248.2 17.8 %collective-permute-done.28 = bf16[512,288]{1,0:T(8,128)(2,1)} collective-permute-done((bf16[512,288]{1,0:T(8,128)(2,1)}, bf16[512,288]{1,0:T(8,128)(2,1)}, u32[]{:S(2)}, u32[]{:S(2)}) %collective-permute-start.28) | collective-permute-done | bytes 294944 | tf_op jit(solution)/shard_map/ppermute | solution.py:50
  267.3 8.2 collective-permute-done.27
  283.2 11.6 %shard_map.216 = (bf16[512,640]{1,0:T(8,128)(2,1)}, bf16[512,640]{1,0:T(8,128)(2,1)}) custom-call(bf16[512,640]{1,0:T(8,128)(2,1)} %convolution_convert_fusion.27.refs_0_, bf16[512,640]{1,0:T(8,128)(2,1)} %convolution_convert_fusion.26.refs_1_, bf16[120,640]{1,0:T(8,128)(2,1)} %convolution_convert_fusion.31.refs_2_, ...), custom_call_target="tpu_custom_call" | custom-call | tf_op jit(solution)/shard_map/pallas_call | solution.py:318
  300.3 33.1 %all-gather.5.cloned.1.call-done = bf16[2,2304,2304]{2,1,0:T(8,128)(2,1)} async-done(((bf16[2,72,2304]{2,1,0:T(8,128)(2,1)}), bf16[2,2304,2304]{2,1,0:T(8,128)(2,1)}) %all-gather.5.cloned.1.call-update) | async-done | bytes 21233680 | tf_op jit(solution)/shard_map/all_gather | solution.py:462
  360.5 8.0 shard_map.221
  369.6 7.9 fusion.13
  378.9 8.4 fusion.23
  387.4 8.1 fusion.20
  395.5 8.2 multiply_reduce_fusion
  403.7 8.2 fusion.21
  412.0 9.6 %fusion.66 = (f32[1152]{0:T(1024)}, bf16[512,1152]{1,0:T(8,128)(2,1)S(1)}, bf16[512,1152]{1,0:T(8,128)(2,1)S(1)}, f32[512,1152]{1,0:T(8,128)S(1)}) fusion(bf16[128,1152]{1,0:T(8,128)(2,1)} %collective-permute-done.12, bf16[128,1152]{1,0:T(8,128)(2,1)} %collective-permute-done.11, bf16[128,1152]{1,0:T(8,128)(2,1)} %collective-permute-done.10, ...), kind=kOutput, calls=%fused_computation.113 | convolution fusion | flops 2742090752 | bytes 23025152 | tf_op jit(solution)/shard_map/dot_general | solution.py:33
  425.6 18.9 %shard_map.217 = (bf16[512,640]{1,0:T(8,128)(2,1)}, bf16[512,640]{1,0:T(8,128)(2,1)}, bf16[120,640]{1,0:T(8,128)(2,1)}, bf16[120,640]{1,0:T(8,128)(2,1)}, bf16[1...) custom-call(bf16[512,640]{1,0:T(8,128)(2,1)} %convolution_convert_fusion.27.refs_0_, ...), custom_call_target="tpu_custom_call" | custom-call | tf_op jit(solution)/shard_map/pallas_call | solution.py:374
  466.6 7.8 shard_map.218
  509.2 8.1 shard_map.224
  543.3 11.4 %collective-permute-done.35.refs_6_ = bf16[512,288]{1,0:T(8,128)(2,1)S(1)} collective-permute-done((bf16[512,288]{1,0:T(8,128)(2,1)S(1)}, bf16[512,288]{1,0:T(8,128)(2,1)S(1)}, u32[]{:S(2)}, u32[]{:S(2)}) %collective-permute-start.35) | collective-permute-done | bytes 294944 | tf_op jit(solution)/shard_map/ppermute | solution.py:50
  555.5 58.1 %shard_map.220 = (bf16[512,896]{1,0:T(8,128)(2,1)}, bf16[512,896]{1,0:T(8,128)(2,1)}, bf16[512,896]{1,0:T(8,128)(2,1)}, bf16[512,896]{1,0:T(8,128)(2,1)}) custom-call(bf16[512,896]{1,0:T(8,128)(2,1)} %get-tuple-element.91.refs_0_, bf16[512,896]{1,0:T(8,128)(2,1)} %copy-done.108, bf16[512,896]{1,0:T(8,128)(2,1)} %collective-permute-done.24.refs_2_, ...), custom_call_target="tpu_custom_call" | custom-call | flops 42949672960 | bytes 14680064 | tf_op jit(solution)/shard_map/pallas_call | solution.py:264
  632.1 19.8 %collective-permute-done.49 = bf16[120,1152]{1,0:T(8,128)(2,1)} collective-permute-done((bf16[120,1152]{1,0:T(8,128)(2,1)S(1)}, bf16[120,1152]{1,0:T(8,128)(2,1)}, u32[]{:S(2)}, u32[]{:S(2)}) %collective-permute-start.49) | collective-permute-done | bytes 276512 | tf_op jit(solution)/shard_map/ppermute | solution.py:50
  656.1 7.4 collective-permute-done.41
  670.7 18.8 %collective-permute-done.39 = bf16[576,1280]{1,0:T(8,128)(2,1)S(1)} collective-permute-done((bf16[576,1280]{1,0:T(8,128)(2,1)S(1)}, bf16[576,1280]{1,0:T(8,128)(2,1)S(1)}, u32[]{:S(2)}, u32[]{:S(2)}) %collective-permute-start.39) | collective-permute-done | bytes 1474592 | tf_op jit(solution)/shard_map/ppermute | solution.py:50
  691.0 22.0 %collective-permute-done.38 = bf16[576,1920]{1,0:T(8,128)(2,1)} collective-permute-done((bf16[576,1920]{1,0:T(8,128)(2,1)}, bf16[576,1920]{1,0:T(8,128)(2,1)}, u32[]{:S(2)}, u32[]{:S(2)}) %collective-permute-start.38) | collective-permute-done | bytes 2211872 | tf_op jit(solution)/shard_map/ppermute | solution.py:50
  743.9 9.9 %fusion.63 = (f32[1152]{0:T(1024)}, f32[512]{0:T(512)}, f32[512]{0:T(512)}, f32[1152]{0:T(1024)}, f32[512,1152]{1,0:T(8,128)}) fusion(f32[512]{0:T(512)} %copy-done.95, f32[512]{0:T(512)} %copy-done.83, bf16[128,1152]{1,0:T(8,128)(2,1)S(1)} %copy-done.17, bf16[128,1152]{1,0:T(8,128)(2,1)S(1)} %copy-done.19, bf16[128,1152]{1,0:T(8,128)(2,1)S(1)} %copy-done.21, ...), kind=kOutput, calls=%fused_computation.110 | convolution fusion | flops 2429629440 | bytes 13625344 | tf_op jit(solution)/shard_map/dot_general | solution.py:33
  788.3 13.3 %collective-permute-done.43 = bf16[128,1152]{1,0:T(8,128)(2,1)} collective-permute-done((bf16[128,1152]{1,0:T(8,128)(2,1)}, bf16[128,1152]{1,0:T(8,128)(2,1)}, u32[]{:S(2)}, u32[]{:S(2)}) %collective-permute-start.43) | collective-permute-done | bytes 294944 | tf_op jit(solution)/shard_map/ppermute | solution.py:50
  831.2 12.8 %collective-permute-done.76 = bf16[72,1920]{1,0:T(8,128)(2,1)S(1)} collective-permute-done((bf16[72,1920]{1,0:T(8,128)(2,1)S(1)}, bf16[72,1920]{1,0:T(8,128)(2,1)S(1)}, u32[]{:S(2)}, u32[]{:S(2)}) %collective-permute-start.76) | collective-permute-done | bytes 276512 | tf_op jit(solution)/shard_map/ppermute | solution.py:50
  (588 shorter events, 396.0 us)
Async XLA Ops:
  7.2 157.1 %all-gather.3.cloned.1.call-start = ((), (), s32[]{:S(2)}) async-start(), calls=%async_computation.2 | async-start | bytes 15206400 | tf_op jit(solution)/shard_map/all_gather | solution.py:462
  12.4 321.0 %all-gather.5.cloned.1.call-start = ((), (), s32[]{:S(2)}) async-start(), calls=%async_computation.3 | async-start | bytes 21897216 | tf_op jit(solution)/shard_map/all_gather | solution.py:462
  13.3 703.1 %reduce-scatter.3.cloned.1.call-start = ((), (), s32[]{:S(2)}) async-start(), calls=%async_computation.4 | async-start | bytes 10948608 | tf_op jit(solution)/shard_map/reduce_scatter | solution.py:466
  74.9 51.0 %collective-permute-start.21 = (bf16[576,896]{1,0:T(8,128)(2,1)}, bf16[576,896]{1,0:T(8,128)(2,1)}, u32[]{:S(2)}, u32[]{:S(2)}) collective-permute-start(bf16[576,896]{1,0:T(8,128)(2,1)} %shard_map.212.refs_0_), channel_id=1, source_target_pairs={{0,1},{1,0},{2,3},{3,2},{4,5},{5,4},{6,7},{7,6},{8,9},{9,8},{10,11... | collective-permute-start | bytes 3096584 | tf_op jit(solution)/shard_map/ppermute | solution.py:50
  80.7 29.3 %collective-permute-start.14 = (bf16[128,1152]{1,0:T(8,128)(2,1)S(1)}, bf16[128,1152]{1,0:T(8,128)(2,1)S(1)}, u32[]{:S(2)}, u32[]{:S(2)}) collective-permute-start(bf16[128,1152]{1,0:T(8,128)(2,1)S(1)} %get-tuple-element.250), channel_id=1, source_target_pairs={{0,8},{4,12},{8,0},{12,4},{1,9},{5,13},{9,1},{13,5},{2,10},{6,14},... | collective-permute-start | bytes 884744 | tf_op jit(solution)/shard_map/ppermute | solution.py:50
  80.7 44.0 %collective-permute-start.3 = (bf16[288,896]{1,0:T(8,128)(2,1)}, bf16[288,896]{1,0:T(8,128)(2,1)}, u32[]{:S(2)}, u32[]{:S(2)}) collective-permute-start(bf16[288,896]{1,0:T(8,128)(2,1)} %get-tuple-element.287.refs_0_), channel_id=1, source_target_pairs={{0,2},{2,0},{1,3},{3,1},{4,6},{6,4},{5,7},{7,5},{8,10},{10,8},{9,1... | collective-permute-start | bytes 1548296 | tf_op jit(solution)/shard_map/ppermute | solution.py:50
  82.3 43.0 %collective-permute-start.7 = (bf16[288,896]{1,0:T(8,128)(2,1)}, bf16[288,896]{1,0:T(8,128)(2,1)}, u32[]{:S(2)}, u32[]{:S(2)}) collective-permute-start(bf16[288,896]{1,0:T(8,128)(2,1)} %collective-permute-done.6.refs_4_), channel_id=1, source_target_pairs={{0,2},{2,0},{1,3},{3,1},{4,6},{6,4},{5,7},{7,5},{8,10},{10,8},{9,1... | collective-permute-start | bytes 1548296 | tf_op jit(solution)/shard_map/ppermute | solution.py:50
  93.9 30.5 %collective-permute-start.13 = (bf16[128,1152]{1,0:T(8,128)(2,1)}, bf16[128,1152]{1,0:T(8,128)(2,1)S(1)}, u32[]{:S(2)}, u32[]{:S(2)}) collective-permute-start(bf16[128,1152]{1,0:T(8,128)(2,1)} %get-tuple-element.248), channel_id=1, source_target_pairs={{0,4},{4,0},{8,12},{12,8},{1,5},{5,1},{9,13},{13,9},{2,6},{6,2},{1... | collective-permute-start | bytes 884744 | tf_op jit(solution)/shard_map/ppermute | solution.py:50
  152.7 30.6 %collective-permute-start.23 = (bf16[512,896]{1,0:T(8,128)(2,1)}, bf16[512,896]{1,0:T(8,128)(2,1)S(1)}, u32[]{:S(2)}, u32[]{:S(2)}) collective-permute-start(bf16[512,896]{1,0:T(8,128)(2,1)} %get-tuple-element.232), channel_id=1, source_target_pairs={{0,1},{1,0},{2,3},{3,2},{4,5},{5,4},{6,7},{7,6},{8,9},{9,8},{10,11... | collective-permute-start | bytes 2752520 | tf_op jit(solution)/shard_map/ppermute | solution.py:50
  157.0 51.3 %collective-permute-start.24 = (bf16[512,896]{1,0:T(8,128)(2,1)}, bf16[512,896]{1,0:T(8,128)(2,1)}, u32[]{:S(2)}, u32[]{:S(2)}) collective-permute-start(bf16[512,896]{1,0:T(8,128)(2,1)} %get-tuple-element.233), channel_id=1, source_target_pairs={{0,2},{1,3},{2,0},{3,1},{4,6},{5,7},{6,4},{7,5},{8,10},{9,11},{10,... | collective-permute-start | bytes 2752520 | tf_op jit(solution)/shard_map/ppermute | solution.py:50
  162.9 45.5 %collective-permute-start.25 = (bf16[512,896]{1,0:T(8,128)(2,1)}, bf16[512,896]{1,0:T(8,128)(2,1)}, u32[]{:S(2)}, u32[]{:S(2)}) collective-permute-start(bf16[512,896]{1,0:T(8,128)(2,1)} %get-tuple-element.231), channel_id=1, source_target_pairs={{0,3},{1,2},{2,1},{3,0},{4,7},{5,6},{6,5},{7,4},{8,11},{9,10},{10,... | collective-permute-start | bytes 2752520 | tf_op jit(solution)/shard_map/ppermute | solution.py:50
  245.8 29.7 %collective-permute-start.27 = (bf16[512,288]{1,0:T(8,128)(2,1)}, bf16[512,288]{1,0:T(8,128)(2,1)S(1)}, u32[]{:S(2)}, u32[]{:S(2)}) collective-permute-start(bf16[512,288]{1,0:T(8,128)(2,1)} %get-tuple-element.95), channel_id=1, source_target_pairs={{0,1},{1,0},{2,3},{3,2},{4,5},{5,4},{6,7},{7,6},{8,9},{9,8},{10,11... | collective-permute-start | bytes 884744 | tf_op jit(solution)/shard_map/ppermute | solution.py:50
  247.1 99.4 %collective-permute-start.12 = (bf16[128,1152]{1,0:T(8,128)(2,1)}, bf16[128,1152]{1,0:T(8,128)(2,1)}, u32[]{:S(2)}, u32[]{:S(2)}) collective-permute-start(bf16[128,1152]{1,0:T(8,128)(2,1)} %get-tuple-element.244), channel_id=1, source_target_pairs={{0,12},{4,8},{8,4},{12,0},{1,13},{5,9},{9,5},{13,1},{2,14},{6,10},... | collective-permute-start | bytes 884744 | tf_op jit(solution)/shard_map/ppermute | solution.py:50
  247.9 98.7 %collective-permute-start.11 = (bf16[128,1152]{1,0:T(8,128)(2,1)}, bf16[128,1152]{1,0:T(8,128)(2,1)}, u32[]{:S(2)}, u32[]{:S(2)}) collective-permute-start(bf16[128,1152]{1,0:T(8,128)(2,1)} %get-tuple-element.245), channel_id=1, source_target_pairs={{0,8},{4,12},{8,0},{12,4},{1,9},{5,13},{9,1},{13,5},{2,10},{6,14},... | collective-permute-start | bytes 884744 | tf_op jit(solution)/shard_map/ppermute | solution.py:50
  266.1 80.5 %collective-permute-start.10 = (bf16[128,1152]{1,0:T(8,128)(2,1)}, bf16[128,1152]{1,0:T(8,128)(2,1)}, u32[]{:S(2)}, u32[]{:S(2)}) collective-permute-start(bf16[128,1152]{1,0:T(8,128)(2,1)} %get-tuple-element.246), channel_id=1, source_target_pairs={{0,4},{4,0},{8,12},{12,8},{1,5},{5,1},{9,13},{13,9},{2,6},{6,2},{1... | collective-permute-start | bytes 884744 | tf_op jit(solution)/shard_map/ppermute | solution.py:50
  368.6 410.2 %reduce-scatter.5.cloned.1.call-start = ((), (), s32[]{:S(2)}) async-start(), calls=%async_computation.5 | async-start | bytes 10948608 | tf_op jit(solution)/shard_map/reduce_scatter | solution.py:466
  474.5 60.4 %collective-permute-start.29 = (bf16[1152,1920]{1,0:T(8,128)(2,1)}, bf16[1152,1920]{1,0:T(8,128)(2,1)}, u32[]{:S(2)}, u32[]{:S(2)}) collective-permute-start(bf16[1152,1920]{1,0:T(8,128)(2,1)} %get-tuple-element.122), channel_id=1, source_target_pairs={{0,16},{16,0},{1,17},{17,1},{2,18},{18,2},{3,19},{19,3},{4,20},{20... | collective-permute-start | bytes 13271048 | tf_op jit(solution)/shard_map/ppermute | solution.py:50
  493.6 37.7 %collective-permute-start.30 = (bf16[1152,1280]{1,0:T(8,128)(2,1)}, bf16[1152,1280]{1,0:T(8,128)(2,1)}, u32[]{:S(2)}, u32[]{:S(2)}) collective-permute-start(bf16[1152,1280]{1,0:T(8,128)(2,1)} %get-tuple-element.126), channel_id=1, source_target_pairs={{0,16},{16,0},{1,17},{17,1},{2,18},{18,2},{3,19},{19,3},{4,20},{20... | collective-permute-start | bytes 8847368 | tf_op jit(solution)/shard_map/ppermute | solution.py:50
  495.5 30.4 %collective-permute-start.32 = (bf16[128,1152]{1,0:T(8,128)(2,1)}, bf16[128,1152]{1,0:T(8,128)(2,1)}, u32[]{:S(2)}, u32[]{:S(2)}) collective-permute-start(bf16[128,1152]{1,0:T(8,128)(2,1)} %get-tuple-element.241), channel_id=1, source_target_pairs={{0,8},{4,12},{8,0},{12,4},{1,9},{5,13},{9,1},{13,5},{2,10},{6,14},... | collective-permute-start | bytes 884744 | tf_op jit(solution)/shard_map/ppermute | solution.py:50
  495.5 31.8 %collective-permute-start.33 = (bf16[128,1152]{1,0:T(8,128)(2,1)S(1)}, bf16[128,1152]{1,0:T(8,128)(2,1)}, u32[]{:S(2)}, u32[]{:S(2)}) collective-permute-start(bf16[128,1152]{1,0:T(8,128)(2,1)S(1)} %get-tuple-element.240), channel_id=1, source_target_pairs={{0,4},{4,0},{8,12},{12,8},{1,5},{5,1},{9,13},{13,9},{2,6},{6,2},{1... | collective-permute-start | bytes 884744 | tf_op jit(solution)/shard_map/ppermute | solution.py:50
  522.9 93.8 %collective-permute-start.47 = (bf16[120,1152]{1,0:T(8,128)(2,1)S(1)}, bf16[120,1152]{1,0:T(8,128)(2,1)}, u32[]{:S(2)}, u32[]{:S(2)}) collective-permute-start(bf16[120,1152]{1,0:T(8,128)(2,1)S(1)} %fusion.54), channel_id=1, source_target_pairs={{0,3},{1,2},{2,1},{3,0},{4,7},{5,6},{6,5},{7,4},{8,11},{9,10},{10,... | collective-permute-start | bytes 829448 | tf_op jit(solution)/shard_map/ppermute | solution.py:50
  526.0 90.7 %collective-permute-start.46 = (bf16[120,1152]{1,0:T(8,128)(2,1)S(1)}, bf16[120,1152]{1,0:T(8,128)(2,1)}, u32[]{:S(2)}, u32[]{:S(2)}) collective-permute-start(bf16[120,1152]{1,0:T(8,128)(2,1)S(1)} %fusion.54), channel_id=1, source_target_pairs={{0,2},{1,3},{2,0},{3,1},{4,6},{5,7},{6,4},{7,5},{8,10},{9,11},{10,... | collective-permute-start | bytes 829448 | tf_op jit(solution)/shard_map/ppermute | solution.py:50
  541.9 74.8 %collective-permute-start.45 = (bf16[120,1152]{1,0:T(8,128)(2,1)S(1)}, bf16[120,1152]{1,0:T(8,128)(2,1)S(1)}, u32[]{:S(2)}, u32[]{:S(2)}) collective-permute-start(bf16[120,1152]{1,0:T(8,128)(2,1)S(1)} %fusion.54), channel_id=1, source_target_pairs={{0,1},{1,0},{2,3},{3,2},{4,5},{5,4},{6,7},{7,6},{8,9},{9,8},{10,11... | collective-permute-start | bytes 829448 | tf_op jit(solution)/shard_map/ppermute | solution.py:50
  613.6 42.4 %collective-permute-start.40 = (bf16[512,896]{1,0:T(8,128)(2,1)}, bf16[512,896]{1,0:T(8,128)(2,1)}, u32[]{:S(2)}, u32[]{:S(2)}) collective-permute-start(bf16[512,896]{1,0:T(8,128)(2,1)} %get-tuple-element.136), channel_id=1, source_target_pairs={{0,3},{1,2},{2,1},{3,0},{4,7},{5,6},{6,5},{7,4},{8,11},{9,10},{10,... | collective-permute-start | bytes 2752520 | tf_op jit(solution)/shard_map/ppermute | solution.py:50
  616.0 47.5 %collective-permute-start.41 = (bf16[512,896]{1,0:T(8,128)(2,1)}, bf16[512,896]{1,0:T(8,128)(2,1)}, u32[]{:S(2)}, u32[]{:S(2)}) collective-permute-start(bf16[512,896]{1,0:T(8,128)(2,1)} %get-tuple-element.137), channel_id=1, source_target_pairs={{0,1},{1,0},{2,3},{3,2},{4,5},{5,4},{6,7},{7,6},{8,9},{9,8},{10,11... | collective-permute-start | bytes 2752520 | tf_op jit(solution)/shard_map/ppermute | solution.py:50
  618.8 33.1 %collective-permute-start.49 = (bf16[120,1152]{1,0:T(8,128)(2,1)S(1)}, bf16[120,1152]{1,0:T(8,128)(2,1)}, u32[]{:S(2)}, u32[]{:S(2)}) collective-permute-start(bf16[120,1152]{1,0:T(8,128)(2,1)S(1)} %add_convert_fusion.14), channel_id=1, source_target_pairs={{0,8},{4,12},{8,0},{12,4},{1,9},{5,13},{9,1},{13,5},{2,10},{6,14},... | collective-permute-start | bytes 829448 | tf_op jit(solution)/shard_map/ppermute | solution.py:50
  619.7 32.7 %collective-permute-start.50 = (bf16[120,1152]{1,0:T(8,128)(2,1)S(1)}, bf16[120,1152]{1,0:T(8,128)(2,1)}, u32[]{:S(2)}, u32[]{:S(2)}) collective-permute-start(bf16[120,1152]{1,0:T(8,128)(2,1)S(1)} %add_convert_fusion.14), channel_id=1, source_target_pairs={{0,4},{4,0},{8,12},{12,8},{1,5},{5,1},{9,13},{13,9},{2,6},{6,2},{1... | collective-permute-start | bytes 829448 | tf_op jit(solution)/shard_map/ppermute | solution.py:50
  629.4 83.6 %collective-permute-start.38 = (bf16[576,1920]{1,0:T(8,128)(2,1)}, bf16[576,1920]{1,0:T(8,128)(2,1)}, u32[]{:S(2)}, u32[]{:S(2)}) collective-permute-start(bf16[576,1920]{1,0:T(8,128)(2,1)} %slice.204), channel_id=1, source_target_pairs={{0,1},{1,0},{2,3},{3,2},{4,5},{5,4},{6,7},{7,6},{8,9},{9,8},{10,11... | collective-permute-start | bytes 6635528 | tf_op jit(solution)/shard_map/ppermute | solution.py:50
  651.9 37.6 %collective-permute-start.39 = (bf16[576,1280]{1,0:T(8,128)(2,1)S(1)}, bf16[576,1280]{1,0:T(8,128)(2,1)S(1)}, u32[]{:S(2)}, u32[]{:S(2)}) collective-permute-start(bf16[576,1280]{1,0:T(8,128)(2,1)S(1)} %slice.206), channel_id=1, source_target_pairs={{0,2},{2,0},{1,3},{3,1},{4,6},{6,4},{5,7},{7,5},{8,10},{10,8},{9,1... | collective-permute-start | bytes 4423688 | tf_op jit(solution)/shard_map/ppermute | solution.py:50
  654.6 63.9 %collective-permute-start.37 = (bf16[512,896]{1,0:T(8,128)(2,1)}, bf16[512,896]{1,0:T(8,128)(2,1)}, u32[]{:S(2)}, u32[]{:S(2)}) collective-permute-start(bf16[512,896]{1,0:T(8,128)(2,1)} %get-tuple-element.131), channel_id=1, source_target_pairs={{0,2},{1,3},{2,0},{3,1},{4,6},{5,7},{6,4},{7,5},{8,10},{9,11},{10,... | collective-permute-start | bytes 2752520 | tf_op jit(solution)/shard_map/ppermute | solution.py:50
  785.7 38.5 %collective-permute-start.58 = (bf16[1152,896]{1,0:T(8,128)(2,1)}, bf16[1152,896]{1,0:T(8,128)(2,1)S(1)}, u32[]{:S(2)}, u32[]{:S(2)}) collective-permute-start(bf16[1152,896]{1,0:T(8,128)(2,1)} %get-tuple-element.147), channel_id=1, source_target_pairs={{0,16},{16,0},{1,17},{17,1},{2,18},{18,2},{3,19},{19,3},{4,20},{20... | collective-permute-start | bytes 6193160 | tf_op jit(solution)/shard_map/ppermute | solution.py:50
  786.9 32.4 %collective-permute-start.74 = (bf16[288,1920]{1,0:T(8,128)(2,1)}, bf16[288,1920]{1,0:T(8,128)(2,1)S(1)}, u32[]{:S(2)}, u32[]{:S(2)}) collective-permute-start(bf16[288,1920]{1,0:T(8,128)(2,1)} %slice.233), channel_id=1, source_target_pairs={{0,2},{2,0},{1,3},{3,1},{4,6},{6,4},{5,7},{7,5},{8,10},{10,8},{9,1... | collective-permute-start | bytes 3317768 | tf_op jit(solution)/shard_map/ppermute | solution.py:50
  (185 other events, 2971.7 us)
Sparse Core Ops, SparseCore 0:
  12.5 143.8 all-gather.2
  159.8 173.5 all-gather.4
  368.7 155.0 reduce-scatter.2
  529.8 149.2 reduce-scatter.4

commit v5 on v4

--- a/solution.py
+++ b/solution.py
@@ -656,7 +656,8 @@
             grad_heads[step] = send_xor(piece, HEAD_GROUP, step) if step else piece
     lefts = [mid_low, grad_out_two, grad_out_one]
     lefts, grad_ck, grad_cv, _ = lax.optimization_barrier((lefts, grad_ck, grad_cv, grad_att))
-    caption_turn = dot(caption, turn).astype(bf16)
+    lefts[0], caption_late, grad_heads = lax.optimization_barrier((lefts[0], caption, grad_heads))
+    caption_turn = dot(caption_late, turn).astype(bf16)
     mid_grads = [
         [dot(left, right, TN).astype(bf16) for right in rights]
         for left, rights in (
@@ -673,10 +674,9 @@
         (grad_heads[0], pack_a, pack_b, result_back)
     )
     pack_a, pack_b = sum_blocks(pack_a, "tensor"), sum_blocks(pack_b, ROW)
+    text_sum = plane_sum(text_terms, bf16)
     grad_mix = list(attend_back(mixed, groups, grad_heads, att_wide, logsum, heads))
-    (grad_mix[0], pack_a, pack_b, down_sum) = lax.optimization_barrier(
-        (grad_mix[0], pack_a, pack_b, down_sum)
-    )
+    (grad_mix[0], down_sum) = tie(grad_mix[0], down_sum)
     for step in range(1, halves):
         for place in range(groups):
             more = send_xor(grad_mix[step * groups + place], "sr", step)
@@ -690,10 +690,11 @@
         )
         for place in range(ranks)
     ]
-    (grad_proj, one_packs) = tie(grad_proj, one_packs)
+    (grad_proj, one_packs, pack_a, pack_b, text_sum) = lax.optimization_barrier(
+        (grad_proj, one_packs, pack_a, pack_b, text_sum)
+    )
     pack_a, pack_b = sum_blocks(pack_a, ROW), sum_blocks(pack_b, "tensor")
     one_packs = [sum_pieces(pack, "fsdp") for pack in one_packs]
-    text_sum = plane_sum(text_terms, bf16)
     grad_hidden_one = sum(
         dot(grad_proj[split][place], qkv_full[place][split], NT)
         for place in range(ranks)

time: 904 us -> 912 us (level)
  waiting for transfers between devices: 299 us -> 345 us
  starting transfers between devices: 121 us -> 95.7 us
    ppermute x78, starting transfers between devices: 121 us -> 95.5 us  [send_xor(): lax.ppermute(piece, axes, [(rank, rank ^ step) for rank in range(size)])]
    all_gather x2, waiting for transfers between devices: 33.1 us -> 57.9 us  [gather_all(): return lax.all_gather(shard, EVERY, axis=shard.ndim - 2, tiled=True)]
    ppermute x78, waiting for transfers between devices: 266 us -> 287 us  [send_xor(): lax.ppermute(piece, axes, [(rank, rank ^ step) for rank in range(size)])]
  transfers between devices with their start and end apart: 82 -> 82, of which waited for: 34 -> 39; matrix products, arithmetic and copies ran while one was open for 27% -> 26% of each run, Pallas kernels for 19% -> 19%
where the time goes in v5:
time: 912 us; the launch traced here: 902 us
  waiting for transfers between devices  345 us (38%)
  matrix products  190 us (21%)
  Pallas kernels  180 us (20%)
  starting transfers between devices  95.7 us (10%)
  other arithmetic  41 us (4%)
  local copies, waits for them, and re-layouts  33.6 us (4%)
  between operations  16 us (2%)
    ppermute x78, waiting for transfers between devices, send_xor(): lax.ppermute(piece, axes, [(rank, rank ^ step) for rank in range(size)])  287 us
    dot_general x60, matrix products, dot(): return lax.dot_general(left, right, dims, preferred_element_type=f32)  190 us
    ppermute x78, starting transfers between devices, send_xor(): lax.ppermute(piece, axes, [(rank, rank ^ step) for rank in range(size)])  95.5 us
    pallas_call x10, Pallas kernels, lay(): pl.pallas_call(partial(assemble_kernel, plan, len(sources)), in_specs=[an...  58.9 us
    pallas_call x1, Pallas kernels, attend_back(): pl.pallas_call(partial(attend_back_kernel, heads, min(512, total), len(pi...  57.9 us
    all_gather x2, waiting for transfers between devices, gather_all(): return lax.all_gather(shard, EVERY, axis=shard.ndim - 2, tiled=True)  57.9 us
    pallas_call x1, Pallas kernels, attend(): pl.pallas_call(partial(attend_kernel, heads, len(pieces), own), grid=(row...  32.4 us
    pallas_call x1, Pallas kernels, cross_back(): pl.pallas_call(partial(cross_back_kernel, part, splits), grid=(rows // bl...  18.9 us
  transfers between devices with their start and end apart: 82, of which 39 were waited for; matrix products, arithmetic and copies ran while one was open for 26% of the time, Pallas kernels for 19%

profile of v5, /device:TPU:0, one launch (start us, length us, event | category | flops | bytes accessed | tf_op | source)
XLA Modules:
  0.0 901.7 jit_solution(13793021121547741200)
XLA Ops:
  24.2 9.6 %collective-permute-start.3 = (bf16[72,896]{1,0:T(8,128)(2,1)S(1)}, bf16[72,896]{1,0:T(8,128)(2,1)S(1)}, u32[]{:S(2)}, u32[]{:S(2)}) collective-permute-start(bf16[72,896]{1,0:T(8,128)(2,1)S(1)} %get-tuple-element.303), channel_id=1, source_target_pairs={{0,4},{4,0},{8,12},{12,8},{1,5},{5,1},{9,13},{13,9},{2,6},{6,2},{1... | collective-permute-start | bytes 387080 | tf_op jit(solution)/shard_map/ppermute | solution.py:50
  33.8 11.2 %collective-permute-done.14 = bf16[72,896]{1,0:T(8,128)(2,1)S(1)} collective-permute-done((bf16[72,896]{1,0:T(8,128)(2,1)S(1)}, bf16[72,896]{1,0:T(8,128)(2,1)S(1)}, u32[]{:S(2)}, u32[]{:S(2)}) %collective-permute-start.14) | collective-permute-done | bytes 129056 | tf_op jit(solution)/shard_map/ppermute | solution.py:50
  54.8 16.4 %collective-permute-done.16.refs_1_ = bf16[288,896]{1,0:T(8,128)(2,1)S(1)} collective-permute-done((bf16[288,896]{1,0:T(8,128)(2,1)S(1)}, bf16[288,896]{1,0:T(8,128)(2,1)S(1)}, u32[]{:S(2)}, u32[]{:S(2)}) %collective-permute-start.16) | collective-permute-done | bytes 516128 | tf_op jit(solution)/shard_map/ppermute | solution.py:50
  83.0 13.5 %collective-permute-done = bf16[128,1152]{1,0:T(8,128)(2,1)S(1)} collective-permute-done((bf16[128,1152]{1,0:T(8,128)(2,1)S(1)}, bf16[128,1152]{1,0:T(8,128)(2,1)S(1)}, u32[]{:S(2)}, u32[]{:S(2)}) %collective-permute-start) | collective-permute-done | bytes 294944 | tf_op jit(solution)/shard_map/ppermute | solution.py:50
  101.0 11.1 %collective-permute-done.1 = bf16[128,1152]{1,0:T(8,128)(2,1)S(1)} collective-permute-done((bf16[128,1152]{1,0:T(8,128)(2,1)}, bf16[128,1152]{1,0:T(8,128)(2,1)S(1)}, u32[]{:S(2)}, u32[]{:S(2)}) %collective-permute-start.1) | collective-permute-done | bytes 294944 | tf_op jit(solution)/shard_map/ppermute | solution.py:50
  148.3 10.2 %all-gather.3.cloned.1.call-done.refs_0_ = bf16[2304,3200]{1,0:T(8,128)(2,1)} async-done(((bf16[72,3200]{1,0:T(8,128)(2,1)}), bf16[2304,3200]{1,0:T(8,128)(2,1)}) %all-gather.3.cloned.1.call-update) | async-done | bytes 14745616 | tf_op jit(solution)/shard_map/all_gather | solution.py:462
  158.4 10.7 %shard_map.214 = (bf16[1152,640]{1,0:T(8,128)(2,1)}, bf16[1152,640]{1,0:T(8,128)(2,1)}, bf16[1152,640]{1,0:T(8,128)(2,1)}, bf16[1152,640]{1,0:T(8,128)(2,1)}, bf...) custom-call(bf16[2304,3200]{1,0:T(8,128)(2,1)} %all-gather.3.cloned., ...), custom_call_target="tpu_custom_call" | custom-call | tf_op jit(solution)/shard_map/pallas_call | solution.py:407
  176.8 11.8 %collective-permute-done.20.refs_1_ = bf16[512,896]{1,0:T(8,128)(2,1)} collective-permute-done((bf16[512,896]{1,0:T(8,128)(2,1)}, bf16[512,896]{1,0:T(8,128)(2,1)}, u32[]{:S(2)}, u32[]{:S(2)}) %collective-permute-start.20) | collective-permute-done | bytes 917536 | tf_op jit(solution)/shard_map/ppermute | solution.py:50
  188.6 32.4 %shard_map.215 = (bf16[512,288]{1,0:T(8,128)(2,1)}, bf16[512,288]{1,0:T(8,128)(2,1)}, bf16[512,288]{1,0:T(8,128)(2,1)}, bf16[512,288]{1,0:T(8,128)(2,1)}, f32[4,2048,72]{2,1,0:T(8,128)}, /*index=5*/f32[8,2048]{1,0:T(8,128)}) custom-call(bf16[512,896]{1,0:T(8,128)(2,1)} %get-tuple-element.97.refs_0_, bf16[512,896]{1,0:T(8,128)(2,1)} %collective-permute-done.20.refs_1_, ...), custom_call_target="tpu_custom_call" | custom-call | flops 17179869184 | bytes 7340032 | tf_op jit(solution)/shard_map/pallas_call | solution.py:160
  227.5 6.7 collective-permute-done.23
  234.2 7.4 collective-permute-done.24
  249.5 12.0 %shard_map.216 = (bf16[512,640]{1,0:T(8,128)(2,1)}, bf16[512,640]{1,0:T(8,128)(2,1)}) custom-call(bf16[512,640]{1,0:T(8,128)(2,1)} %convolution_convert_fusion.27.refs_0_, bf16[512,640]{1,0:T(8,128)(2,1)} %convolution_convert_fusion.26.refs_1_, bf16[120,640]{1,0:T(8,128)(2,1)} %convolution_convert_fusion.31.refs_2_, ...), custom_call_target="tpu_custom_call" | custom-call | tf_op jit(solution)/shard_map/pallas_call | solution.py:318
  267.1 47.7 %all-gather.5.cloned.1.call-done = bf16[2,2304,2304]{2,1,0:T(8,128)(2,1)} async-done(((bf16[2,72,2304]{2,1,0:T(8,128)(2,1)}), bf16[2,2304,2304]{2,1,0:T(8,128)(2,1)}) %all-gather.5.cloned.1.call-update) | async-done | bytes 21233680 | tf_op jit(solution)/shard_map/all_gather | solution.py:462
  320.6 7.4 fusion.24
  328.1 7.2 convolution_convert_fusion.2.refs_1_
  341.8 8.1 shard_map.221
  350.9 8.6 fusion.20
  359.5 8.9 fusion.13
  374.5 6.7 multiply_reduce_fusion
  381.3 8.1 fusion.21
  389.4 9.8 %fusion.66 = (f32[1152]{0:T(1024)S(1)}, bf16[512,1152]{1,0:T(8,128)(2,1)}, bf16[512,1152]{1,0:T(8,128)(2,1)S(1)}, f32[512,1152]{1,0:T(8,128)S(1)}) fusion(bf16[128,1152]{1,0:T(8,128)(2,1)} %collective-permute-done.28, bf16[128,1152]{1,0:T(8,128)(2,1)} %collective-permute-done.27, bf16[128,1152]{1,0:T(8,128)(2,1)} %collective-permute-done.26, ...), kind=kOutput, calls=%fused_computation.113 | convolution fusion | flops 2742090752 | bytes 23025152 | tf_op jit(solution)/shard_map/dot_general | solution.py:33
  403.3 18.9 %shard_map.217 = (bf16[512,640]{1,0:T(8,128)(2,1)}, bf16[512,640]{1,0:T(8,128)(2,1)}, bf16[120,640]{1,0:T(8,128)(2,1)}, bf16[120,640]{1,0:T(8,128)(2,1)}, bf16[1...) custom-call(bf16[512,640]{1,0:T(8,128)(2,1)} %convolution_convert_fusion.27.refs_0_, ...), custom_call_target="tpu_custom_call" | custom-call | tf_op jit(solution)/shard_map/pallas_call | solution.py:374
  468.9 7.4 shard_map.218
  493.4 8.1 shard_map.224
  515.1 57.9 %shard_map.220 = (bf16[512,896]{1,0:T(8,128)(2,1)}, bf16[512,896]{1,0:T(8,128)(2,1)}, bf16[512,896]{1,0:T(8,128)(2,1)}, bf16[512,896]{1,0:T(8,128)(2,1)}) custom-call(bf16[512,896]{1,0:T(8,128)(2,1)} %get-tuple-element.97.refs_0_, bf16[512,896]{1,0:T(8,128)(2,1)} %collective-permute-done.20.refs_1_, bf16[512,896]{1,0:T(8,128)(2,1)} %collective-permute-done.21.refs_2_, ...), custom_call_target="tpu_custom_call" | custom-call | flops 42949672960 | bytes 14680064 | tf_op jit(solution)/shard_map/pallas_call | solution.py:264
  581.2 58.8 %collective-permute-done.44 = bf16[120,1152]{1,0:T(8,128)(2,1)S(1)} collective-permute-done((bf16[120,1152]{1,0:T(8,128)(2,1)S(1)}, bf16[120,1152]{1,0:T(8,128)(2,1)S(1)}, u32[]{:S(2)}, u32[]{:S(2)}) %collective-permute-start.44) | collective-permute-done | bytes 276512 | tf_op jit(solution)/shard_map/ppermute | solution.py:50
  653.0 33.6 %collective-permute-done.41 = bf16[576,1280]{1,0:T(8,128)(2,1)S(1)} collective-permute-done((bf16[576,1280]{1,0:T(8,128)(2,1)S(1)}, bf16[576,1280]{1,0:T(8,128)(2,1)S(1)}, u32[]{:S(2)}, u32[]{:S(2)}) %collective-permute-start.41) | collective-permute-done | bytes 1474592 | tf_op jit(solution)/shard_map/ppermute | solution.py:50
  688.0 11.0 %collective-permute-done.40 = bf16[576,1920]{1,0:T(8,128)(2,1)S(1)} collective-permute-done((bf16[576,1920]{1,0:T(8,128)(2,1)S(1)}, bf16[576,1920]{1,0:T(8,128)(2,1)S(1)}, u32[]{:S(2)}, u32[]{:S(2)}) %collective-permute-start.40) | collective-permute-done | bytes 2211872 | tf_op jit(solution)/shard_map/ppermute | solution.py:50
  731.3 9.8 %fusion.63 = (f32[1152]{0:T(1024)}, f32[512]{0:T(512)}, f32[512]{0:T(512)}, f32[1152]{0:T(1024)}, f32[512,1152]{1,0:T(8,128)}) fusion(f32[512]{0:T(512)} %copy-done.87, f32[512]{0:T(512)} %copy-done.79, bf16[128,1152]{1,0:T(8,128)(2,1)S(1)} %copy-done.18, bf16[128,1152]{1,0:T(8,128)(2,1)S(1)} %copy-done.20, bf16[128,1152]{1,0:T(8,128)(2,1)S(1)} %copy-done.16, ...), kind=kOutput, calls=%fused_computation.110 | convolution fusion | flops 2429629440 | bytes 13625344 | tf_op jit(solution)/shard_map/dot_general | solution.py:33
  768.2 8.1 collective-permute-done.55
  792.1 12.1 %collective-permute-done.46 = bf16[128,1152]{1,0:T(8,128)(2,1)S(1)} collective-permute-done((bf16[128,1152]{1,0:T(8,128)(2,1)}, bf16[128,1152]{1,0:T(8,128)(2,1)S(1)}, u32[]{:S(2)}, u32[]{:S(2)}) %collective-permute-start.46) | collective-permute-done | bytes 294944 | tf_op jit(solution)/shard_map/ppermute | solution.py:50
  844.0 10.9 %collective-permute-done.76 = bf16[72,1920]{1,0:T(8,128)(2,1)S(1)} collective-permute-done((bf16[72,1920]{1,0:T(8,128)(2,1)S(1)}, bf16[72,1920]{1,0:T(8,128)(2,1)S(1)}, u32[]{:S(2)}, u32[]{:S(2)}) %collective-permute-start.76) | collective-permute-done | bytes 276512 | tf_op jit(solution)/shard_map/ppermute | solution.py:50
  (570 shorter events, 383.6 us)
Async XLA Ops:
  7.2 151.2 %all-gather.3.cloned.1.call-start = ((), (), s32[]{:S(2)}) async-start(), calls=%async_computation.2 | async-start | bytes 15206400 | tf_op jit(solution)/shard_map/all_gather | solution.py:462
  12.4 302.4 %all-gather.5.cloned.1.call-start = ((), (), s32[]{:S(2)}) async-start(), calls=%async_computation.3 | async-start | bytes 21897216 | tf_op jit(solution)/shard_map/all_gather | solution.py:462
  13.4 687.6 %reduce-scatter.3.cloned.1.call-start = ((), (), s32[]{:S(2)}) async-start(), calls=%async_computation.4 | async-start | bytes 10948608 | tf_op jit(solution)/shard_map/reduce_scatter | solution.py:466
  24.2 27.4 %collective-permute-start.4 = (bf16[72,896]{1,0:T(8,128)(2,1)S(1)}, bf16[72,896]{1,0:T(8,128)(2,1)S(1)}, u32[]{:S(2)}, u32[]{:S(2)}) collective-permute-start(bf16[72,896]{1,0:T(8,128)(2,1)S(1)} %get-tuple-element.303), channel_id=1, source_target_pairs={{0,8},{4,12},{8,0},{12,4},{1,9},{5,13},{9,1},{13,5},{2,10},{6,14},... | collective-permute-start | bytes 387080 | tf_op jit(solution)/shard_map/ppermute | solution.py:50
  24.2 27.4 %collective-permute-start.3 = (bf16[72,896]{1,0:T(8,128)(2,1)S(1)}, bf16[72,896]{1,0:T(8,128)(2,1)S(1)}, u32[]{:S(2)}, u32[]{:S(2)}) collective-permute-start(bf16[72,896]{1,0:T(8,128)(2,1)S(1)} %get-tuple-element.303), channel_id=1, source_target_pairs={{0,4},{4,0},{8,12},{12,8},{1,5},{5,1},{9,13},{13,9},{2,6},{6,2},{1... | collective-permute-start | bytes 387080 | tf_op jit(solution)/shard_map/ppermute | solution.py:50
  53.3 28.2 %collective-permute-start.9 = (bf16[288,896]{1,0:T(8,128)(2,1)S(1)}, bf16[288,896]{1,0:T(8,128)(2,1)}, u32[]{:S(2)}, u32[]{:S(2)}) collective-permute-start(bf16[288,896]{1,0:T(8,128)(2,1)S(1)} %get-tuple-element.301.refs_0_), channel_id=1, source_target_pairs={{0,1},{1,0},{2,3},{3,2},{4,5},{5,4},{6,7},{7,6},{8,9},{9,8},{10,11... | collective-permute-start | bytes 1548296 | tf_op jit(solution)/shard_map/ppermute | solution.py:50
  74.2 39.4 %collective-permute-start.18 = (bf16[576,896]{1,0:T(8,128)(2,1)}, bf16[576,896]{1,0:T(8,128)(2,1)}, u32[]{:S(2)}, u32[]{:S(2)}) collective-permute-start(bf16[576,896]{1,0:T(8,128)(2,1)} %shard_map.212.refs_0_), channel_id=1, source_target_pairs={{0,1},{1,0},{2,3},{3,2},{4,5},{5,4},{6,7},{7,6},{8,9},{9,8},{10,11... | collective-permute-start | bytes 3096584 | tf_op jit(solution)/shard_map/ppermute | solution.py:50
  80.0 32.4 %collective-permute-start.6 = (bf16[288,896]{1,0:T(8,128)(2,1)S(1)}, bf16[288,896]{1,0:T(8,128)(2,1)}, u32[]{:S(2)}, u32[]{:S(2)}) collective-permute-start(bf16[288,896]{1,0:T(8,128)(2,1)S(1)} %get-tuple-element.301.refs_0_), channel_id=1, source_target_pairs={{0,2},{2,0},{1,3},{3,1},{4,6},{6,4},{5,7},{7,5},{8,10},{10,8},{9,1... | collective-permute-start | bytes 1548296 | tf_op jit(solution)/shard_map/ppermute | solution.py:50
  81.6 31.4 %collective-permute-start.10 = (bf16[288,896]{1,0:T(8,128)(2,1)}, bf16[288,896]{1,0:T(8,128)(2,1)}, u32[]{:S(2)}, u32[]{:S(2)}) collective-permute-start(bf16[288,896]{1,0:T(8,128)(2,1)} %collective-permute-done.9.refs_4_), channel_id=1, source_target_pairs={{0,2},{2,0},{1,3},{3,1},{4,6},{6,4},{5,7},{7,5},{8,10},{10,8},{9,1... | collective-permute-start | bytes 1548296 | tf_op jit(solution)/shard_map/ppermute | solution.py:50
  140.4 36.4 %collective-permute-start.22 = (bf16[512,896]{1,0:T(8,128)(2,1)}, bf16[512,896]{1,0:T(8,128)(2,1)S(1)}, u32[]{:S(2)}, u32[]{:S(2)}) collective-permute-start(bf16[512,896]{1,0:T(8,128)(2,1)} %get-tuple-element.245), channel_id=1, source_target_pairs={{0,3},{1,2},{2,1},{3,0},{4,7},{5,6},{6,5},{7,4},{8,11},{9,10},{10,... | collective-permute-start | bytes 2752520 | tf_op jit(solution)/shard_map/ppermute | solution.py:50
  142.3 46.3 %collective-permute-start.20 = (bf16[512,896]{1,0:T(8,128)(2,1)}, bf16[512,896]{1,0:T(8,128)(2,1)}, u32[]{:S(2)}, u32[]{:S(2)}) collective-permute-start(bf16[512,896]{1,0:T(8,128)(2,1)} %get-tuple-element.246), channel_id=1, source_target_pairs={{0,1},{1,0},{2,3},{3,2},{4,5},{5,4},{6,7},{7,6},{8,9},{9,8},{10,11... | collective-permute-start | bytes 2752520 | tf_op jit(solution)/shard_map/ppermute | solution.py:50
  147.9 40.7 %collective-permute-start.21 = (bf16[512,896]{1,0:T(8,128)(2,1)}, bf16[512,896]{1,0:T(8,128)(2,1)}, u32[]{:S(2)}, u32[]{:S(2)}) collective-permute-start(bf16[512,896]{1,0:T(8,128)(2,1)} %get-tuple-element.247), channel_id=1, source_target_pairs={{0,2},{1,3},{2,0},{3,1},{4,6},{5,7},{6,4},{7,5},{8,10},{9,11},{10,... | collective-permute-start | bytes 2752520 | tf_op jit(solution)/shard_map/ppermute | solution.py:50
  225.6 102.4 %collective-permute-start.28 = (bf16[128,1152]{1,0:T(8,128)(2,1)}, bf16[128,1152]{1,0:T(8,128)(2,1)}, u32[]{:S(2)}, u32[]{:S(2)}) collective-permute-start(bf16[128,1152]{1,0:T(8,128)(2,1)} %get-tuple-element.258), channel_id=1, source_target_pairs={{0,12},{4,8},{8,4},{12,0},{1,13},{5,9},{9,5},{13,1},{2,14},{6,10},... | collective-permute-start | bytes 884744 | tf_op jit(solution)/shard_map/ppermute | solution.py:50
  227.5 100.6 %collective-permute-start.27 = (bf16[128,1152]{1,0:T(8,128)(2,1)}, bf16[128,1152]{1,0:T(8,128)(2,1)}, u32[]{:S(2)}, u32[]{:S(2)}) collective-permute-start(bf16[128,1152]{1,0:T(8,128)(2,1)} %get-tuple-element.259), channel_id=1, source_target_pairs={{0,8},{4,12},{8,0},{12,4},{1,9},{5,13},{9,1},{13,5},{2,10},{6,14},... | collective-permute-start | bytes 884744 | tf_op jit(solution)/shard_map/ppermute | solution.py:50
  234.2 93.8 %collective-permute-start.26 = (bf16[128,1152]{1,0:T(8,128)(2,1)}, bf16[128,1152]{1,0:T(8,128)(2,1)}, u32[]{:S(2)}, u32[]{:S(2)}) collective-permute-start(bf16[128,1152]{1,0:T(8,128)(2,1)} %get-tuple-element.260), channel_id=1, source_target_pairs={{0,4},{4,0},{8,12},{12,8},{1,5},{5,1},{9,13},{13,9},{2,6},{6,2},{1... | collective-permute-start | bytes 884744 | tf_op jit(solution)/shard_map/ppermute | solution.py:50
  349.9 415.3 %reduce-scatter.5.cloned.1.call-start = ((), (), s32[]{:S(2)}) async-start(), calls=%async_computation.5 | async-start | bytes 10948608 | tf_op jit(solution)/shard_map/reduce_scatter | solution.py:466
  453.4 55.1 %collective-permute-start.33 = (bf16[1152,1280]{1,0:T(8,128)(2,1)}, bf16[1152,1280]{1,0:T(8,128)(2,1)}, u32[]{:S(2)}, u32[]{:S(2)}) collective-permute-start(bf16[1152,1280]{1,0:T(8,128)(2,1)} %get-tuple-element.136), channel_id=1, source_target_pairs={{0,16},{16,0},{1,17},{17,1},{2,18},{18,2},{3,19},{19,3},{4,20},{20... | collective-permute-start | bytes 8847368 | tf_op jit(solution)/shard_map/ppermute | solution.py:50
  476.4 35.0 %collective-permute-start.32 = (bf16[1152,1920]{1,0:T(8,128)(2,1)}, bf16[1152,1920]{1,0:T(8,128)(2,1)}, u32[]{:S(2)}, u32[]{:S(2)}) collective-permute-start(bf16[1152,1920]{1,0:T(8,128)(2,1)} %get-tuple-element.132), channel_id=1, source_target_pairs={{0,16},{16,0},{1,17},{17,1},{2,18},{18,2},{3,19},{19,3},{4,20},{20... | collective-permute-start | bytes 13271048 | tf_op jit(solution)/shard_map/ppermute | solution.py:50
  477.5 26.9 %collective-permute-start.36 = (bf16[128,1152]{1,0:T(8,128)(2,1)}, bf16[128,1152]{1,0:T(8,128)(2,1)}, u32[]{:S(2)}, u32[]{:S(2)}) collective-permute-start(bf16[128,1152]{1,0:T(8,128)(2,1)} %get-tuple-element.254), channel_id=1, source_target_pairs={{0,4},{4,0},{8,12},{12,8},{1,5},{5,1},{9,13},{13,9},{2,6},{6,2},{1... | collective-permute-start | bytes 884744 | tf_op jit(solution)/shard_map/ppermute | solution.py:50
  477.9 26.5 %collective-permute-start.35 = (bf16[128,1152]{1,0:T(8,128)(2,1)}, bf16[128,1152]{1,0:T(8,128)(2,1)}, u32[]{:S(2)}, u32[]{:S(2)}) collective-permute-start(bf16[128,1152]{1,0:T(8,128)(2,1)} %get-tuple-element.255), channel_id=1, source_target_pairs={{0,8},{4,12},{8,0},{12,4},{1,9},{5,13},{9,1},{13,5},{2,10},{6,14},... | collective-permute-start | bytes 884744 | tf_op jit(solution)/shard_map/ppermute | solution.py:50
  573.0 74.3 %collective-permute-start.38 = (bf16[512,896]{1,0:T(8,128)(2,1)}, bf16[512,896]{1,0:T(8,128)(2,1)S(1)}, u32[]{:S(2)}, u32[]{:S(2)}) collective-permute-start(bf16[512,896]{1,0:T(8,128)(2,1)} %get-tuple-element.147), channel_id=1, source_target_pairs={{0,3},{1,2},{2,1},{3,0},{4,7},{5,6},{6,5},{7,4},{8,11},{9,10},{10,... | collective-permute-start | bytes 2752520 | tf_op jit(solution)/shard_map/ppermute | solution.py:50
  574.2 73.0 %collective-permute-start.39 = (bf16[512,896]{1,0:T(8,128)(2,1)}, bf16[512,896]{1,0:T(8,128)(2,1)S(1)}, u32[]{:S(2)}, u32[]{:S(2)}) collective-permute-start(bf16[512,896]{1,0:T(8,128)(2,1)} %get-tuple-element.148), channel_id=1, source_target_pairs={{0,1},{1,0},{2,3},{3,2},{4,5},{5,4},{6,7},{7,6},{8,9},{9,8},{10,11... | collective-permute-start | bytes 2752520 | tf_op jit(solution)/shard_map/ppermute | solution.py:50
  577.4 62.5 %collective-permute-start.44 = (bf16[120,1152]{1,0:T(8,128)(2,1)S(1)}, bf16[120,1152]{1,0:T(8,128)(2,1)S(1)}, u32[]{:S(2)}, u32[]{:S(2)}) collective-permute-start(bf16[120,1152]{1,0:T(8,128)(2,1)S(1)} %fusion.54), channel_id=1, source_target_pairs={{0,3},{1,2},{2,1},{3,0},{4,7},{5,6},{6,5},{7,4},{8,11},{9,10},{10,... | collective-permute-start | bytes 829448 | tf_op jit(solution)/shard_map/ppermute | solution.py:50
  579.6 62.1 %collective-permute-start.43 = (bf16[120,1152]{1,0:T(8,128)(2,1)S(1)}, bf16[120,1152]{1,0:T(8,128)(2,1)S(1)}, u32[]{:S(2)}, u32[]{:S(2)}) collective-permute-start(bf16[120,1152]{1,0:T(8,128)(2,1)S(1)} %fusion.54), channel_id=1, source_target_pairs={{0,2},{1,3},{2,0},{3,1},{4,6},{5,7},{6,4},{7,5},{8,10},{9,11},{10,... | collective-permute-start | bytes 829448 | tf_op jit(solution)/shard_map/ppermute | solution.py:50
  580.0 65.1 %collective-permute-start.42 = (bf16[120,1152]{1,0:T(8,128)(2,1)S(1)}, bf16[120,1152]{1,0:T(8,128)(2,1)S(1)}, u32[]{:S(2)}, u32[]{:S(2)}) collective-permute-start(bf16[120,1152]{1,0:T(8,128)(2,1)S(1)} %fusion.54), channel_id=1, source_target_pairs={{0,1},{1,0},{2,3},{3,2},{4,5},{5,4},{6,7},{7,6},{8,9},{9,8},{10,11... | collective-permute-start | bytes 829448 | tf_op jit(solution)/shard_map/ppermute | solution.py:50
  639.9 59.1 %collective-permute-start.40 = (bf16[576,1920]{1,0:T(8,128)(2,1)S(1)}, bf16[576,1920]{1,0:T(8,128)(2,1)S(1)}, u32[]{:S(2)}, u32[]{:S(2)}) collective-permute-start(bf16[576,1920]{1,0:T(8,128)(2,1)S(1)} %slice.204), channel_id=1, source_target_pairs={{0,1},{1,0},{2,3},{3,2},{4,5},{5,4},{6,7},{7,6},{8,9},{9,8},{10,11... | collective-permute-start | bytes 6635528 | tf_op jit(solution)/shard_map/ppermute | solution.py:50
  641.7 44.8 %collective-permute-start.41 = (bf16[576,1280]{1,0:T(8,128)(2,1)S(1)}, bf16[576,1280]{1,0:T(8,128)(2,1)S(1)}, u32[]{:S(2)}, u32[]{:S(2)}) collective-permute-start(bf16[576,1280]{1,0:T(8,128)(2,1)S(1)} %slice.206), channel_id=1, source_target_pairs={{0,2},{2,0},{1,3},{3,1},{4,6},{6,4},{5,7},{7,5},{8,10},{10,8},{9,1... | collective-permute-start | bytes 4423688 | tf_op jit(solution)/shard_map/ppermute | solution.py:50
  646.0 60.9 %collective-permute-start.37 = (bf16[512,896]{1,0:T(8,128)(2,1)}, bf16[512,896]{1,0:T(8,128)(2,1)}, u32[]{:S(2)}, u32[]{:S(2)}) collective-permute-start(bf16[512,896]{1,0:T(8,128)(2,1)} %get-tuple-element.144), channel_id=1, source_target_pairs={{0,2},{1,3},{2,0},{3,1},{4,6},{5,7},{6,4},{7,5},{8,10},{9,11},{10,... | collective-permute-start | bytes 2752520 | tf_op jit(solution)/shard_map/ppermute | solution.py:50
  752.6 28.0 %collective-permute-start.50 = (bf16[120,1152]{1,0:T(8,128)(2,1)}, bf16[120,1152]{1,0:T(8,128)(2,1)}, u32[]{:S(2)}, u32[]{:S(2)}) collective-permute-start(bf16[120,1152]{1,0:T(8,128)(2,1)} %convert_add_fusion.3), channel_id=1, source_target_pairs={{0,4},{4,0},{8,12},{12,8},{1,5},{5,1},{9,13},{13,9},{2,6},{6,2},{1... | collective-permute-start | bytes 829448 | tf_op jit(solution)/shard_map/ppermute | solution.py:50
  776.3 29.1 %collective-permute-start.70 = (bf16[288,1280]{1,0:T(8,128)(2,1)S(1)}, bf16[288,1280]{1,0:T(8,128)(2,1)S(1)}, u32[]{:S(2)}, u32[]{:S(2)}) collective-permute-start(bf16[288,1280]{1,0:T(8,128)(2,1)S(1)} %slice.226), channel_id=1, source_target_pairs={{0,1},{1,0},{2,3},{3,2},{4,5},{5,4},{6,7},{7,6},{8,9},{9,8},{10,11... | collective-permute-start | bytes 2211848 | tf_op jit(solution)/shard_map/ppermute | solution.py:50
  784.3 44.3 %collective-permute-start.74 = (bf16[288,1920]{1,0:T(8,128)(2,1)}, bf16[288,1920]{1,0:T(8,128)(2,1)S(1)}, u32[]{:S(2)}, u32[]{:S(2)}) collective-permute-start(bf16[288,1920]{1,0:T(8,128)(2,1)} %slice.233), channel_id=1, source_target_pairs={{0,2},{2,0},{1,3},{3,1},{4,6},{6,4},{5,7},{7,5},{8,10},{10,8},{9,1... | collective-permute-start | bytes 3317768 | tf_op jit(solution)/shard_map/ppermute | solution.py:50
  792.1 40.5 %collective-permute-start.58 = (bf16[1152,896]{1,0:T(8,128)(2,1)S(1)}, bf16[1152,896]{1,0:T(8,128)(2,1)S(1)}, u32[]{:S(2)}, u32[]{:S(2)}) collective-permute-start(bf16[1152,896]{1,0:T(8,128)(2,1)S(1)} %copy-done.96), channel_id=1, source_target_pairs={{0,16},{16,0},{1,17},{17,1},{2,18},{18,2},{3,19},{19,3},{4,20},{20... | collective-permute-start | bytes 6193160 | tf_op jit(solution)/shard_map/ppermute | solution.py:50
  (176 other events, 2486.5 us)
Sparse Core Ops, SparseCore 0:
  12.5 145.9 all-gather.2
  161.9 152.8 all-gather.4
  350.0 165.1 reduce-scatter.2
  521.2 182.5 reduce-scatter.4

commit v6 on v5

--- a/solution.py
+++ b/solution.py
@@ -676,7 +676,9 @@
     pack_a, pack_b = sum_blocks(pack_a, "tensor"), sum_blocks(pack_b, ROW)
     text_sum = plane_sum(text_terms, bf16)
     grad_mix = list(attend_back(mixed, groups, grad_heads, att_wide, logsum, heads))
-    (grad_mix[0], down_sum) = tie(grad_mix[0], down_sum)
+    (grad_mix[0], pack_a, pack_b, down_sum) = lax.optimization_barrier(
+        (grad_mix[0], pack_a, pack_b, down_sum)
+    )
     for step in range(1, halves):
         for place in range(groups):
             more = send_xor(grad_mix[step * groups + place], "sr", step)

time: 912 us -> 912 us (level)
  no operation moved by 1% of the time
where the time goes in v6:
time: 912 us; the launch traced here: 902 us
  waiting for transfers between devices  345 us (38%)
  matrix products  190 us (21%)
  Pallas kernels  180 us (20%)
  starting transfers between devices  95.7 us (10%)
  other arithmetic  41 us (4%)
  local copies, waits for them, and re-layouts  33.6 us (4%)
  between operations  16 us (2%)
    ppermute x78, waiting for transfers between devices, send_xor(): lax.ppermute(piece, axes, [(rank, rank ^ step) for rank in range(size)])  287 us
    dot_general x60, matrix products, dot(): return lax.dot_general(left, right, dims, preferred_element_type=f32)  190 us
    ppermute x78, starting transfers between devices, send_xor(): lax.ppermute(piece, axes, [(rank, rank ^ step) for rank in range(size)])  95.5 us
    pallas_call x10, Pallas kernels, lay(): pl.pallas_call(partial(assemble_kernel, plan, len(sources)), in_specs=[an...  58.9 us
    pallas_call x1, Pallas kernels, attend_back(): pl.pallas_call(partial(attend_back_kernel, heads, min(512, total), len(pi...  57.9 us
    all_gather x2, waiting for transfers between devices, gather_all(): return lax.all_gather(shard, EVERY, axis=shard.ndim - 2, tiled=True)  57.9 us
    pallas_call x1, Pallas kernels, attend(): pl.pallas_call(partial(attend_kernel, heads, len(pieces), own), grid=(row...  32.4 us
    pallas_call x1, Pallas kernels, cross_back(): pl.pallas_call(partial(cross_back_kernel, part, splits), grid=(rows // bl...  18.9 us
  transfers between devices with their start and end apart: 82, of which 39 were waited for; matrix products, arithmetic and copies ran while one was open for 26% of the time, Pallas kernels for 19%

profile of v6, /device:TPU:0, one launch (start us, length us, event | category | flops | bytes accessed | tf_op | source)
XLA Modules:
  0.0 901.7 jit_solution(10876794863057938910)
XLA Ops:
  24.2 9.6 %collective-permute-start.3 = (bf16[72,896]{1,0:T(8,128)(2,1)S(1)}, bf16[72,896]{1,0:T(8,128)(2,1)S(1)}, u32[]{:S(2)}, u32[]{:S(2)}) collective-permute-start(bf16[72,896]{1,0:T(8,128)(2,1)S(1)} %get-tuple-element.307), channel_id=1, source_target_pairs={{0,4},{4,0},{8,12},{12,8},{1,5},{5,1},{9,13},{13,9},{2,6},{6,2},{1... | collective-permute-start | bytes 387080 | tf_op jit(solution)/shard_map/ppermute | solution.py:50
  33.8 11.2 %collective-permute-done.14 = bf16[72,896]{1,0:T(8,128)(2,1)S(1)} collective-permute-done((bf16[72,896]{1,0:T(8,128)(2,1)S(1)}, bf16[72,896]{1,0:T(8,128)(2,1)S(1)}, u32[]{:S(2)}, u32[]{:S(2)}) %collective-permute-start.14) | collective-permute-done | bytes 129056 | tf_op jit(solution)/shard_map/ppermute | solution.py:50
  54.8 16.4 %collective-permute-done.16.refs_1_ = bf16[288,896]{1,0:T(8,128)(2,1)S(1)} collective-permute-done((bf16[288,896]{1,0:T(8,128)(2,1)S(1)}, bf16[288,896]{1,0:T(8,128)(2,1)S(1)}, u32[]{:S(2)}, u32[]{:S(2)}) %collective-permute-start.16) | collective-permute-done | bytes 516128 | tf_op jit(solution)/shard_map/ppermute | solution.py:50
  83.0 13.5 %collective-permute-done = bf16[128,1152]{1,0:T(8,128)(2,1)S(1)} collective-permute-done((bf16[128,1152]{1,0:T(8,128)(2,1)S(1)}, bf16[128,1152]{1,0:T(8,128)(2,1)S(1)}, u32[]{:S(2)}, u32[]{:S(2)}) %collective-permute-start) | collective-permute-done | bytes 294944 | tf_op jit(solution)/shard_map/ppermute | solution.py:50
  101.0 11.1 %collective-permute-done.1 = bf16[128,1152]{1,0:T(8,128)(2,1)S(1)} collective-permute-done((bf16[128,1152]{1,0:T(8,128)(2,1)}, bf16[128,1152]{1,0:T(8,128)(2,1)S(1)}, u32[]{:S(2)}, u32[]{:S(2)}) %collective-permute-start.1) | collective-permute-done | bytes 294944 | tf_op jit(solution)/shard_map/ppermute | solution.py:50
  148.3 10.2 %all-gather.3.cloned.1.call-done.refs_0_ = bf16[2304,3200]{1,0:T(8,128)(2,1)} async-done(((bf16[72,3200]{1,0:T(8,128)(2,1)}), bf16[2304,3200]{1,0:T(8,128)(2,1)}) %all-gather.3.cloned.1.call-update) | async-done | bytes 14745616 | tf_op jit(solution)/shard_map/all_gather | solution.py:462
  158.4 10.7 %shard_map.214 = (bf16[1152,640]{1,0:T(8,128)(2,1)}, bf16[1152,640]{1,0:T(8,128)(2,1)}, bf16[1152,640]{1,0:T(8,128)(2,1)}, bf16[1152,640]{1,0:T(8,128)(2,1)}, bf...) custom-call(bf16[2304,3200]{1,0:T(8,128)(2,1)} %all-gather.3.cloned., ...), custom_call_target="tpu_custom_call" | custom-call | tf_op jit(solution)/shard_map/pallas_call | solution.py:407
  176.8 11.8 %collective-permute-done.20.refs_1_ = bf16[512,896]{1,0:T(8,128)(2,1)} collective-permute-done((bf16[512,896]{1,0:T(8,128)(2,1)}, bf16[512,896]{1,0:T(8,128)(2,1)}, u32[]{:S(2)}, u32[]{:S(2)}) %collective-permute-start.20) | collective-permute-done | bytes 917536 | tf_op jit(solution)/shard_map/ppermute | solution.py:50
  188.6 32.4 %shard_map.215 = (bf16[512,288]{1,0:T(8,128)(2,1)}, bf16[512,288]{1,0:T(8,128)(2,1)}, bf16[512,288]{1,0:T(8,128)(2,1)}, bf16[512,288]{1,0:T(8,128)(2,1)}, f32[4,2048,72]{2,1,0:T(8,128)}, /*index=5*/f32[8,2048]{1,0:T(8,128)}) custom-call(bf16[512,896]{1,0:T(8,128)(2,1)} %get-tuple-element.99.refs_0_, bf16[512,896]{1,0:T(8,128)(2,1)} %collective-permute-done.20.refs_1_, ...), custom_call_target="tpu_custom_call" | custom-call | flops 17179869184 | bytes 7340032 | tf_op jit(solution)/shard_map/pallas_call | solution.py:160
  227.5 6.7 collective-permute-done.23
  234.2 7.4 collective-permute-done.24
  249.5 12.0 %shard_map.216 = (bf16[512,640]{1,0:T(8,128)(2,1)}, bf16[512,640]{1,0:T(8,128)(2,1)}) custom-call(bf16[512,640]{1,0:T(8,128)(2,1)} %convolution_convert_fusion.27.refs_0_, bf16[512,640]{1,0:T(8,128)(2,1)} %convolution_convert_fusion.26.refs_1_, bf16[120,640]{1,0:T(8,128)(2,1)} %convolution_convert_fusion.31.refs_2_, ...), custom_call_target="tpu_custom_call" | custom-call | tf_op jit(solution)/shard_map/pallas_call | solution.py:318
  267.1 47.7 %all-gather.5.cloned.1.call-done = bf16[2,2304,2304]{2,1,0:T(8,128)(2,1)} async-done(((bf16[2,72,2304]{2,1,0:T(8,128)(2,1)}), bf16[2,2304,2304]{2,1,0:T(8,128)(2,1)}) %all-gather.5.cloned.1.call-update) | async-done | bytes 21233680 | tf_op jit(solution)/shard_map/all_gather | solution.py:462
  320.6 7.4 fusion.24
  328.1 7.2 convolution_convert_fusion.2.refs_1_
  341.8 8.1 shard_map.221
  350.9 8.6 fusion.20
  359.5 8.9 fusion.13
  374.5 6.7 multiply_reduce_fusion
  381.3 8.1 fusion.21
  389.4 9.8 %fusion.66 = (f32[1152]{0:T(1024)S(1)}, bf16[512,1152]{1,0:T(8,128)(2,1)}, bf16[512,1152]{1,0:T(8,128)(2,1)S(1)}, f32[512,1152]{1,0:T(8,128)S(1)}) fusion(bf16[128,1152]{1,0:T(8,128)(2,1)} %collective-permute-done.28, bf16[128,1152]{1,0:T(8,128)(2,1)} %collective-permute-done.27, bf16[128,1152]{1,0:T(8,128)(2,1)} %collective-permute-done.26, ...), kind=kOutput, calls=%fused_computation.113 | convolution fusion | flops 2742090752 | bytes 23025152 | tf_op jit(solution)/shard_map/dot_general | solution.py:33
  403.3 18.9 %shard_map.217 = (bf16[512,640]{1,0:T(8,128)(2,1)}, bf16[512,640]{1,0:T(8,128)(2,1)}, bf16[120,640]{1,0:T(8,128)(2,1)}, bf16[120,640]{1,0:T(8,128)(2,1)}, bf16[1...) custom-call(bf16[512,640]{1,0:T(8,128)(2,1)} %convolution_convert_fusion.27.refs_0_, ...), custom_call_target="tpu_custom_call" | custom-call | tf_op jit(solution)/shard_map/pallas_call | solution.py:374
  468.9 7.4 shard_map.218
  493.4 8.1 shard_map.224
  515.1 57.9 %shard_map.220 = (bf16[512,896]{1,0:T(8,128)(2,1)}, bf16[512,896]{1,0:T(8,128)(2,1)}, bf16[512,896]{1,0:T(8,128)(2,1)}, bf16[512,896]{1,0:T(8,128)(2,1)}) custom-call(bf16[512,896]{1,0:T(8,128)(2,1)} %get-tuple-element.99.refs_0_, bf16[512,896]{1,0:T(8,128)(2,1)} %collective-permute-done.20.refs_1_, bf16[512,896]{1,0:T(8,128)(2,1)} %collective-permute-done.21.refs_2_, ...), custom_call_target="tpu_custom_call" | custom-call | flops 42949672960 | bytes 14680064 | tf_op jit(solution)/shard_map/pallas_call | solution.py:264
  581.2 58.8 %collective-permute-done.44 = bf16[120,1152]{1,0:T(8,128)(2,1)S(1)} collective-permute-done((bf16[120,1152]{1,0:T(8,128)(2,1)S(1)}, bf16[120,1152]{1,0:T(8,128)(2,1)S(1)}, u32[]{:S(2)}, u32[]{:S(2)}) %collective-permute-start.44) | collective-permute-done | bytes 276512 | tf_op jit(solution)/shard_map/ppermute | solution.py:50
  653.0 33.6 %collective-permute-done.39 = bf16[576,1280]{1,0:T(8,128)(2,1)S(1)} collective-permute-done((bf16[576,1280]{1,0:T(8,128)(2,1)S(1)}, bf16[576,1280]{1,0:T(8,128)(2,1)S(1)}, u32[]{:S(2)}, u32[]{:S(2)}) %collective-permute-start.39) | collective-permute-done | bytes 1474592 | tf_op jit(solution)/shard_map/ppermute | solution.py:50
  688.0 11.0 %collective-permute-done.38 = bf16[576,1920]{1,0:T(8,128)(2,1)S(1)} collective-permute-done((bf16[576,1920]{1,0:T(8,128)(2,1)S(1)}, bf16[576,1920]{1,0:T(8,128)(2,1)S(1)}, u32[]{:S(2)}, u32[]{:S(2)}) %collective-permute-start.38) | collective-permute-done | bytes 2211872 | tf_op jit(solution)/shard_map/ppermute | solution.py:50
  731.3 9.8 %fusion.63 = (f32[1152]{0:T(1024)}, f32[512]{0:T(512)}, f32[512]{0:T(512)}, f32[1152]{0:T(1024)}, f32[512,1152]{1,0:T(8,128)}) fusion(f32[512]{0:T(512)} %copy-done.87, f32[512]{0:T(512)} %copy-done.79, bf16[128,1152]{1,0:T(8,128)(2,1)S(1)} %copy-done.18, bf16[128,1152]{1,0:T(8,128)(2,1)S(1)} %copy-done.20, bf16[128,1152]{1,0:T(8,128)(2,1)S(1)} %copy-done.16, ...), kind=kOutput, calls=%fused_computation.110 | convolution fusion | flops 2429629440 | bytes 13625344 | tf_op jit(solution)/shard_map/dot_general | solution.py:33
  768.2 8.1 collective-permute-done.55
  792.1 12.1 %collective-permute-done.46 = bf16[128,1152]{1,0:T(8,128)(2,1)S(1)} collective-permute-done((bf16[128,1152]{1,0:T(8,128)(2,1)}, bf16[128,1152]{1,0:T(8,128)(2,1)S(1)}, u32[]{:S(2)}, u32[]{:S(2)}) %collective-permute-start.46) | collective-permute-done | bytes 294944 | tf_op jit(solution)/shard_map/ppermute | solution.py:50
  844.0 10.9 %collective-permute-done.76 = bf16[72,1920]{1,0:T(8,128)(2,1)S(1)} collective-permute-done((bf16[72,1920]{1,0:T(8,128)(2,1)S(1)}, bf16[72,1920]{1,0:T(8,128)(2,1)S(1)}, u32[]{:S(2)}, u32[]{:S(2)}) %collective-permute-start.76) | collective-permute-done | bytes 276512 | tf_op jit(solution)/shard_map/ppermute | solution.py:50
  (570 shorter events, 383.6 us)
Async XLA Ops:
  7.2 151.2 %all-gather.3.cloned.1.call-start = ((), (), s32[]{:S(2)}) async-start(), calls=%async_computation.2 | async-start | bytes 15206400 | tf_op jit(solution)/shard_map/all_gather | solution.py:462
  12.4 302.4 %all-gather.5.cloned.1.call-start = ((), (), s32[]{:S(2)}) async-start(), calls=%async_computation.3 | async-start | bytes 21897216 | tf_op jit(solution)/shard_map/all_gather | solution.py:462
  13.4 687.6 %reduce-scatter.3.cloned.1.call-start = ((), (), s32[]{:S(2)}) async-start(), calls=%async_computation.4 | async-start | bytes 10948608 | tf_op jit(solution)/shard_map/reduce_scatter | solution.py:466
  24.2 27.4 %collective-permute-start.4 = (bf16[72,896]{1,0:T(8,128)(2,1)S(1)}, bf16[72,896]{1,0:T(8,128)(2,1)S(1)}, u32[]{:S(2)}, u32[]{:S(2)}) collective-permute-start(bf16[72,896]{1,0:T(8,128)(2,1)S(1)} %get-tuple-element.307), channel_id=1, source_target_pairs={{0,8},{4,12},{8,0},{12,4},{1,9},{5,13},{9,1},{13,5},{2,10},{6,14},... | collective-permute-start | bytes 387080 | tf_op jit(solution)/shard_map/ppermute | solution.py:50
  24.2 27.4 %collective-permute-start.3 = (bf16[72,896]{1,0:T(8,128)(2,1)S(1)}, bf16[72,896]{1,0:T(8,128)(2,1)S(1)}, u32[]{:S(2)}, u32[]{:S(2)}) collective-permute-start(bf16[72,896]{1,0:T(8,128)(2,1)S(1)} %get-tuple-element.307), channel_id=1, source_target_pairs={{0,4},{4,0},{8,12},{12,8},{1,5},{5,1},{9,13},{13,9},{2,6},{6,2},{1... | collective-permute-start | bytes 387080 | tf_op jit(solution)/shard_map/ppermute | solution.py:50
  53.3 28.2 %collective-permute-start.9 = (bf16[288,896]{1,0:T(8,128)(2,1)S(1)}, bf16[288,896]{1,0:T(8,128)(2,1)}, u32[]{:S(2)}, u32[]{:S(2)}) collective-permute-start(bf16[288,896]{1,0:T(8,128)(2,1)S(1)} %get-tuple-element.305.refs_0_), channel_id=1, source_target_pairs={{0,1},{1,0},{2,3},{3,2},{4,5},{5,4},{6,7},{7,6},{8,9},{9,8},{10,11... | collective-permute-start | bytes 1548296 | tf_op jit(solution)/shard_map/ppermute | solution.py:50
  74.2 39.4 %collective-permute-start.18 = (bf16[576,896]{1,0:T(8,128)(2,1)}, bf16[576,896]{1,0:T(8,128)(2,1)}, u32[]{:S(2)}, u32[]{:S(2)}) collective-permute-start(bf16[576,896]{1,0:T(8,128)(2,1)} %shard_map.212.refs_0_), channel_id=1, source_target_pairs={{0,1},{1,0},{2,3},{3,2},{4,5},{5,4},{6,7},{7,6},{8,9},{9,8},{10,11... | collective-permute-start | bytes 3096584 | tf_op jit(solution)/shard_map/ppermute | solution.py:50
  80.0 32.4 %collective-permute-start.6 = (bf16[288,896]{1,0:T(8,128)(2,1)S(1)}, bf16[288,896]{1,0:T(8,128)(2,1)}, u32[]{:S(2)}, u32[]{:S(2)}) collective-permute-start(bf16[288,896]{1,0:T(8,128)(2,1)S(1)} %get-tuple-element.305.refs_0_), channel_id=1, source_target_pairs={{0,2},{2,0},{1,3},{3,1},{4,6},{6,4},{5,7},{7,5},{8,10},{10,8},{9,1... | collective-permute-start | bytes 1548296 | tf_op jit(solution)/shard_map/ppermute | solution.py:50
  81.6 31.4 %collective-permute-start.10 = (bf16[288,896]{1,0:T(8,128)(2,1)}, bf16[288,896]{1,0:T(8,128)(2,1)}, u32[]{:S(2)}, u32[]{:S(2)}) collective-permute-start(bf16[288,896]{1,0:T(8,128)(2,1)} %collective-permute-done.9.refs_4_), channel_id=1, source_target_pairs={{0,2},{2,0},{1,3},{3,1},{4,6},{6,4},{5,7},{7,5},{8,10},{10,8},{9,1... | collective-permute-start | bytes 1548296 | tf_op jit(solution)/shard_map/ppermute | solution.py:50
  140.4 36.4 %collective-permute-start.22 = (bf16[512,896]{1,0:T(8,128)(2,1)}, bf16[512,896]{1,0:T(8,128)(2,1)S(1)}, u32[]{:S(2)}, u32[]{:S(2)}) collective-permute-start(bf16[512,896]{1,0:T(8,128)(2,1)} %get-tuple-element.249), channel_id=1, source_target_pairs={{0,3},{1,2},{2,1},{3,0},{4,7},{5,6},{6,5},{7,4},{8,11},{9,10},{10,... | collective-permute-start | bytes 2752520 | tf_op jit(solution)/shard_map/ppermute | solution.py:50
  142.3 46.3 %collective-permute-start.20 = (bf16[512,896]{1,0:T(8,128)(2,1)}, bf16[512,896]{1,0:T(8,128)(2,1)}, u32[]{:S(2)}, u32[]{:S(2)}) collective-permute-start(bf16[512,896]{1,0:T(8,128)(2,1)} %get-tuple-element.250), channel_id=1, source_target_pairs={{0,1},{1,0},{2,3},{3,2},{4,5},{5,4},{6,7},{7,6},{8,9},{9,8},{10,11... | collective-permute-start | bytes 2752520 | tf_op jit(solution)/shard_map/ppermute | solution.py:50
  147.9 40.7 %collective-permute-start.21 = (bf16[512,896]{1,0:T(8,128)(2,1)}, bf16[512,896]{1,0:T(8,128)(2,1)}, u32[]{:S(2)}, u32[]{:S(2)}) collective-permute-start(bf16[512,896]{1,0:T(8,128)(2,1)} %get-tuple-element.251), channel_id=1, source_target_pairs={{0,2},{1,3},{2,0},{3,1},{4,6},{5,7},{6,4},{7,5},{8,10},{9,11},{10,... | collective-permute-start | bytes 2752520 | tf_op jit(solution)/shard_map/ppermute | solution.py:50
  225.6 102.4 %collective-permute-start.28 = (bf16[128,1152]{1,0:T(8,128)(2,1)}, bf16[128,1152]{1,0:T(8,128)(2,1)}, u32[]{:S(2)}, u32[]{:S(2)}) collective-permute-start(bf16[128,1152]{1,0:T(8,128)(2,1)} %get-tuple-element.262), channel_id=1, source_target_pairs={{0,12},{4,8},{8,4},{12,0},{1,13},{5,9},{9,5},{13,1},{2,14},{6,10},... | collective-permute-start | bytes 884744 | tf_op jit(solution)/shard_map/ppermute | solution.py:50
  227.5 100.6 %collective-permute-start.27 = (bf16[128,1152]{1,0:T(8,128)(2,1)}, bf16[128,1152]{1,0:T(8,128)(2,1)}, u32[]{:S(2)}, u32[]{:S(2)}) collective-permute-start(bf16[128,1152]{1,0:T(8,128)(2,1)} %get-tuple-element.263), channel_id=1, source_target_pairs={{0,8},{4,12},{8,0},{12,4},{1,9},{5,13},{9,1},{13,5},{2,10},{6,14},... | collective-permute-start | bytes 884744 | tf_op jit(solution)/shard_map/ppermute | solution.py:50
  234.2 93.8 %collective-permute-start.26 = (bf16[128,1152]{1,0:T(8,128)(2,1)}, bf16[128,1152]{1,0:T(8,128)(2,1)}, u32[]{:S(2)}, u32[]{:S(2)}) collective-permute-start(bf16[128,1152]{1,0:T(8,128)(2,1)} %get-tuple-element.264), channel_id=1, source_target_pairs={{0,4},{4,0},{8,12},{12,8},{1,5},{5,1},{9,13},{13,9},{2,6},{6,2},{1... | collective-permute-start | bytes 884744 | tf_op jit(solution)/shard_map/ppermute | solution.py:50
  349.9 415.3 %reduce-scatter.5.cloned.1.call-start = ((), (), s32[]{:S(2)}) async-start(), calls=%async_computation.5 | async-start | bytes 10948608 | tf_op jit(solution)/shard_map/reduce_scatter | solution.py:466
  453.4 55.1 %collective-permute-start.33 = (bf16[1152,1280]{1,0:T(8,128)(2,1)}, bf16[1152,1280]{1,0:T(8,128)(2,1)}, u32[]{:S(2)}, u32[]{:S(2)}) collective-permute-start(bf16[1152,1280]{1,0:T(8,128)(2,1)} %get-tuple-element.138), channel_id=1, source_target_pairs={{0,16},{16,0},{1,17},{17,1},{2,18},{18,2},{3,19},{19,3},{4,20},{20... | collective-permute-start | bytes 8847368 | tf_op jit(solution)/shard_map/ppermute | solution.py:50
  476.4 35.0 %collective-permute-start.32 = (bf16[1152,1920]{1,0:T(8,128)(2,1)}, bf16[1152,1920]{1,0:T(8,128)(2,1)}, u32[]{:S(2)}, u32[]{:S(2)}) collective-permute-start(bf16[1152,1920]{1,0:T(8,128)(2,1)} %get-tuple-element.134), channel_id=1, source_target_pairs={{0,16},{16,0},{1,17},{17,1},{2,18},{18,2},{3,19},{19,3},{4,20},{20... | collective-permute-start | bytes 13271048 | tf_op jit(solution)/shard_map/ppermute | solution.py:50
  477.5 26.9 %collective-permute-start.36 = (bf16[128,1152]{1,0:T(8,128)(2,1)}, bf16[128,1152]{1,0:T(8,128)(2,1)}, u32[]{:S(2)}, u32[]{:S(2)}) collective-permute-start(bf16[128,1152]{1,0:T(8,128)(2,1)} %get-tuple-element.258), channel_id=1, source_target_pairs={{0,4},{4,0},{8,12},{12,8},{1,5},{5,1},{9,13},{13,9},{2,6},{6,2},{1... | collective-permute-start | bytes 884744 | tf_op jit(solution)/shard_map/ppermute | solution.py:50
  477.9 26.5 %collective-permute-start.35 = (bf16[128,1152]{1,0:T(8,128)(2,1)}, bf16[128,1152]{1,0:T(8,128)(2,1)}, u32[]{:S(2)}, u32[]{:S(2)}) collective-permute-start(bf16[128,1152]{1,0:T(8,128)(2,1)} %get-tuple-element.259), channel_id=1, source_target_pairs={{0,8},{4,12},{8,0},{12,4},{1,9},{5,13},{9,1},{13,5},{2,10},{6,14},... | collective-permute-start | bytes 884744 | tf_op jit(solution)/shard_map/ppermute | solution.py:50
  573.0 74.3 %collective-permute-start.40 = (bf16[512,896]{1,0:T(8,128)(2,1)}, bf16[512,896]{1,0:T(8,128)(2,1)S(1)}, u32[]{:S(2)}, u32[]{:S(2)}) collective-permute-start(bf16[512,896]{1,0:T(8,128)(2,1)} %get-tuple-element.151), channel_id=1, source_target_pairs={{0,3},{1,2},{2,1},{3,0},{4,7},{5,6},{6,5},{7,4},{8,11},{9,10},{10,... | collective-permute-start | bytes 2752520 | tf_op jit(solution)/shard_map/ppermute | solution.py:50
  574.2 73.0 %collective-permute-start.41 = (bf16[512,896]{1,0:T(8,128)(2,1)}, bf16[512,896]{1,0:T(8,128)(2,1)S(1)}, u32[]{:S(2)}, u32[]{:S(2)}) collective-permute-start(bf16[512,896]{1,0:T(8,128)(2,1)} %get-tuple-element.152), channel_id=1, source_target_pairs={{0,1},{1,0},{2,3},{3,2},{4,5},{5,4},{6,7},{7,6},{8,9},{9,8},{10,11... | collective-permute-start | bytes 2752520 | tf_op jit(solution)/shard_map/ppermute | solution.py:50
  577.4 62.5 %collective-permute-start.44 = (bf16[120,1152]{1,0:T(8,128)(2,1)S(1)}, bf16[120,1152]{1,0:T(8,128)(2,1)S(1)}, u32[]{:S(2)}, u32[]{:S(2)}) collective-permute-start(bf16[120,1152]{1,0:T(8,128)(2,1)S(1)} %fusion.54), channel_id=1, source_target_pairs={{0,3},{1,2},{2,1},{3,0},{4,7},{5,6},{6,5},{7,4},{8,11},{9,10},{10,... | collective-permute-start | bytes 829448 | tf_op jit(solution)/shard_map/ppermute | solution.py:50
  579.6 62.1 %collective-permute-start.43 = (bf16[120,1152]{1,0:T(8,128)(2,1)S(1)}, bf16[120,1152]{1,0:T(8,128)(2,1)S(1)}, u32[]{:S(2)}, u32[]{:S(2)}) collective-permute-start(bf16[120,1152]{1,0:T(8,128)(2,1)S(1)} %fusion.54), channel_id=1, source_target_pairs={{0,2},{1,3},{2,0},{3,1},{4,6},{5,7},{6,4},{7,5},{8,10},{9,11},{10,... | collective-permute-start | bytes 829448 | tf_op jit(solution)/shard_map/ppermute | solution.py:50
  580.0 65.1 %collective-permute-start.42 = (bf16[120,1152]{1,0:T(8,128)(2,1)S(1)}, bf16[120,1152]{1,0:T(8,128)(2,1)S(1)}, u32[]{:S(2)}, u32[]{:S(2)}) collective-permute-start(bf16[120,1152]{1,0:T(8,128)(2,1)S(1)} %fusion.54), channel_id=1, source_target_pairs={{0,1},{1,0},{2,3},{3,2},{4,5},{5,4},{6,7},{7,6},{8,9},{9,8},{10,11... | collective-permute-start | bytes 829448 | tf_op jit(solution)/shard_map/ppermute | solution.py:50
  639.9 59.1 %collective-permute-start.38 = (bf16[576,1920]{1,0:T(8,128)(2,1)S(1)}, bf16[576,1920]{1,0:T(8,128)(2,1)S(1)}, u32[]{:S(2)}, u32[]{:S(2)}) collective-permute-start(bf16[576,1920]{1,0:T(8,128)(2,1)S(1)} %slice.204), channel_id=1, source_target_pairs={{0,1},{1,0},{2,3},{3,2},{4,5},{5,4},{6,7},{7,6},{8,9},{9,8},{10,11... | collective-permute-start | bytes 6635528 | tf_op jit(solution)/shard_map/ppermute | solution.py:50
  641.7 44.8 %collective-permute-start.39 = (bf16[576,1280]{1,0:T(8,128)(2,1)S(1)}, bf16[576,1280]{1,0:T(8,128)(2,1)S(1)}, u32[]{:S(2)}, u32[]{:S(2)}) collective-permute-start(bf16[576,1280]{1,0:T(8,128)(2,1)S(1)} %slice.206), channel_id=1, source_target_pairs={{0,2},{2,0},{1,3},{3,1},{4,6},{6,4},{5,7},{7,5},{8,10},{10,8},{9,1... | collective-permute-start | bytes 4423688 | tf_op jit(solution)/shard_map/ppermute | solution.py:50
  646.0 60.9 %collective-permute-start.37 = (bf16[512,896]{1,0:T(8,128)(2,1)}, bf16[512,896]{1,0:T(8,128)(2,1)}, u32[]{:S(2)}, u32[]{:S(2)}) collective-permute-start(bf16[512,896]{1,0:T(8,128)(2,1)} %get-tuple-element.146), channel_id=1, source_target_pairs={{0,2},{1,3},{2,0},{3,1},{4,6},{5,7},{6,4},{7,5},{8,10},{9,11},{10,... | collective-permute-start | bytes 2752520 | tf_op jit(solution)/shard_map/ppermute | solution.py:50
  752.6 28.0 %collective-permute-start.50 = (bf16[120,1152]{1,0:T(8,128)(2,1)}, bf16[120,1152]{1,0:T(8,128)(2,1)}, u32[]{:S(2)}, u32[]{:S(2)}) collective-permute-start(bf16[120,1152]{1,0:T(8,128)(2,1)} %convert_add_fusion.3), channel_id=1, source_target_pairs={{0,4},{4,0},{8,12},{12,8},{1,5},{5,1},{9,13},{13,9},{2,6},{6,2},{1... | collective-permute-start | bytes 829448 | tf_op jit(solution)/shard_map/ppermute | solution.py:50
  776.3 29.1 %collective-permute-start.70 = (bf16[288,1280]{1,0:T(8,128)(2,1)S(1)}, bf16[288,1280]{1,0:T(8,128)(2,1)S(1)}, u32[]{:S(2)}, u32[]{:S(2)}) collective-permute-start(bf16[288,1280]{1,0:T(8,128)(2,1)S(1)} %slice.226), channel_id=1, source_target_pairs={{0,1},{1,0},{2,3},{3,2},{4,5},{5,4},{6,7},{7,6},{8,9},{9,8},{10,11... | collective-permute-start | bytes 2211848 | tf_op jit(solution)/shard_map/ppermute | solution.py:50
  784.3 44.3 %collective-permute-start.74 = (bf16[288,1920]{1,0:T(8,128)(2,1)}, bf16[288,1920]{1,0:T(8,128)(2,1)S(1)}, u32[]{:S(2)}, u32[]{:S(2)}) collective-permute-start(bf16[288,1920]{1,0:T(8,128)(2,1)} %slice.233), channel_id=1, source_target_pairs={{0,2},{2,0},{1,3},{3,1},{4,6},{6,4},{5,7},{7,5},{8,10},{10,8},{9,1... | collective-permute-start | bytes 3317768 | tf_op jit(solution)/shard_map/ppermute | solution.py:50
  792.1 40.5 %collective-permute-start.58 = (bf16[1152,896]{1,0:T(8,128)(2,1)S(1)}, bf16[1152,896]{1,0:T(8,128)(2,1)S(1)}, u32[]{:S(2)}, u32[]{:S(2)}) collective-permute-start(bf16[1152,896]{1,0:T(8,128)(2,1)S(1)} %copy-done.96), channel_id=1, source_target_pairs={{0,16},{16,0},{1,17},{17,1},{2,18},{18,2},{3,19},{19,3},{4,20},{20... | collective-permute-start | bytes 6193160 | tf_op jit(solution)/shard_map/ppermute | solution.py:50
  (176 other events, 2486.5 us)
Sparse Core Ops, SparseCore 0:
  12.5 145.9 all-gather.2
  161.9 152.8 all-gather.4
  350.0 165.1 reduce-scatter.2
  521.2 182.5 reduce-scatter.4
